TPU v7x, 32 devices: a whole 2x2x4 slice. The times are simulated.
32 devices in a mesh: row: 8 (over y, x, core), col: 4 (over z).
Axes of the slice: x: 2, y: 2, z: 4, core: 2. Of those that a mesh axis runs over, the one named last changes fastest.
Arguments:
- a_tiles: bfloat16 [4096, 128, 128], P(('row', 'col')), may hold values from -6 to 6
- a_row: int32 [4096], P(('row', 'col')), may hold values from 0 to 15
- a_col: int32 [4096], P(('row', 'col')), may hold values from 0 to 11
- a_count: int32 [32], P(('row', 'col')), may hold values from 32 to 128
- p_tiles: bfloat16 [128, 128, 128], P(('row', 'col')), may hold values from -0.5 to 0.5
Outputs:
- coarse_tiles: bfloat16 [384, 128, 128], P(('row', 'col'))
All inputs are finite; a program needn't handle non-finite values.
Results may differ from a plain program's by a relative error of at most 0.0049.
Values may be sent and summed in bfloat16 or wider, within the bound.
No kernel may reach another device: no remote copies, remote signals or barrier semaphores. Data moves between devices by JAX's collectives and lax.ppermute only.
A program may use at most 64 MiB of HBM per device.

v0:
```python
import math

import jax
import jax.numpy as jnp
from jax import lax
from jax.sharding import PartitionSpec as P


def shifted(block, axis, distance):
    devices = range(lax.axis_size(axis))
    route = [((i - distance) % len(devices), i) for i in devices]
    return lax.ppermute(block, axis, route)


def shards(a_tiles, a_row, a_col, a_count, p_tiles):
    tile_slots = a_tiles.shape[0]
    width = a_tiles.shape[1]
    held_blocks = p_tiles.shape[0]
    coarse_total = 3 * held_blocks * held_blocks
    block_size = math.gcd(tile_slots, 32)
    row_side = lax.all_gather(p_tiles, "col", axis=0, tiled=True)
    lower = shifted(p_tiles, "row", 1)
    upper = shifted(p_tiles, "row", -1)
    col_side = jnp.concatenate([lower, p_tiles, upper], axis=0)
    count = a_count[0]

    def advance(block_index, accum):
        start = block_index * block_size
        tiles = lax.dynamic_slice_in_dim(a_tiles, start, block_size, 0)
        rows = lax.dynamic_slice_in_dim(a_row, start, block_size, 0)
        cols = lax.dynamic_slice_in_dim(a_col, start, block_size, 0)
        slots = rows % held_blocks * (3 * held_blocks) + cols
        is_live = start + jnp.arange(block_size, dtype=jnp.int32) < count
        right = jnp.take(col_side, cols, axis=0)
        image = jnp.einsum("tij,tjk->tik", tiles, right, preferred_element_type=jnp.float32).astype(
            jnp.bfloat16
        )
        left = jnp.take(row_side, rows, axis=0)
        terms = jnp.einsum("tji,tjk->tik", left, image, preferred_element_type=jnp.float32)
        terms = jnp.where(is_live[:, None, None], terms, jnp.float32(0.0))
        return accum.at[slots].add(terms)

    empty = jnp.zeros((coarse_total, width, width), jnp.float32)
    live_blocks = (count + block_size - 1) // block_size
    accum = lax.fori_loop(0, live_blocks, advance, empty)
    summed = lax.psum_scatter(accum, "col", scatter_dimension=0, tiled=True)
    return summed.astype(jnp.bfloat16)


def solution(mesh):
    in_specs = (
        P(("row", "col"), None, None),
        P(("row", "col")),
        P(("row", "col")),
        P(("row", "col")),
        P(("row", "col"), None, None),
    )
    out_specs = P(("row", "col"), None, None)
    return jax.shard_map(shards, mesh=mesh, in_specs=in_specs, out_specs=out_specs, check_vma=False)
```

profile of v0, /device:TPU:0, one launch (start us, length us, event | category | flops | bytes accessed | tf_op | source)
XLA Modules:
  0.0 161.0 jit_solution(240133967048295615)
XLA Ops:
  6.5 0.0 reduce-scatter.2.cloned.1.call-start
  6.5 0.5 collective-permute-start
  7.0 2.9 %collective-permute-start.1 = (bf16[4,128,128]{2,1,0:T(8,128)(2,1)}, bf16[4,128,128]{2,1,0:T(8,128)(2,1)S(1)}, u32[]{:S(2)}, u32[]{:S(2)}) collective-permute-start(bf16[4,128,128]{2,1,0:T(8,128)(2,1)} %param.11), channel_id=1, source_target_pairs={{4,0},{8,4},{12,8},{16,12},{20,16},{24,20},{28,24},{0,28},{5,1},{9... | collective-permute-start | bytes 393224 | tf_op jit(solution)/shard_map/ppermute | solution.py:12
  10.6 18.3 %all_gather.3 = bf16[16,128,128]{2,1,0:T(8,128)(2,1)} all-gather(bf16[4,128,128]{2,1,0:T(8,128)(2,1)} %param.11), channel_id=1, replica_groups=mesh['row'=8,'col'=4] {'col'}, dimensions={0}, use_global_device_ids=true | all-gather | bytes 655360 | tf_op jit(solution)/shard_map/all_gather | solution.py:21
  28.9 0.0 collective-permute-done
  28.9 0.0 collective-permute-done.1
  28.9 1.0 pad_maximum_fusion
  29.9 0.4 broadcast_in_dim.66
  30.2 0.0 copy-done.2
  30.3 0.0 copy-done.1
  30.3 60.7 %while.12 = (s32[]{:T(128)}, f32[48,128,128]{2,1,0:T(8,128)S(1)}, s32[]{:T(128)}, s32[128]{0:T(128)S(1)}, s32[128]{0:T(128)S(1)}, /*index=5*/s32[]{:T(128)}, bf1...) while((s32[]{:T(128)}, f32[48,128,128]{2,1,0:T(8,128)S(1)}, ...), condition=%wide.region_2.3_spmd, body=%wide.region_0.2_spmd.sunk | while | flops 271059904 | bytes 15742275 | solution.py:45
  30.3 1.2 add_compare_fusion.2
  31.5 0.1 compare_select_fusion.8
  31.6 0.7 compare_and_fusion.3
  32.3 2.7 %gather_fusion.1 = bf16[32,128,128]{2,1,0:T(8,128)(2,1)} fusion(bf16[16,128,128]{2,1,0:T(8,128)(2,1)} %get-tuple-element.243, s32[1024]{0:T(1024)S(1)} %pad_clamp_fusion.5), kind=kCustom, calls=%fused_computation.clone.1 | custom fusion | bytes 2097280 | tf_op jit(solution)/shard_map/while/body/jit(_take)/gather | solution.py:38
  35.0 1.7 %gather_fusion = bf16[32,128,128]{2,1,0:T(8,128)(2,1)} fusion(bf16[12,128,128]{2,1,0:T(8,128)(2,1)S(1)} %get-tuple-element.245, s32[1024]{0:T(1024)S(1)} %pad_clamp_fusion.4), kind=kCustom, calls=%fused_computation.1.clone.1 | custom fusion | bytes 2097280 | tf_op jit(solution)/shard_map/while/body/jit(_take)/gather | solution.py:34
  36.7 4.1 %convolution_select_fusion.2 = f32[32,128,128]{2,1,0:T(8,128)} fusion(bf16[32,128,128]{2,1,0:T(8,128)(2,1)} %gather_fusion, bf16[128,128,128]{2,1,0:T(8,128)(2,1)} %get-tuple-element.244, s32[]{:T(128)S(6)} %select_n.97, bf16[32,128,128]{2,1,0:T(8,128)(2,1)} %gather_fusion.1, pred[32]{0:T(512)(128)(4,1)} %get-tuple-element.209, ...), kind=kOutput, calls=%fused_computation.3.clone.1 | convolution fusion | flops 270532608 | bytes 5244420 | tf_op jit(solution)/shard_map/while/body/tji,tjk->tik/dot_general | solution.py:39
  40.8 4.7 %scatter_fusion = f32[48,128,128]{2,1,0:T(8,128)S(1)} fusion(f32[48,128,128]{2,1,0:T(8,128)S(1)} %get-tuple-element.225, s32[32]{0:T(128)S(1)} %compare_select_fusion.8, f32[32,128,128]{2,1,0:T(8,128)} %convolution_select_fusion.2), kind=kCustom, calls=%fused_computation.2.clone.1 | custom fusion | flops 524288 | bytes 6291584 | tf_op jit(solution)/shard_map/while/body/scatter-add | solution.py:41
  45.4 0.0 copy-done.3
  45.5 1.2 add_compare_fusion.2
  46.7 0.1 compare_select_fusion.8
  46.8 0.7 compare_and_fusion.3
  47.5 2.7 %gather_fusion.1 = bf16[32,128,128]{2,1,0:T(8,128)(2,1)} fusion(bf16[16,128,128]{2,1,0:T(8,128)(2,1)} %get-tuple-element.243, s32[1024]{0:T(1024)S(1)} %pad_clamp_fusion.5), kind=kCustom, calls=%fused_computation.clone.1 | custom fusion | bytes 2097280 | tf_op jit(solution)/shard_map/while/body/jit(_take)/gather | solution.py:38
  50.2 1.7 %gather_fusion = bf16[32,128,128]{2,1,0:T(8,128)(2,1)} fusion(bf16[12,128,128]{2,1,0:T(8,128)(2,1)S(1)} %get-tuple-element.245, s32[1024]{0:T(1024)S(1)} %pad_clamp_fusion.4), kind=kCustom, calls=%fused_computation.1.clone.1 | custom fusion | bytes 2097280 | tf_op jit(solution)/shard_map/while/body/jit(_take)/gather | solution.py:34
  51.8 4.1 %convolution_select_fusion.2 = f32[32,128,128]{2,1,0:T(8,128)} fusion(bf16[32,128,128]{2,1,0:T(8,128)(2,1)} %gather_fusion, bf16[128,128,128]{2,1,0:T(8,128)(2,1)} %get-tuple-element.244, s32[]{:T(128)S(6)} %select_n.97, bf16[32,128,128]{2,1,0:T(8,128)(2,1)} %gather_fusion.1, pred[32]{0:T(512)(128)(4,1)} %get-tuple-element.209, ...), kind=kOutput, calls=%fused_computation.3.clone.1 | convolution fusion | flops 270532608 | bytes 5244420 | tf_op jit(solution)/shard_map/while/body/tji,tjk->tik/dot_general | solution.py:39
  56.0 4.7 %scatter_fusion = f32[48,128,128]{2,1,0:T(8,128)S(1)} fusion(f32[48,128,128]{2,1,0:T(8,128)S(1)} %get-tuple-element.225, s32[32]{0:T(128)S(1)} %compare_select_fusion.8, f32[32,128,128]{2,1,0:T(8,128)} %convolution_select_fusion.2), kind=kCustom, calls=%fused_computation.2.clone.1 | custom fusion | flops 524288 | bytes 6291584 | tf_op jit(solution)/shard_map/while/body/scatter-add | solution.py:41
  60.6 0.0 copy-done.3
  60.7 1.2 add_compare_fusion.2
  61.9 0.1 compare_select_fusion.8
  62.0 0.7 compare_and_fusion.3
  62.7 2.7 %gather_fusion.1 = bf16[32,128,128]{2,1,0:T(8,128)(2,1)} fusion(bf16[16,128,128]{2,1,0:T(8,128)(2,1)} %get-tuple-element.243, s32[1024]{0:T(1024)S(1)} %pad_clamp_fusion.5), kind=kCustom, calls=%fused_computation.clone.1 | custom fusion | bytes 2097280 | tf_op jit(solution)/shard_map/while/body/jit(_take)/gather | solution.py:38
  65.4 1.7 %gather_fusion = bf16[32,128,128]{2,1,0:T(8,128)(2,1)} fusion(bf16[12,128,128]{2,1,0:T(8,128)(2,1)S(1)} %get-tuple-element.245, s32[1024]{0:T(1024)S(1)} %pad_clamp_fusion.4), kind=kCustom, calls=%fused_computation.1.clone.1 | custom fusion | bytes 2097280 | tf_op jit(solution)/shard_map/while/body/jit(_take)/gather | solution.py:34
  67.0 4.1 %convolution_select_fusion.2 = f32[32,128,128]{2,1,0:T(8,128)} fusion(bf16[32,128,128]{2,1,0:T(8,128)(2,1)} %gather_fusion, bf16[128,128,128]{2,1,0:T(8,128)(2,1)} %get-tuple-element.244, s32[]{:T(128)S(6)} %select_n.97, bf16[32,128,128]{2,1,0:T(8,128)(2,1)} %gather_fusion.1, pred[32]{0:T(512)(128)(4,1)} %get-tuple-element.209, ...), kind=kOutput, calls=%fused_computation.3.clone.1 | convolution fusion | flops 270532608 | bytes 5244420 | tf_op jit(solution)/shard_map/while/body/tji,tjk->tik/dot_general | solution.py:39
  71.1 4.7 %scatter_fusion = f32[48,128,128]{2,1,0:T(8,128)S(1)} fusion(f32[48,128,128]{2,1,0:T(8,128)S(1)} %get-tuple-element.225, s32[32]{0:T(128)S(1)} %compare_select_fusion.8, f32[32,128,128]{2,1,0:T(8,128)} %convolution_select_fusion.2), kind=kCustom, calls=%fused_computation.2.clone.1 | custom fusion | flops 524288 | bytes 6291584 | tf_op jit(solution)/shard_map/while/body/scatter-add | solution.py:41
  75.8 0.0 copy-done.3
  75.8 1.2 add_compare_fusion.2
  77.1 0.1 compare_select_fusion.8
  77.2 0.7 compare_and_fusion.3
  77.9 2.7 %gather_fusion.1 = bf16[32,128,128]{2,1,0:T(8,128)(2,1)} fusion(bf16[16,128,128]{2,1,0:T(8,128)(2,1)} %get-tuple-element.243, s32[1024]{0:T(1024)S(1)} %pad_clamp_fusion.5), kind=kCustom, calls=%fused_computation.clone.1 | custom fusion | bytes 2097280 | tf_op jit(solution)/shard_map/while/body/jit(_take)/gather | solution.py:38
  80.6 1.7 %gather_fusion = bf16[32,128,128]{2,1,0:T(8,128)(2,1)} fusion(bf16[12,128,128]{2,1,0:T(8,128)(2,1)S(1)} %get-tuple-element.245, s32[1024]{0:T(1024)S(1)} %pad_clamp_fusion.4), kind=kCustom, calls=%fused_computation.1.clone.1 | custom fusion | bytes 2097280 | tf_op jit(solution)/shard_map/while/body/jit(_take)/gather | solution.py:34
  82.2 4.1 %convolution_select_fusion.2 = f32[32,128,128]{2,1,0:T(8,128)} fusion(bf16[32,128,128]{2,1,0:T(8,128)(2,1)} %gather_fusion, bf16[128,128,128]{2,1,0:T(8,128)(2,1)} %get-tuple-element.244, s32[]{:T(128)S(6)} %select_n.97, bf16[32,128,128]{2,1,0:T(8,128)(2,1)} %gather_fusion.1, pred[32]{0:T(512)(128)(4,1)} %get-tuple-element.209, ...), kind=kOutput, calls=%fused_computation.3.clone.1 | convolution fusion | flops 270532608 | bytes 5244420 | tf_op jit(solution)/shard_map/while/body/tji,tjk->tik/dot_general | solution.py:39
  86.3 4.7 %scatter_fusion = f32[48,128,128]{2,1,0:T(8,128)S(1)} fusion(f32[48,128,128]{2,1,0:T(8,128)S(1)} %get-tuple-element.225, s32[32]{0:T(128)S(1)} %compare_select_fusion.8, f32[32,128,128]{2,1,0:T(8,128)} %convolution_select_fusion.2), kind=kCustom, calls=%fused_computation.2.clone.1 | custom fusion | flops 524288 | bytes 6291584 | tf_op jit(solution)/shard_map/while/body/scatter-add | solution.py:41
  91.0 0.0 copy-done.3
  91.0 0.0 copy-start
  91.0 1.6 %copy-done = f32[48,128,128]{2,1,0:T(8,128)} copy-done((f32[48,128,128]{2,1,0:T(8,128)}, f32[48,128,128]{2,1,0:T(8,128)S(1)}, u32[]{:S(2)}) %copy-start) | copy-done | bytes 3145752
  92.7 0.0 reduce-scatter.2.cloned.1.call-update
  92.7 59.5 %reduce-scatter.2.cloned.1.call-done = f32[12,128,128]{2,1,0:T(8,128)} async-done(((f32[48,128,128]{2,1,0:T(8,128)}), f32[12,128,128]{2,1,0:T(8,128)}) %reduce-scatter.2.cloned.1.call-update) | async-done | bytes 786448 | tf_op jit(solution)/shard_map/reduce_scatter | solution.py:46
  152.2 1.9 %convert_element_type.9 = bf16[12,128,128]{2,1,0:T(8,128)(2,1)} convert(f32[12,128,128]{2,1,0:T(8,128)} %reduce-scatter.2.cloned.1.call-done) | non-fusion elementwise | flops 196608 | bytes 1179648 | tf_op jit(solution)/shard_map/convert_element_type | solution.py:47
  (14 shorter events, 0.1 us)
Async XLA Ops:
  6.5 23.7 %copy-start.2 = (s32[128]{0:T(128)S(1)}, s32[128]{0:T(128)}, u32[]{:S(2)}) copy-start(s32[128]{0:T(128)} %param.9) | copy-start | bytes 1540
  6.5 23.7 %copy-start.1 = (s32[128]{0:T(128)S(1)}, s32[128]{0:T(128)}, u32[]{:S(2)}) copy-start(s32[128]{0:T(128)} %param.8) | copy-start | bytes 1540
  6.5 145.7 %reduce-scatter.2.cloned.1.call-start = ((), (), s32[]{:S(2)}) async-start(), calls=%async_computation.1 | async-start | bytes 3932160 | tf_op jit(solution)/shard_map/reduce_scatter | solution.py:46
  6.5 22.4 %collective-permute-start = (bf16[4,128,128]{2,1,0:T(8,128)(2,1)}, bf16[4,128,128]{2,1,0:T(8,128)(2,1)S(1)}, u32[]{:S(2)}, u32[]{:S(2)}) collective-permute-start(bf16[4,128,128]{2,1,0:T(8,128)(2,1)} %param.11), channel_id=1, source_target_pairs={{28,0},{0,4},{4,8},{8,12},{12,16},{16,20},{20,24},{24,28},{29,1},{... | collective-permute-start | bytes 393224 | tf_op jit(solution)/shard_map/ppermute | solution.py:12
  7.0 21.9 %collective-permute-start.1 = (bf16[4,128,128]{2,1,0:T(8,128)(2,1)}, bf16[4,128,128]{2,1,0:T(8,128)(2,1)S(1)}, u32[]{:S(2)}, u32[]{:S(2)}) collective-permute-start(bf16[4,128,128]{2,1,0:T(8,128)(2,1)} %param.11), channel_id=1, source_target_pairs={{4,0},{8,4},{12,8},{16,12},{20,16},{24,20},{28,24},{0,28},{5,1},{9... | collective-permute-start | bytes 393224 | tf_op jit(solution)/shard_map/ppermute | solution.py:12
  40.8 4.7 %copy-start.3 = (s32[128]{0:T(128)S(1)}, s32[128]{0:T(128)}, u32[]{:S(2)}) copy-start(s32[128]{0:T(128)} %get-tuple-element.271) | copy-start | bytes 1540 | tf_op jit(solution)/shard_map/while
  55.9 4.7 %copy-start.3 = (s32[128]{0:T(128)S(1)}, s32[128]{0:T(128)}, u32[]{:S(2)}) copy-start(s32[128]{0:T(128)} %get-tuple-element.271) | copy-start | bytes 1540 | tf_op jit(solution)/shard_map/while
  71.1 4.7 %copy-start.3 = (s32[128]{0:T(128)S(1)}, s32[128]{0:T(128)}, u32[]{:S(2)}) copy-start(s32[128]{0:T(128)} %get-tuple-element.271) | copy-start | bytes 1540 | tf_op jit(solution)/shard_map/while
  86.3 4.7 %copy-start.3 = (s32[128]{0:T(128)S(1)}, s32[128]{0:T(128)}, u32[]{:S(2)}) copy-start(s32[128]{0:T(128)} %get-tuple-element.271) | copy-start | bytes 1540 | tf_op jit(solution)/shard_map/while
  91.0 1.7 %copy-start = (f32[48,128,128]{2,1,0:T(8,128)}, f32[48,128,128]{2,1,0:T(8,128)S(1)}, u32[]{:S(2)}) copy-start(f32[48,128,128]{2,1,0:T(8,128)S(1)} %get-tuple-element.259) | copy-start | bytes 9437188
Sparse Core Ops, SparseCore 0:
  92.8 59.3 reduce-scatter.1
where the time goes:
time: 162 us; the launch traced here: 161 us
  waiting for transfers between devices  59.5 us (37%)
  other arithmetic  29.6 us (18%)
  local copies, waits for them, and re-layouts  19.5 us (12%)
  blocking collectives  18.3 us (11%)
  matrix products  16.4 us (10%)
  between operations  14.1 us (9%)
  starting transfers between devices  3.39 us (2%)
    reduce_scatter x1, waiting for transfers between devices, shards(): summed = lax.psum_scatter(accum, 'col', scatter_dimension=0, tiled=True)  59.5 us
    scatter-add x4, other arithmetic, advance(): return accum.at[slots].add(terms)  18.7 us
    all_gather x1, blocking collectives, shards(): row_side = lax.all_gather(p_tiles, 'col', axis=0, tiled=True)  18.3 us
    dot_general x4, matrix products, advance(): jnp.einsum('tji,tjk->tik', left, image, preferred_element_type=jnp.float32)  16.4 us
    gather x4, local copies, waits for them, and re-layouts, advance(): left = jnp.take(row_side, rows, axis=0)  10.8 us
    gather x4, local copies, waits for them, and re-layouts, advance(): right = jnp.take(col_side, cols, axis=0)  6.66 us
    lt x4, other arithmetic, advance(): is_live = start + jnp.arange(block_size, dtype=jnp.int32) < count  4.97 us
    ppermute x2, starting transfers between devices, shifted(): return lax.ppermute(block, axis, route)  3.39 us
  transfers between devices with their start and end apart: 3, of which 1 were waited for; matrix products, arithmetic and copies ran while one was open for 0% of the time, Pallas kernels for 0%

commit v1 on v0

v1 whole, which is shorter than its diff:
```python
import functools

import jax
import jax.numpy as jnp
from jax import lax
from jax.experimental import pallas as pl
from jax.experimental.pallas import tpu as pltpu
from jax.sharding import PartitionSpec as P

UNROLL = 4
LIMIT = 40 * 1024 * 1024
VMEM = pl.BlockSpec(memory_space=pltpu.VMEM)
SMEM = pl.BlockSpec(memory_space=pltpu.SMEM)


def bits(extent):
    return (extent - 1).bit_length()


def plan_kernel(held, chunk, a_row, a_col, a_count, items, counts):
    slots, n = a_row.shape[0], counts.shape[0]
    for d in range(n):
        counts[d] = 0

    def place(t, carry):
        row, col = a_row[t], a_col[t]
        place = row % held * (3 * held) + col
        d = place // chunk
        at = counts[d]
        item = (row << bits(3 * held)) + col
        item = (item << bits(chunk)) + place - d * chunk
        items[d * slots + at] = (item << bits(slots)) + t
        counts[d] = at + 1
        return carry

    lax.fori_loop(0, a_count[0], place, 0)


def plan(held, chunk, n, a_row, a_col, a_count):
    return pl.pallas_call(
        functools.partial(plan_kernel, held, chunk),
        out_shape=(
            jax.ShapeDtypeStruct((n * a_row.shape[0],), jnp.int32),
            jax.ShapeDtypeStruct((n,), jnp.int32),
        ),
        in_specs=[SMEM] * 3,
        out_specs=(SMEM, SMEM),
        name="plan",
    )(a_row, a_col, a_count)


def chunk_kernel(held, chunk, n_right, n_left, dest, items, counts, a, *rest):
    rights, lefts = rest[:n_right], rest[n_right : n_right + n_left]
    out, right, left, accum = rest[n_right + n_left :]
    slots = a.shape[0]
    d = dest[0]
    base, count = d * slots, counts[d]
    for i in range(n_right):
        right[i * held : (i + 1) * held] = rights[i][...]
    at = 0
    for ref in lefts:
        for i in range(ref.shape[0]):
            left[at] = ref[i].T
            at += 1
    accum[...] = jnp.zeros_like(accum)

    def advance(step, carry):
        for u in range(UNROLL):
            e = step * UNROLL + u
            item = items[base + jnp.minimum(e, count - 1)]
            t, item = item & ((1 << bits(slots)) - 1), item >> bits(slots)
            s, item = item & ((1 << bits(chunk)) - 1), item >> bits(chunk)
            col, row = item & ((1 << bits(3 * held)) - 1), item >> bits(3 * held)
            s = jnp.where(e < count, s, chunk)
            image = jnp.dot(a[t], right[col], preferred_element_type=jnp.float32)
            accum[s] += jnp.dot(
                left[row], image.astype(jnp.bfloat16), preferred_element_type=jnp.float32
            )
        return carry

    lax.fori_loop(0, (count + UNROLL - 1) // UNROLL, advance, 0)
    out[...] = accum[:chunk].astype(out.dtype)


def coarse_chunk(held, chunk, dest, items, counts, a, rights, lefts, dtype):
    width = a.shape[1]
    n_left = sum(x.shape[0] for x in lefts)
    return pl.pallas_call(
        functools.partial(chunk_kernel, held, chunk, len(rights), len(lefts)),
        out_shape=jax.ShapeDtypeStruct((chunk, width, width), dtype),
        in_specs=[SMEM] * 3 + [VMEM] * (1 + len(rights) + len(lefts)),
        out_specs=VMEM,
        scratch_shapes=[
            pltpu.VMEM((3 * held, width, width), jnp.bfloat16),
            pltpu.VMEM((n_left, width, width), jnp.bfloat16),
            pltpu.VMEM((chunk + 1, width, width), jnp.float32),
        ],
        compiler_params=pltpu.CompilerParams(vmem_limit_bytes=LIMIT),
        name="coarse_chunk",
    )(dest, items, counts, a, *rights, *lefts)


def shifted(block, axis, distance):
    n = lax.axis_size(axis)
    return lax.ppermute(block, axis, [((i - distance) % n, i) for i in range(n)])


def shards(a_tiles, a_row, a_col, a_count, p_tiles):
    n, me = lax.axis_size("col"), lax.axis_index("col")
    held = p_tiles.shape[0]
    total = 3 * held * held
    chunk = total // n
    rights = [shifted(p_tiles, "row", 1), p_tiles, shifted(p_tiles, "row", -1)]
    row_side = lax.all_gather(p_tiles, "col", axis=0, tiled=True)
    items, counts = plan(held, total, 1, a_row, a_col, a_count)
    zero = jnp.zeros((1,), jnp.int32)
    sums = coarse_chunk(held, total, zero, items, counts, a_tiles, rights, [row_side], jnp.bfloat16)
    parts = sums.reshape(n, chunk, *sums.shape[1:])
    parts = lax.all_to_all(parts, "col", 0, 0, tiled=True)
    return jnp.sum(parts.astype(jnp.float32), axis=0).astype(jnp.bfloat16)


def solution(mesh):
    in_specs = (
        P(("row", "col"), None, None),
        P(("row", "col")),
        P(("row", "col")),
        P(("row", "col")),
        P(("row", "col"), None, None),
    )
    out_specs = P(("row", "col"), None, None)
    return jax.shard_map(shards, mesh=mesh, in_specs=in_specs, out_specs=out_specs, check_vma=False)
```

time: 162 us -> 79.3 us (0.49)
  the two profiles are of different devices: /device:TPU:0 before, /device:TPU:2 now
where the time goes in v1:
time: 79.3 us; the launch traced here: 78.2 us
  blocking collectives  65.7 us (83%)
  Pallas kernels  6.47 us (8%)
  local copies, waits for them, and re-layouts  3.74 us (5%)
  other arithmetic  1.11 us (1%)
    all_to_all x1, blocking collectives, shards(): parts = lax.all_to_all(parts, 'col', 0, 0, tiled=True)  48.8 us
    all_gather x1, blocking collectives, shards(): row_side = lax.all_gather(p_tiles, 'col', axis=0, tiled=True)  16.9 us
    pallas_call x1, Pallas kernels, coarse_chunk(): pl.pallas_call(functools.partial(chunk_kernel, held, chunk, len(rights),...  4.42 us
    unnamed x6, local copies, waits for them, and re-layouts  3.74 us
    pallas_call x1, Pallas kernels, plan(): pl.pallas_call(functools.partial(plan_kernel, held, chunk), out_shape=(ja...  2.06 us
  transfers between devices with their start and end apart: 2, of which 0 were waited for; matrix products, arithmetic and copies ran while one was open for 0% of the time, Pallas kernels for 3%

profile of v1, /device:TPU:2, one launch (start us, length us, event | category | flops | bytes accessed | tf_op | source)
XLA Modules:
  0.0 78.2 jit_solution(12211720364886604841)
XLA Ops:
  0.0 0.0 collective-permute-start.1
  0.0 0.5 collective-permute-start
  1.2 2.1 %plan.1 = (s32[128]{0:T(128)}, s32[1]{0:T(128)}) custom-call(s32[128]{0:T(128)} %a_row.1, s32[128]{0:T(128)} %a_col.1, s32[1]{0:T(128)S(6)} %copy.6.a_count), custom_call_target="tpu_custom_call" | custom-call | tf_op jit(solution)/shard_map/plan/pallas_call | solution.py:40
  3.2 16.9 %all_gather.3.rest_3_ = bf16[16,128,128]{2,1,0:T(8,128)(2,1)S(1)} all-gather(bf16[4,128,128]{2,1,0:T(8,128)(2,1)} %rest_1_.1), channel_id=1, replica_groups=mesh['row'=8,'col'=4] {'col'}, dimensions={0}, use_global_device_ids=true | all-gather | bytes 655360 | tf_op jit(solution)/shard_map/all_gather | solution.py:114
  20.2 0.0 collective-permute-done.1.rest_2_
  20.2 0.0 collective-permute-done.rest_0_
  20.2 0.0 copy-start
  20.2 2.2 %copy-done = bf16[128,128,128]{2,1,0:T(8,128)(2,1)S(1)} copy-done((bf16[128,128,128]{2,1,0:T(8,128)(2,1)S(1)}, bf16[128,128,128]{2,1,0:T(8,128)(2,1)}, u32[]{:S(2)}) %copy-start) | copy-done | bytes 4194328
  22.4 0.0 copy-start.1
  22.4 0.9 %copy-done.1 = bf16[4,128,128]{2,1,0:T(8,128)(2,1)S(1)} copy-done((bf16[4,128,128]{2,1,0:T(8,128)(2,1)S(1)}, bf16[4,128,128]{2,1,0:T(8,128)(2,1)}, u32[]{:S(2)}) %copy-start.1) | copy-done | bytes 131096
  23.3 0.0 copy-start.2
  23.3 0.7 copy-done.2
  23.9 4.4 %coarse_chunk.1 = bf16[48,128,128]{2,1,0:T(8,128)(2,1)S(1)} custom-call(s32[1]{0:T(128)} %constant.1.clone.1.dest, s32[128]{0:T(128)S(1)} %copy-done.2, s32[1]{0:T(128)} %get-tuple-element.8.counts, bf16[128,128,128]{2,1,0:T(8,128)(2,1)S(1)} %copy-done, bf16[4,128,128]{2,1,0:T(8,128)(2,1)S(1)} %collective-permute-done.rest_0_, ...), custom_call_target="tpu_custom_call" | custom-call | tf_op jit(solution)/shard_map/coarse_chunk/pallas_call | solution.py:88
  28.4 48.8 %all_to_all.5 = bf16[4,12,128,128]{3,2,1,0:T(8,128)(2,1)S(1)} all-to-all(bf16[4,12,128,128]{3,2,1,0:T(8,128)(2,1)S(1)} %bitcast.1), channel_id=1, replica_groups=mesh['row'=8,'col'=4] {'col'}, dimensions={0} | all-to-all | bytes 3145728 | tf_op jit(solution)/shard_map/all_to_all | solution.py:119
  77.1 1.1 %reduce_sum.12 = bf16[12,128,128]{2,1,0:T(8,128)(2,1)} reduce(bf16[4,12,128,128]{3,2,1,0:T(8,128)(2,1)S(1)} %all_to_all.5, bf16[]{:T(256)} %constant.4.clone.1), dimensions={0}, to_apply=%region_0.0 | reduce | flops 589824 | bytes 1966082 | tf_op jit(solution)/shard_map/reduce_sum | solution.py:120
Async XLA Ops:
  0.0 20.2 %collective-permute-start.1 = (bf16[4,128,128]{2,1,0:T(8,128)(2,1)}, bf16[4,128,128]{2,1,0:T(8,128)(2,1)S(1)}, u32[]{:S(2)}, u32[]{:S(2)}) collective-permute-start(bf16[4,128,128]{2,1,0:T(8,128)(2,1)} %rest_1_.1), channel_id=1, source_target_pairs={{4,0},{8,4},{12,8},{16,12},{20,16},{24,20},{28,24},{0,28},{5,1},{9... | collective-permute-start | bytes 393224 | tf_op jit(solution)/shard_map/ppermute | solution.py:105
  0.0 20.2 %collective-permute-start = (bf16[4,128,128]{2,1,0:T(8,128)(2,1)}, bf16[4,128,128]{2,1,0:T(8,128)(2,1)S(1)}, u32[]{:S(2)}, u32[]{:S(2)}) collective-permute-start(bf16[4,128,128]{2,1,0:T(8,128)(2,1)} %rest_1_.1), channel_id=1, source_target_pairs={{28,0},{0,4},{4,8},{8,12},{12,16},{16,20},{20,24},{24,28},{29,1},{... | collective-permute-start | bytes 393224 | tf_op jit(solution)/shard_map/ppermute | solution.py:105
  20.2 2.2 %copy-start = (bf16[128,128,128]{2,1,0:T(8,128)(2,1)S(1)}, bf16[128,128,128]{2,1,0:T(8,128)(2,1)}, u32[]{:S(2)}) copy-start(bf16[128,128,128]{2,1,0:T(8,128)(2,1)} %a.1) | copy-start | bytes 12582916
  22.4 0.9 %copy-start.1 = (bf16[4,128,128]{2,1,0:T(8,128)(2,1)S(1)}, bf16[4,128,128]{2,1,0:T(8,128)(2,1)}, u32[]{:S(2)}) copy-start(bf16[4,128,128]{2,1,0:T(8,128)(2,1)} %rest_1_.1) | copy-start | bytes 393220
  23.3 0.7 copy-start.2

commit v2 on v0

v2 whole, which is shorter than its diff:
```python
import functools

import jax
import jax.numpy as jnp
from jax import lax
from jax.experimental import pallas as pl
from jax.experimental.pallas import tpu as pltpu
from jax.sharding import PartitionSpec as P

UNROLLS = (16, 4)
LIMIT = 12 * 1024 * 1024
VMEM = pl.BlockSpec(memory_space=pltpu.VMEM)
SMEM = pl.BlockSpec(memory_space=pltpu.SMEM)
HBM = pl.BlockSpec(memory_space=pltpu.HBM)


def bits(extent):
    return (extent - 1).bit_length()


def divide(x, n):
    if n & (n - 1):
        return lax.div(x, n), lax.rem(x, n)
    return x >> bits(n), x & (n - 1)


def plan_kernel(held, n, me, a_row, a_col, a_count, a, p, items, counts, a_out, p_out, sems):
    slots = a_row.shape[0]
    copies = [pltpu.make_async_copy(p, p_out, sems.at[0]), pltpu.make_async_copy(a, a_out, sems.at[1])]
    for copy in copies:
        copy.start()
    field = 32 // n
    group = 8 if slots % 8 == 0 else 1
    live = a_count[0]

    def place(step, taken):
        for u in range(group):
            t = step * group + u
            row, col = a_row[t], a_col[t]
            d = divide(divide(row, held)[1] * n, held)[0]
            at = (taken >> (d * field)) & ((1 << min(field, 16)) - 1)
            items[d * slots + at] = t + (col << bits(slots)) + (row << (bits(slots) + bits(3 * held)))
            taken = taken + (jnp.where(t < live, 1, 0) << (d * field))
        return taken

    taken = lax.fori_loop(0, lax.div(live + group - 1, group), place, jnp.int32(0))
    for d in range(n):
        counts[d] = (taken >> (d * field)) & ((1 << min(field, 16)) - 1)
    counts[n] = me[0]
    for copy in copies:
        copy.wait()


def plan(held, n, me, a_row, a_col, a_count, a_tiles, p_tiles):
    return pl.pallas_call(
        functools.partial(plan_kernel, held, n),
        out_shape=(
            jax.ShapeDtypeStruct((n * a_row.shape[0],), jnp.int32),
            jax.ShapeDtypeStruct((n + 1,), jnp.int32),
            pltpu.VMEM(a_tiles.shape, a_tiles.dtype),
            pltpu.VMEM(p_tiles.shape, p_tiles.dtype),
        ),
        in_specs=[SMEM] * 4 + [HBM] * 2,
        out_specs=(SMEM, SMEM, VMEM, VMEM),
        scratch_shapes=[pltpu.SemaphoreType.DMA((2,))],
        compiler_params=pltpu.CompilerParams(vmem_limit_bytes=LIMIT),
        name="plan",
    )(me, a_row, a_col, a_count, a_tiles, p_tiles)


def chunk_kernel(held, flip, n_left, n_out, items, counts, a, below, own, above, *rest):
    lefts, outs, (right, left, accum) = rest[:n_left], rest[-3 - n_out : -3], rest[-3:]
    slots, chunk = a.shape[0], outs[0].shape[0]
    me = counts[counts.shape[0] - 1]
    d = 0 if flip is None else me ^ flip
    base, count = d * slots, counts[d]
    for i, ref in enumerate((below, own, above)):
        right[i * held : (i + 1) * held] = ref[...]
    if flip is None:
        for i in range(left.shape[0]):
            left[i] = lefts[0][i].T
    else:
        for i in range(n_left):
            left[i] = lefts[i][d].T
    accum[...] = jnp.zeros_like(accum)

    def take(e):
        item = items[base + jnp.minimum(e, count - 1)]
        t, item = item & ((1 << bits(slots)) - 1), item >> bits(slots)
        col, row = item & ((1 << bits(3 * held)) - 1), item >> bits(3 * held)
        if flip is None:
            s = divide(row, held)[1] * (3 * held) + col
        else:
            row, s = divide(row, held)[0] ^ me, col
        s = jnp.where(e < count, s, chunk)
        image = jnp.dot(a[t], right[col], preferred_element_type=jnp.float32)
        accum[s] += jnp.dot(left[row], image.astype(jnp.bfloat16), preferred_element_type=jnp.float32)

    done = jnp.int32(0)
    for unroll in UNROLLS:

        def advance(step, carry, done=done, unroll=unroll):
            for u in range(unroll):
                take(done + step * unroll + u)
            return carry

        spare = unroll - 1 if unroll == UNROLLS[-1] else 0
        steps = lax.div(count - done + spare, unroll)
        lax.fori_loop(0, steps, advance, 0)
        done = done + steps * unroll
    for out in outs:
        out[...] = accum[:chunk].astype(out.dtype)


def coarse_chunk(flip, listed, rights, lefts, dtypes, after=()):
    items, counts, a = listed
    held, width = rights[0].shape[0], a.shape[1]
    chunk = 3 * held * (held if flip is None else 1)
    n_left = lefts[0].shape[0] if flip is None else len(lefts)
    return pl.pallas_call(
        functools.partial(chunk_kernel, held, flip, len(lefts), len(dtypes)),
        out_shape=[jax.ShapeDtypeStruct((chunk, width, width), dtype) for dtype in dtypes],
        in_specs=[SMEM] * 2 + [VMEM] * (4 + len(lefts)) + [pl.BlockSpec(memory_space=pl.ANY)] * len(after),
        out_specs=[VMEM] * len(dtypes),
        scratch_shapes=[
            pltpu.VMEM((3 * held, width, width), jnp.bfloat16),
            pltpu.VMEM((n_left, width, width), jnp.bfloat16),
            pltpu.VMEM((chunk + 1, width, width), jnp.float32),
        ],
        compiler_params=pltpu.CompilerParams(vmem_limit_bytes=LIMIT),
        cost_estimate=pl.CostEstimate(flops=1 << 31, bytes_accessed=1 << 20, transcendentals=0),
        name="coarse_chunk",
    )(items, counts, a, *rights, *lefts, *after)


def add_kernel(n, *refs):
    xs, out = refs[:n], refs[-1]
    total = xs[0][...]
    for x in xs[1:]:
        total = total.astype(jnp.float32) + x[...].astype(jnp.float32)
    out[...] = total.astype(out.dtype)


def added(xs, dtype, after=()):
    return pl.pallas_call(
        functools.partial(add_kernel, len(xs)),
        out_shape=jax.ShapeDtypeStruct(xs[0].shape, dtype),
        in_specs=[VMEM] * len(xs) + [pl.BlockSpec(memory_space=pl.ANY)] * len(after),
        out_specs=VMEM,
        compiler_params=pltpu.CompilerParams(vmem_limit_bytes=LIMIT),
        name="added",
    )(*xs, *after)


def shifted(block, axis, distance):
    n = lax.axis_size(axis)
    return lax.ppermute(block, axis, [((i - distance) % n, i) for i in range(n)])


def line_of_four(a_tiles, a_row, a_col, a_count, p_tiles):
    me = lax.axis_index("col").reshape(1)
    held, width = p_tiles.shape[:2]
    stay = lambda x: pltpu.with_memory_space_constraint(x, pltpu.HBM)
    a_tiles, a_row, a_col, p_tiles = stay(a_tiles), stay(a_row), stay(a_col), stay(p_tiles)
    cross = lambda block, pairs: lax.ppermute(block, "col", pairs)
    flips = [[(i, i ^ m) for i in range(4)] for m in range(4)]
    far = {m: cross(p_tiles, flips[m]) for m in (2, 3, 1)}
    items, counts, a, own = plan(held, 4, me, a_row, a_col, a_count, a_tiles, p_tiles)
    below, above = shifted(own, "row", 1), shifted(own, "row", -1)
    keep = lambda x: pltpu.with_memory_space_constraint(x, pltpu.VMEM)
    listed = (items, counts, a)
    rights, lefts = [keep(below), own, keep(above)], [own] + [keep(far[m]) for m in (1, 2, 3)]

    bf16, f32 = jnp.bfloat16, jnp.float32
    (first,) = coarse_chunk(3, listed, rights, lefts, [bf16])
    got1 = cross(first, [(0, 1), (3, 2)])
    got3 = cross(added([first], bf16), [(1, 2), (2, 1)])
    second, wide = coarse_chunk(2, listed, rights, lefts, [bf16, f32], [first])
    got5 = cross(second, [(0, 2), (3, 1)])
    (third,) = coarse_chunk(1, listed, rights, lefts, [bf16], [second])
    got2 = cross(third, flips[1])
    joined = added([wide, got1], bf16, [third])
    got4 = cross(joined, [(1, 3), (2, 0)])
    (last,) = coarse_chunk(0, listed, rights, lefts, [f32], [joined])
    return added([last, got3, got5, got2, got4], bf16)


def any_columns(a_tiles, a_row, a_col, a_count, p_tiles):
    n = lax.axis_size("col")
    held = p_tiles.shape[0]
    total = 3 * held * held
    rights = [shifted(p_tiles, "row", 1), p_tiles, shifted(p_tiles, "row", -1)]
    row_side = lax.all_gather(p_tiles, "col", axis=0, tiled=True)
    me = jnp.zeros((1,), jnp.int32)
    items, counts, a, own = plan(held, 1, me, a_row, a_col, a_count, a_tiles, p_tiles)
    rights = (rights[0], own, rights[2])
    (sums,) = coarse_chunk(None, (items, counts, a), rights, [row_side], [jnp.bfloat16])
    parts = sums.reshape(n, total // n, *sums.shape[1:])
    parts = lax.all_to_all(parts, "col", 0, 0, tiled=True)
    return jnp.sum(parts.astype(jnp.float32), axis=0).astype(jnp.bfloat16)


def shards(a_tiles, a_row, a_col, a_count, p_tiles):
    special = lax.axis_size("col") == 4 and p_tiles.shape[0] == 4
    body = line_of_four if special else any_columns
    return body(a_tiles, a_row, a_col, a_count, p_tiles)


def solution(mesh):
    in_specs = (
        P(("row", "col"), None, None),
        P(("row", "col")),
        P(("row", "col")),
        P(("row", "col")),
        P(("row", "col"), None, None),
    )
    out_specs = P(("row", "col"), None, None)
    return jax.shard_map(shards, mesh=mesh, in_specs=in_specs, out_specs=out_specs, check_vma=False)
```

time: 162 us -> 50.7 us (0.31)
  waiting for transfers between devices: 59.5 us -> 20.5 us
  other arithmetic: 29.6 us -> 0 us
  local copies, waits for them, and re-layouts: 19.5 us -> 0 us
  blocking collectives: 18.3 us -> 0 us
  matrix products: 16.4 us -> 0 us
  Pallas kernels: 0 us -> 14 us
  between operations: 14.1 us -> 0.77 us
  starting transfers between devices: 3.39 us -> 15.1 us
    reduce_scatter x1 -> x0, waiting for transfers between devices: 59.5 us -> none  [shards(): summed = lax.psum_scatter(accum, 'col', scatter_dimension=0, tiled=True)]
    ppermute x2 -> x10, waiting for transfers between devices: 0.01 us -> 20.5 us  [the longest x8 20.5 us: line_of_four(): cross = lambda block, pairs: lax.ppermute(block, 'col', pairs)]
    scatter-add x4 -> x0, other arithmetic: 18.7 us -> none  [advance(): return accum.at[slots].add(terms)]
    all_gather x1 -> x0, blocking collectives: 18.3 us -> none  [shards(): row_side = lax.all_gather(p_tiles, 'col', axis=0, tiled=True)]
    gather x8 -> x0, local copies, waits for them, and re-layouts: 17.5 us -> none  [the longest x4 10.8 us: advance(): left = jnp.take(row_side, rows, axis=0)]
    dot_general x4 -> x0, matrix products: 16.4 us -> none  [advance(): jnp.einsum('tji,tjk->tik', left, image, preferred_element_type=jnp.float32)]
    pallas_call x0 -> x8, Pallas kernels: none -> 14 us  [the longest x4 9.34 us: coarse_chunk(): pl.pallas_call(functools.partial(chunk_kernel, held, flip, len(lefts), le...]
    ppermute x2 -> x10, starting transfers between devices: 3.39 us -> 15.1 us  [the longest x8 13.7 us: line_of_four(): cross = lambda block, pairs: lax.ppermute(block, 'col', pairs)]
  transfers between devices with their start and end apart: 3 -> 10, of which waited for: 1 -> 4; matrix products, arithmetic and copies ran while one was open for 0% -> 0% of each run, Pallas kernels for 0% -> 22%
where the time goes in v2:
time: 50.7 us; the launch traced here: 50.3 us
  waiting for transfers between devices  20.5 us (40%)
  starting transfers between devices  15.1 us (30%)
  Pallas kernels  14 us (28%)
  between operations  0.77 us (2%)
    ppermute x8, waiting for transfers between devices, line_of_four(): cross = lambda block, pairs: lax.ppermute(block, 'col', pairs)  20.5 us
    ppermute x8, starting transfers between devices, line_of_four(): cross = lambda block, pairs: lax.ppermute(block, 'col', pairs)  13.7 us
    pallas_call x4, Pallas kernels, coarse_chunk(): pl.pallas_call(functools.partial(chunk_kernel, held, flip, len(lefts), le...  9.34 us
    pallas_call x1, Pallas kernels, plan(): pl.pallas_call(functools.partial(plan_kernel, held, n), out_shape=(jax.Sh...  3.58 us
    ppermute x2, starting transfers between devices, shifted(): lax.ppermute(block, axis, [((i - distance) % n, i) for i in range(n)])  1.38 us
    pallas_call x3, Pallas kernels, added(): pl.pallas_call(functools.partial(add_kernel, len(xs)), out_shape=jax.Shap...  1.06 us
  transfers between devices with their start and end apart: 10, of which 4 were waited for; matrix products, arithmetic and copies ran while one was open for 0% of the time, Pallas kernels for 22%

profile of v2, /device:TPU:0, one launch (start us, length us, event | category | flops | bytes accessed | tf_op | source)
XLA Modules:
  0.0 50.3 jit_solution(14608772888613045159)
XLA Ops:
  0.0 3.0 %collective-permute-start.2 = (bf16[4,128,128]{2,1,0:T(8,128)(2,1)}, bf16[4,128,128]{2,1,0:T(8,128)(2,1)S(1)}, u32[]{:S(2)}, u32[]{:S(2)}) collective-permute-start(bf16[4,128,128]{2,1,0:T(8,128)(2,1)} %p.1), channel_id=1, source_target_pairs={{0,1},{1,0},{2,3},{3,2},{4,5},{5,4},{6,7},{7,6},{8,9},{9,8},{10,11... | collective-permute-start | bytes 393224 | tf_op jit(solution)/shard_map/ppermute | solution.py:165
  3.0 2.5 %collective-permute-start.4 = (bf16[4,128,128]{2,1,0:T(8,128)(2,1)}, bf16[4,128,128]{2,1,0:T(8,128)(2,1)S(1)}, u32[]{:S(2)}, u32[]{:S(2)}) collective-permute-start(bf16[4,128,128]{2,1,0:T(8,128)(2,1)} %p.1), channel_id=1, source_target_pairs={{0,3},{1,2},{2,1},{3,0},{4,7},{5,6},{6,5},{7,4},{8,11},{9,10},{10,... | collective-permute-start | bytes 393224 | tf_op jit(solution)/shard_map/ppermute | solution.py:165
  5.5 0.1 collective-permute-start.3
  6.3 3.6 %plan.1 = (s32[512]{0:T(512)S(1)}, s32[5]{0:T(128)S(1)}, bf16[128,128,128]{2,1,0:T(8,128)(2,1)S(1)}, bf16[4,128,128]{2,1,0:T(8,128)(2,1)S(1)}) custom-call(s32[1]{0:T(128)} %bitcast.me, s32[128]{0:T(128)} %a_row.1, s32[128]{0:T(128)} %a_col.1, s32[1]{0:T(128)S(6)} %copy.6.a_count, bf16[128,128,128]{2,1,0:T(8,128)(2,1)} %a.1, bf16[4,128,128]{2,1,0:T(8,128)(2,1)} %p.1), custom_call_target="tpu_custom_call" | custom-call | tf_op jit(solution)/shard_map/plan/pallas_call | solution.py:55
  9.9 1.4 %collective-permute-start.1 = (bf16[4,128,128]{2,1,0:T(8,128)(2,1)S(1)}, bf16[4,128,128]{2,1,0:T(8,128)(2,1)S(1)}, u32[]{:S(2)}, u32[]{:S(2)}) collective-permute-start(bf16[4,128,128]{2,1,0:T(8,128)(2,1)S(1)} %get-tuple-element.14.own.rest_0_), channel_id=1, source_target_pairs={{4,0},{8,4},{12,8},{16,12},{20,16},{24,20},{28,24},{0,28},{5,1},{9... | collective-permute-start | bytes 393224 | tf_op jit(solution)/shard_map/ppermute | solution.py:157
  11.2 0.0 collective-permute-start
  11.2 0.0 collective-permute-done.2.rest_1_
  11.2 1.7 %collective-permute-done.4.rest_3_ = bf16[4,128,128]{2,1,0:T(8,128)(2,1)S(1)} collective-permute-done((bf16[4,128,128]{2,1,0:T(8,128)(2,1)}, bf16[4,128,128]{2,1,0:T(8,128)(2,1)S(1)}, u32[]{:S(2)}, u32[]{:S(2)}) %collective-permute-start.4) | collective-permute-done | bytes 131104 | tf_op jit(solution)/shard_map/ppermute | solution.py:165
  13.0 4.5 %collective-permute-done.3.rest_2_ = bf16[4,128,128]{2,1,0:T(8,128)(2,1)S(1)} collective-permute-done((bf16[4,128,128]{2,1,0:T(8,128)(2,1)}, bf16[4,128,128]{2,1,0:T(8,128)(2,1)S(1)}, u32[]{:S(2)}, u32[]{:S(2)}) %collective-permute-start.3) | collective-permute-done | bytes 131104 | tf_op jit(solution)/shard_map/ppermute | solution.py:165
  17.5 0.0 collective-permute-done.1.above
  17.5 0.0 collective-permute-done.below
  17.5 1.8 %coarse_chunk.4.rest_4_.refs_0_ = bf16[12,128,128]{2,1,0:T(8,128)(2,1)S(1)} custom-call(s32[512]{0:T(512)S(1)} %get-tuple-element.11.items, s32[5]{0:T(128)S(1)} %get-tuple-element.12.counts, bf16[128,128,128]{2,1,0:T(8,128)(2,1)S(1)} %get-tuple-element.13.a, bf16[4,128,128]{2,1,0:T(8,128)(2,1)S(1)} %collective-permute-done.below, ...), custom_call_target="tpu_custom_call" | custom-call | flops 2147483648 | bytes 1048576 | tf_op jit(solution)/shard_map/coarse_chunk/pallas_call | solution.py:120
  19.4 2.5 %collective-permute-start.5 = (bf16[12,128,128]{2,1,0:T(8,128)(2,1)S(1)}, bf16[12,128,128]{2,1,0:T(8,128)(2,1)S(1)}, u32[]{:S(2)}, u32[]{:S(2)}) collective-permute-start(bf16[12,128,128]{2,1,0:T(8,128)(2,1)S(1)} %coarse_chunk.4.rest_4_.refs_0_), channel_id=1, source_target_pairs={{0,1},{3,2},{4,5},{7,6},{8,9},{11,10},{12,13},{15,14},{16,17},{19,... | collective-permute-start | bytes 1179656 | tf_op jit(solution)/shard_map/ppermute | solution.py:165
  21.9 0.7 %collective-permute-start.6 = (bf16[12,128,128]{2,1,0:T(8,128)(2,1)S(1)}, bf16[12,128,128]{2,1,0:T(8,128)(2,1)S(1)}, u32[]{:S(2)}, u32[]{:S(2)}) collective-permute-start(bf16[12,128,128]{2,1,0:T(8,128)(2,1)S(1)} %added.4), channel_id=1, source_target_pairs={{1,2},{2,1},{5,6},{6,5},{9,10},{10,9},{13,14},{14,13},{17,18},{18,... | collective-permute-start | bytes 1179656 | tf_op jit(solution)/shard_map/ppermute | solution.py:165
  22.6 2.7 %coarse_chunk.5 = (bf16[12,128,128]{2,1,0:T(8,128)(2,1)S(1)}, f32[12,128,128]{2,1,0:T(8,128)S(1)}) custom-call(s32[512]{0:T(512)S(1)} %get-tuple-element.11.items, s32[5]{0:T(128)S(1)} %get-tuple-element.12.counts, bf16[128,128,128]{2,1,0:T(8,128)(2,1)S(1)} %get-tuple-element.13.a, bf16[4,128,128]{2,1,0:T(8,128)(2,1)S(1)} %collective-permute-done.below, ...), custom_call_target="tpu_custom_call" | custom-call | flops 2147483648 | bytes 1048576 | tf_op jit(solution)/shard_map/coarse_chunk/pallas_call | solution.py:120
  25.3 3.5 %collective-permute-start.7 = (bf16[12,128,128]{2,1,0:T(8,128)(2,1)S(1)}, bf16[12,128,128]{2,1,0:T(8,128)(2,1)S(1)}, u32[]{:S(2)}, u32[]{:S(2)}) collective-permute-start(bf16[12,128,128]{2,1,0:T(8,128)(2,1)S(1)} %get-tuple-element.16.rest_4_), channel_id=1, source_target_pairs={{0,2},{3,1},{4,6},{7,5},{8,10},{11,9},{12,14},{15,13},{16,18},{19,... | collective-permute-start | bytes 1179656 | tf_op jit(solution)/shard_map/ppermute | solution.py:165
  28.8 2.6 %coarse_chunk.6.refs_2_ = bf16[12,128,128]{2,1,0:T(8,128)(2,1)S(1)} custom-call(s32[512]{0:T(512)S(1)} %get-tuple-element.11.items, s32[5]{0:T(128)S(1)} %get-tuple-element.12.counts, bf16[128,128,128]{2,1,0:T(8,128)(2,1)S(1)} %get-tuple-element.13.a, bf16[4,128,128]{2,1,0:T(8,128)(2,1)S(1)} %collective-permute-done.below, ...), custom_call_target="tpu_custom_call" | custom-call | flops 2147483648 | bytes 1048576 | tf_op jit(solution)/shard_map/coarse_chunk/pallas_call | solution.py:120
  31.4 0.1 collective-permute-start.8
  31.5 0.0 collective-permute-done.5.refs_1_
  31.5 0.1 added.3.rest_4_
  31.6 1.3 %collective-permute-start.9 = (bf16[12,128,128]{2,1,0:T(8,128)(2,1)S(1)}, bf16[12,128,128]{2,1,0:T(8,128)(2,1)S(1)}, u32[]{:S(2)}, u32[]{:S(2)}) collective-permute-start(bf16[12,128,128]{2,1,0:T(8,128)(2,1)S(1)} %added.3.rest_4_), channel_id=1, source_target_pairs={{1,3},{2,0},{5,7},{6,4},{9,11},{10,8},{13,15},{14,12},{17,19},{18,... | collective-permute-start | bytes 1179656 | tf_op jit(solution)/shard_map/ppermute | solution.py:165
  32.9 2.2 %coarse_chunk.7.refs_0_ = f32[12,128,128]{2,1,0:T(8,128)S(1)} custom-call(s32[512]{0:T(512)S(1)} %get-tuple-element.11.items, s32[5]{0:T(128)S(1)} %get-tuple-element.12.counts, bf16[128,128,128]{2,1,0:T(8,128)(2,1)S(1)} %get-tuple-element.13.a, bf16[4,128,128]{2,1,0:T(8,128)(2,1)S(1)} %collective-permute-done.below, ...), custom_call_target="tpu_custom_call" | custom-call | flops 2147483648 | bytes 1048576 | tf_op jit(solution)/shard_map/coarse_chunk/pallas_call | solution.py:120
  35.1 0.0 collective-permute-done.6.refs_1_
  35.1 10.3 %collective-permute-done.8.refs_3_ = bf16[12,128,128]{2,1,0:T(8,128)(2,1)S(1)} collective-permute-done((bf16[12,128,128]{2,1,0:T(8,128)(2,1)S(1)}, bf16[12,128,128]{2,1,0:T(8,128)(2,1)S(1)}, u32[]{:S(2)}, u32[]{:S(2)}) %collective-permute-start.8) | collective-permute-done | bytes 393248 | tf_op jit(solution)/shard_map/ppermute | solution.py:165
  45.4 0.0 collective-permute-done.7.refs_2_
  45.4 3.9 %collective-permute-done.9.refs_4_ = bf16[12,128,128]{2,1,0:T(8,128)(2,1)S(1)} collective-permute-done((bf16[12,128,128]{2,1,0:T(8,128)(2,1)S(1)}, bf16[12,128,128]{2,1,0:T(8,128)(2,1)S(1)}, u32[]{:S(2)}, u32[]{:S(2)}) %collective-permute-start.9) | collective-permute-done | bytes 393248 | tf_op jit(solution)/shard_map/ppermute | solution.py:165
  49.3 1.0 %added.5 = bf16[12,128,128]{2,1,0:T(8,128)(2,1)} custom-call(f32[12,128,128]{2,1,0:T(8,128)S(1)} %coarse_chunk.7.refs_0_, bf16[12,128,128]{2,1,0:T(8,128)(2,1)S(1)} %collective-permute-done.6.refs_1_, bf16[12,128,128]{2,1,0:T(8,128)(2,1)S(1)} %collective-permute-done.7.refs_2_, bf16[12,128,128]{2,1,0:T(8,128)(2,1)S(1)} %collective-permute-done.8.refs_3_, ...), custom_call_target="tpu_custom_call" | custom-call | tf_op jit(solution)/shard_map/added/pallas_call | solution.py:145
  (1 shorter events, 0.0 us)
Async XLA Ops:
  0.0 11.2 %collective-permute-start.2 = (bf16[4,128,128]{2,1,0:T(8,128)(2,1)}, bf16[4,128,128]{2,1,0:T(8,128)(2,1)S(1)}, u32[]{:S(2)}, u32[]{:S(2)}) collective-permute-start(bf16[4,128,128]{2,1,0:T(8,128)(2,1)} %p.1), channel_id=1, source_target_pairs={{0,1},{1,0},{2,3},{3,2},{4,5},{5,4},{6,7},{7,6},{8,9},{9,8},{10,11... | collective-permute-start | bytes 393224 | tf_op jit(solution)/shard_map/ppermute | solution.py:165
  3.0 10.0 %collective-permute-start.4 = (bf16[4,128,128]{2,1,0:T(8,128)(2,1)}, bf16[4,128,128]{2,1,0:T(8,128)(2,1)S(1)}, u32[]{:S(2)}, u32[]{:S(2)}) collective-permute-start(bf16[4,128,128]{2,1,0:T(8,128)(2,1)} %p.1), channel_id=1, source_target_pairs={{0,3},{1,2},{2,1},{3,0},{4,7},{5,6},{6,5},{7,4},{8,11},{9,10},{10,... | collective-permute-start | bytes 393224 | tf_op jit(solution)/shard_map/ppermute | solution.py:165
  5.5 12.0 %collective-permute-start.3 = (bf16[4,128,128]{2,1,0:T(8,128)(2,1)}, bf16[4,128,128]{2,1,0:T(8,128)(2,1)S(1)}, u32[]{:S(2)}, u32[]{:S(2)}) collective-permute-start(bf16[4,128,128]{2,1,0:T(8,128)(2,1)} %p.1), channel_id=1, source_target_pairs={{0,2},{1,3},{2,0},{3,1},{4,6},{5,7},{6,4},{7,5},{8,10},{9,11},{10,... | collective-permute-start | bytes 393224 | tf_op jit(solution)/shard_map/ppermute | solution.py:165
  9.9 7.6 %collective-permute-start.1 = (bf16[4,128,128]{2,1,0:T(8,128)(2,1)S(1)}, bf16[4,128,128]{2,1,0:T(8,128)(2,1)S(1)}, u32[]{:S(2)}, u32[]{:S(2)}) collective-permute-start(bf16[4,128,128]{2,1,0:T(8,128)(2,1)S(1)} %get-tuple-element.14.own.rest_0_), channel_id=1, source_target_pairs={{4,0},{8,4},{12,8},{16,12},{20,16},{24,20},{28,24},{0,28},{5,1},{9... | collective-permute-start | bytes 393224 | tf_op jit(solution)/shard_map/ppermute | solution.py:157
  11.2 6.3 %collective-permute-start = (bf16[4,128,128]{2,1,0:T(8,128)(2,1)S(1)}, bf16[4,128,128]{2,1,0:T(8,128)(2,1)S(1)}, u32[]{:S(2)}, u32[]{:S(2)}) collective-permute-start(bf16[4,128,128]{2,1,0:T(8,128)(2,1)S(1)} %get-tuple-element.14.own.rest_0_), channel_id=1, source_target_pairs={{28,0},{0,4},{4,8},{8,12},{12,16},{16,20},{20,24},{24,28},{29,1},{... | collective-permute-start | bytes 393224 | tf_op jit(solution)/shard_map/ppermute | solution.py:157
  19.4 12.1 %collective-permute-start.5 = (bf16[12,128,128]{2,1,0:T(8,128)(2,1)S(1)}, bf16[12,128,128]{2,1,0:T(8,128)(2,1)S(1)}, u32[]{:S(2)}, u32[]{:S(2)}) collective-permute-start(bf16[12,128,128]{2,1,0:T(8,128)(2,1)S(1)} %coarse_chunk.4.rest_4_.refs_0_), channel_id=1, source_target_pairs={{0,1},{3,2},{4,5},{7,6},{8,9},{11,10},{12,13},{15,14},{16,17},{19,... | collective-permute-start | bytes 1179656 | tf_op jit(solution)/shard_map/ppermute | solution.py:165
  21.9 13.2 %collective-permute-start.6 = (bf16[12,128,128]{2,1,0:T(8,128)(2,1)S(1)}, bf16[12,128,128]{2,1,0:T(8,128)(2,1)S(1)}, u32[]{:S(2)}, u32[]{:S(2)}) collective-permute-start(bf16[12,128,128]{2,1,0:T(8,128)(2,1)S(1)} %added.4), channel_id=1, source_target_pairs={{1,2},{2,1},{5,6},{6,5},{9,10},{10,9},{13,14},{14,13},{17,18},{18,... | collective-permute-start | bytes 1179656 | tf_op jit(solution)/shard_map/ppermute | solution.py:165
  25.3 20.1 %collective-permute-start.7 = (bf16[12,128,128]{2,1,0:T(8,128)(2,1)S(1)}, bf16[12,128,128]{2,1,0:T(8,128)(2,1)S(1)}, u32[]{:S(2)}, u32[]{:S(2)}) collective-permute-start(bf16[12,128,128]{2,1,0:T(8,128)(2,1)S(1)} %get-tuple-element.16.rest_4_), channel_id=1, source_target_pairs={{0,2},{3,1},{4,6},{7,5},{8,10},{11,9},{12,14},{15,13},{16,18},{19,... | collective-permute-start | bytes 1179656 | tf_op jit(solution)/shard_map/ppermute | solution.py:165
  31.4 14.0 %collective-permute-start.8 = (bf16[12,128,128]{2,1,0:T(8,128)(2,1)S(1)}, bf16[12,128,128]{2,1,0:T(8,128)(2,1)S(1)}, u32[]{:S(2)}, u32[]{:S(2)}) collective-permute-start(bf16[12,128,128]{2,1,0:T(8,128)(2,1)S(1)} %coarse_chunk.6.refs_2_), channel_id=1, source_target_pairs={{0,1},{1,0},{2,3},{3,2},{4,5},{5,4},{6,7},{7,6},{8,9},{9,8},{10,11... | collective-permute-start | bytes 1179656 | tf_op jit(solution)/shard_map/ppermute | solution.py:165
  31.6 17.7 %collective-permute-start.9 = (bf16[12,128,128]{2,1,0:T(8,128)(2,1)S(1)}, bf16[12,128,128]{2,1,0:T(8,128)(2,1)S(1)}, u32[]{:S(2)}, u32[]{:S(2)}) collective-permute-start(bf16[12,128,128]{2,1,0:T(8,128)(2,1)S(1)} %added.3.rest_4_), channel_id=1, source_target_pairs={{1,3},{2,0},{5,7},{6,4},{9,11},{10,8},{13,15},{14,12},{17,19},{18,... | collective-permute-start | bytes 1179656 | tf_op jit(solution)/shard_map/ppermute | solution.py:165

commit v3 on v2

--- a/solution.py
+++ b/solution.py
@@ -7,7 +7,8 @@
 from jax.experimental.pallas import tpu as pltpu
 from jax.sharding import PartitionSpec as P
 
-UNROLLS = (16, 4)
+UNROLLS = (32, 16, 8, 4)
+PARTS = ("twice", "once", "thrice", "below", "own", "above")
 LIMIT = 12 * 1024 * 1024
 VMEM = pl.BlockSpec(memory_space=pltpu.VMEM)
 SMEM = pl.BlockSpec(memory_space=pltpu.SMEM)
@@ -26,7 +27,12 @@
 
 def plan_kernel(held, n, me, a_row, a_col, a_count, a, p, items, counts, a_out, p_out, sems):
     slots = a_row.shape[0]
-    copies = [pltpu.make_async_copy(p, p_out, sems.at[0]), pltpu.make_async_copy(a, a_out, sems.at[1])]
+    parts = sems.shape[0] - 1
+    size = slots // parts
+    copies = [pltpu.make_async_copy(p, p_out, sems.at[parts])]
+    for i in range(parts):
+        part = pl.ds(i * size, size)
+        copies.append(pltpu.make_async_copy(a.at[part], a_out.at[part], sems.at[i]))
     for copy in copies:
         copy.start()
     field = 32 // n
@@ -62,29 +68,34 @@
         ),
         in_specs=[SMEM] * 4 + [HBM] * 2,
         out_specs=(SMEM, SMEM, VMEM, VMEM),
-        scratch_shapes=[pltpu.SemaphoreType.DMA((2,))],
+        scratch_shapes=[pltpu.SemaphoreType.DMA((5 if a_row.shape[0] % 4 == 0 else 2,))],
         compiler_params=pltpu.CompilerParams(vmem_limit_bytes=LIMIT),
         name="plan",
     )(me, a_row, a_col, a_count, a_tiles, p_tiles)
 
 
-def chunk_kernel(held, flip, n_left, n_out, items, counts, a, below, own, above, *rest):
-    lefts, outs, (right, left, accum) = rest[:n_left], rest[-3 - n_out : -3], rest[-3:]
+def chunk_kernel(held, flip, n_block, n_out, items, counts, a, *rest):
+    blocks, outs, (right, left, accum) = rest[:n_block], rest[-3 - n_out : -3], rest[-3:]
     slots, chunk = a.shape[0], outs[0].shape[0]
     me = counts[counts.shape[0] - 1]
     d = 0 if flip is None else me ^ flip
     base, count = d * slots, counts[d]
-    for i, ref in enumerate((below, own, above)):
+    if flip is None:
+        rights, rows = blocks[:3], blocks[3]
+        for i in range(left.shape[0]):
+            left[i] = rows[i].T
+    else:
+        part = dict(zip(PARTS, blocks))
+        rights = part["below"], part["own"], part["above"]
+        left[0] = part["own"][d].T
+        left[1] = part["once"][d].T
+        left[2] = part["twice"][d].T
+        left[3] = part["thrice"][d].T
+    for i, ref in enumerate(rights):
         right[i * held : (i + 1) * held] = ref[...]
-    if flip is None:
-        for i in range(left.shape[0]):
-            left[i] = lefts[0][i].T
-    else:
-        for i in range(n_left):
-            left[i] = lefts[i][d].T
     accum[...] = jnp.zeros_like(accum)
 
-    def take(e):
+    def unpack(e):
         item = items[base + jnp.minimum(e, count - 1)]
         t, item = item & ((1 << bits(slots)) - 1), item >> bits(slots)
         col, row = item & ((1 << bits(3 * held)) - 1), item >> bits(3 * held)
@@ -92,35 +103,37 @@
             s = divide(row, held)[1] * (3 * held) + col
         else:
             row, s = divide(row, held)[0] ^ me, col
-        s = jnp.where(e < count, s, chunk)
-        image = jnp.dot(a[t], right[col], preferred_element_type=jnp.float32)
-        accum[s] += jnp.dot(left[row], image.astype(jnp.bfloat16), preferred_element_type=jnp.float32)
+        return t, col, row, jnp.where(e < count, s, chunk)
 
     done = jnp.int32(0)
-    for unroll in UNROLLS:
+    for unroll, smaller in zip(UNROLLS, (*UNROLLS[1:], 0)):
 
         def advance(step, carry, done=done, unroll=unroll):
-            for u in range(unroll):
-                take(done + step * unroll + u)
+            work = [unpack(done + step * unroll + u) for u in range(unroll)]
+            f32 = jnp.float32
+            images = [jnp.dot(a[t], right[col], preferred_element_type=f32) for t, col, _, _ in work]
+            images = [image.astype(jnp.bfloat16) for image in images]
+            terms = [jnp.dot(left[w[2]], x, preferred_element_type=f32) for w, x in zip(work, images)]
+            for w, term in zip(work, terms):
+                accum[w[3]] += term
             return carry
 
-        spare = unroll - 1 if unroll == UNROLLS[-1] else 0
-        steps = lax.div(count - done + spare, unroll)
+        steps = lax.div(jnp.maximum(count - done, 0) + unroll - smaller - 1, unroll)
         lax.fori_loop(0, steps, advance, 0)
         done = done + steps * unroll
     for out in outs:
         out[...] = accum[:chunk].astype(out.dtype)
 
 
-def coarse_chunk(flip, listed, rights, lefts, dtypes, after=()):
+def coarse_chunk(flip, listed, blocks, dtypes, after=()):
     items, counts, a = listed
-    held, width = rights[0].shape[0], a.shape[1]
+    held, width = blocks[0].shape[0], a.shape[1]
     chunk = 3 * held * (held if flip is None else 1)
-    n_left = lefts[0].shape[0] if flip is None else len(lefts)
+    n_left = blocks[-1].shape[0] if flip is None else 4
     return pl.pallas_call(
-        functools.partial(chunk_kernel, held, flip, len(lefts), len(dtypes)),
+        functools.partial(chunk_kernel, held, flip, len(blocks), len(dtypes)),
         out_shape=[jax.ShapeDtypeStruct((chunk, width, width), dtype) for dtype in dtypes],
-        in_specs=[SMEM] * 2 + [VMEM] * (4 + len(lefts)) + [pl.BlockSpec(memory_space=pl.ANY)] * len(after),
+        in_specs=[SMEM] * 2 + [VMEM] * (1 + len(blocks)) + [pl.BlockSpec(memory_space=pl.ANY)] * len(after),
         out_specs=[VMEM] * len(dtypes),
         scratch_shapes=[
             pltpu.VMEM((3 * held, width, width), jnp.bfloat16),
@@ -130,7 +143,7 @@
         compiler_params=pltpu.CompilerParams(vmem_limit_bytes=LIMIT),
         cost_estimate=pl.CostEstimate(flops=1 << 31, bytes_accessed=1 << 20, transcendentals=0),
         name="coarse_chunk",
-    )(items, counts, a, *rights, *lefts, *after)
+    )(items, counts, a, *blocks, *after)
 
 
 def add_kernel(n, *refs):
@@ -164,25 +177,27 @@
     a_tiles, a_row, a_col, p_tiles = stay(a_tiles), stay(a_row), stay(a_col), stay(p_tiles)
     cross = lambda block, pairs: lax.ppermute(block, "col", pairs)
     flips = [[(i, i ^ m) for i in range(4)] for m in range(4)]
-    far = {m: cross(p_tiles, flips[m]) for m in (2, 3, 1)}
+    once, twice, thrice = (cross(p_tiles, flips[m]) for m in (1, 2, 3))
     items, counts, a, own = plan(held, 4, me, a_row, a_col, a_count, a_tiles, p_tiles)
-    below, above = shifted(own, "row", 1), shifted(own, "row", -1)
-    keep = lambda x: pltpu.with_memory_space_constraint(x, pltpu.VMEM)
-    listed = (items, counts, a)
-    rights, lefts = [keep(below), own, keep(above)], [own] + [keep(far[m]) for m in (1, 2, 3)]
+    below, above = shifted(p_tiles, "row", 1), shifted(p_tiles, "row", -1)
+    part = dict(once=once, twice=twice, thrice=thrice, below=below, above=above)
+    part = {name: pltpu.with_memory_space_constraint(x, pltpu.VMEM) for name, x in part.items()}
+    part["own"] = own
+    listed, blocks = (items, counts, a), [part[name] for name in PARTS]
 
     bf16, f32 = jnp.bfloat16, jnp.float32
-    (first,) = coarse_chunk(3, listed, rights, lefts, [bf16])
+    (first,) = coarse_chunk(3, listed, blocks, [bf16])
     got1 = cross(first, [(0, 1), (3, 2)])
     got3 = cross(added([first], bf16), [(1, 2), (2, 1)])
-    second, wide = coarse_chunk(2, listed, rights, lefts, [bf16, f32], [first])
+    second, wide = coarse_chunk(2, listed, blocks, [bf16, f32], [first])
     got5 = cross(second, [(0, 2), (3, 1)])
-    (third,) = coarse_chunk(1, listed, rights, lefts, [bf16], [second])
+    (third,) = coarse_chunk(1, listed, blocks, [bf16], [second])
     got2 = cross(third, flips[1])
     joined = added([wide, got1], bf16, [third])
     got4 = cross(joined, [(1, 3), (2, 0)])
-    (last,) = coarse_chunk(0, listed, rights, lefts, [f32], [joined])
-    return added([last, got3, got5, got2, got4], bf16)
+    (last,) = coarse_chunk(0, listed, blocks, [f32], [joined])
+    most = added([last, got3, got5, got2], f32)
+    return added([most, got4], bf16)
 
 
 def any_columns(a_tiles, a_row, a_col, a_count, p_tiles):
@@ -193,8 +208,8 @@
     row_side = lax.all_gather(p_tiles, "col", axis=0, tiled=True)
     me = jnp.zeros((1,), jnp.int32)
     items, counts, a, own = plan(held, 1, me, a_row, a_col, a_count, a_tiles, p_tiles)
-    rights = (rights[0], own, rights[2])
-    (sums,) = coarse_chunk(None, (items, counts, a), rights, [row_side], [jnp.bfloat16])
+    blocks = (rights[0], own, rights[2], row_side)
+    (sums,) = coarse_chunk(None, (items, counts, a), blocks, [jnp.bfloat16])
     parts = sums.reshape(n, total // n, *sums.shape[1:])
     parts = lax.all_to_all(parts, "col", 0, 0, tiled=True)
     return jnp.sum(parts.astype(jnp.float32), axis=0).astype(jnp.bfloat16)

time: 50.7 us -> 47.8 us (0.943)
  Pallas kernels: 14 us -> 11.4 us
  starting transfers between devices: 15.1 us -> 13.7 us
  waiting for transfers between devices: 20.5 us -> 21.6 us
    pallas_call x4, Pallas kernels: 9.34 us -> 6.75 us  [coarse_chunk(): pl.pallas_call(functools.partial(chunk_kernel, held, flip, len(blocks), l...]
    ppermute x8, starting transfers between devices: 13.7 us -> 12.4 us  [line_of_four(): cross = lambda block, pairs: lax.ppermute(block, 'col', pairs)]
    ppermute x8, waiting for transfers between devices: 20.5 us -> 21.6 us  [line_of_four(): cross = lambda block, pairs: lax.ppermute(block, 'col', pairs)]
    pallas_call x3 -> x4, Pallas kernels: 1.06 us -> 1.09 us  [added(): pl.pallas_call(functools.partial(add_kernel, len(xs)), out_shape=jax.Shap...]
  transfers between devices with their start and end apart: 10 -> 10, of which waited for: 4 -> 5; matrix products, arithmetic and copies ran while one was open for 0% -> 0% of each run, Pallas kernels for 22% -> 18%
where the time goes in v3:
time: 47.8 us; the launch traced here: 47.5 us
  waiting for transfers between devices  21.6 us (45%)
  starting transfers between devices  13.7 us (29%)
  Pallas kernels  11.4 us (24%)
  between operations  0.77 us (2%)
    ppermute x8, waiting for transfers between devices, line_of_four(): cross = lambda block, pairs: lax.ppermute(block, 'col', pairs)  21.6 us
    ppermute x8, starting transfers between devices, line_of_four(): cross = lambda block, pairs: lax.ppermute(block, 'col', pairs)  12.4 us
    pallas_call x4, Pallas kernels, coarse_chunk(): pl.pallas_call(functools.partial(chunk_kernel, held, flip, len(blocks), l...  6.75 us
    pallas_call x1, Pallas kernels, plan(): pl.pallas_call(functools.partial(plan_kernel, held, n), out_shape=(jax.Sh...  3.59 us
    ppermute x2, starting transfers between devices, shifted(): lax.ppermute(block, axis, [((i - distance) % n, i) for i in range(n)])  1.33 us
    pallas_call x4, Pallas kernels, added(): pl.pallas_call(functools.partial(add_kernel, len(xs)), out_shape=jax.Shap...  1.09 us
  transfers between devices with their start and end apart: 10, of which 5 were waited for; matrix products, arithmetic and copies ran while one was open for 0% of the time, Pallas kernels for 18%

profile of v3, /device:TPU:0, one launch (start us, length us, event | category | flops | bytes accessed | tf_op | source)
XLA Modules:
  0.0 47.5 jit_solution(3742363385847225391)
XLA Ops:
  0.0 5.0 %collective-permute-start.2 = (bf16[4,128,128]{2,1,0:T(8,128)(2,1)}, bf16[4,128,128]{2,1,0:T(8,128)(2,1)S(1)}, u32[]{:S(2)}, u32[]{:S(2)}) collective-permute-start(bf16[4,128,128]{2,1,0:T(8,128)(2,1)} %p.1), channel_id=1, source_target_pairs={{0,3},{1,2},{2,1},{3,0},{4,7},{5,6},{6,5},{7,4},{8,11},{9,10},{10,... | collective-permute-start | bytes 393224 | tf_op jit(solution)/shard_map/ppermute | solution.py:178
  5.0 0.0 collective-permute-start.1
  5.1 0.6 %collective-permute-start = (bf16[4,128,128]{2,1,0:T(8,128)(2,1)}, bf16[4,128,128]{2,1,0:T(8,128)(2,1)S(1)}, u32[]{:S(2)}, u32[]{:S(2)}) collective-permute-start(bf16[4,128,128]{2,1,0:T(8,128)(2,1)} %p.1), channel_id=1, source_target_pairs={{0,2},{1,3},{2,0},{3,1},{4,6},{5,7},{6,4},{7,5},{8,10},{9,11},{10,... | collective-permute-start | bytes 393224 | tf_op jit(solution)/shard_map/ppermute | solution.py:178
  5.6 1.3 %collective-permute-start.4 = (bf16[4,128,128]{2,1,0:T(8,128)(2,1)}, bf16[4,128,128]{2,1,0:T(8,128)(2,1)S(1)}, u32[]{:S(2)}, u32[]{:S(2)}) collective-permute-start(bf16[4,128,128]{2,1,0:T(8,128)(2,1)} %p.1), channel_id=1, source_target_pairs={{4,0},{8,4},{12,8},{16,12},{20,16},{24,20},{28,24},{0,28},{5,1},{9... | collective-permute-start | bytes 393224 | tf_op jit(solution)/shard_map/ppermute | solution.py:170
  6.9 0.0 collective-permute-start.3
  7.6 3.6 %plan.1 = (s32[512]{0:T(512)S(1)}, s32[5]{0:T(128)S(1)}, bf16[128,128,128]{2,1,0:T(8,128)(2,1)S(1)}, bf16[4,128,128]{2,1,0:T(8,128)(2,1)S(1)}) custom-call(s32[1]{0:T(128)} %bitcast.me, s32[128]{0:T(128)} %a_row.1, s32[128]{0:T(128)} %a_col.1, s32[1]{0:T(128)S(6)} %copy.6.a_count, bf16[128,128,128]{2,1,0:T(8,128)(2,1)} %a.1, bf16[4,128,128]{2,1,0:T(8,128)(2,1)} %p.1), custom_call_target="tpu_custom_call" | custom-call | tf_op jit(solution)/shard_map/plan/pallas_call | solution.py:61
  11.2 0.0 collective-permute-done.2.rest_2_
  11.2 1.4 %collective-permute-done.1.rest_1_ = bf16[4,128,128]{2,1,0:T(8,128)(2,1)S(1)} collective-permute-done((bf16[4,128,128]{2,1,0:T(8,128)(2,1)}, bf16[4,128,128]{2,1,0:T(8,128)(2,1)S(1)}, u32[]{:S(2)}, u32[]{:S(2)}) %collective-permute-start.1) | collective-permute-done | bytes 131104 | tf_op jit(solution)/shard_map/ppermute | solution.py:178
  12.7 3.7 %collective-permute-done.rest_0_ = bf16[4,128,128]{2,1,0:T(8,128)(2,1)S(1)} collective-permute-done((bf16[4,128,128]{2,1,0:T(8,128)(2,1)}, bf16[4,128,128]{2,1,0:T(8,128)(2,1)S(1)}, u32[]{:S(2)}, u32[]{:S(2)}) %collective-permute-start) | collective-permute-done | bytes 131104 | tf_op jit(solution)/shard_map/ppermute | solution.py:178
  16.3 0.0 collective-permute-done.4.rest_5_
  16.3 0.0 collective-permute-done.3.rest_3_
  16.3 1.8 %coarse_chunk.4.rest_6_.refs_0_ = bf16[12,128,128]{2,1,0:T(8,128)(2,1)S(1)} custom-call(s32[512]{0:T(512)S(1)} %get-tuple-element.11.items, s32[5]{0:T(128)S(1)} %get-tuple-element.12.counts, bf16[128,128,128]{2,1,0:T(8,128)(2,1)S(1)} %get-tuple-element.13.a, bf16[4,128,128]{2,1,0:T(8,128)(2,1)S(1)} %collective-permute-done.rest_0_, ...), custom_call_target="tpu_custom_call" | custom-call | flops 2147483648 | bytes 1048576 | tf_op jit(solution)/shard_map/coarse_chunk/pallas_call | solution.py:133
  18.2 1.3 %collective-permute-start.5 = (bf16[12,128,128]{2,1,0:T(8,128)(2,1)S(1)}, bf16[12,128,128]{2,1,0:T(8,128)(2,1)S(1)}, u32[]{:S(2)}, u32[]{:S(2)}) collective-permute-start(bf16[12,128,128]{2,1,0:T(8,128)(2,1)S(1)} %coarse_chunk.4.rest_6_.refs_0_), channel_id=1, source_target_pairs={{0,1},{3,2},{4,5},{7,6},{8,9},{11,10},{12,13},{15,14},{16,17},{19,... | collective-permute-start | bytes 1179656 | tf_op jit(solution)/shard_map/ppermute | solution.py:178
  19.5 0.7 %collective-permute-start.6 = (bf16[12,128,128]{2,1,0:T(8,128)(2,1)S(1)}, bf16[12,128,128]{2,1,0:T(8,128)(2,1)S(1)}, u32[]{:S(2)}, u32[]{:S(2)}) collective-permute-start(bf16[12,128,128]{2,1,0:T(8,128)(2,1)S(1)} %added.5), channel_id=1, source_target_pairs={{1,2},{2,1},{5,6},{6,5},{9,10},{10,9},{13,14},{14,13},{17,18},{18,... | collective-permute-start | bytes 1179656 | tf_op jit(solution)/shard_map/ppermute | solution.py:178
  20.2 1.5 %coarse_chunk.5 = (bf16[12,128,128]{2,1,0:T(8,128)(2,1)S(1)}, f32[12,128,128]{2,1,0:T(8,128)S(1)}) custom-call(s32[512]{0:T(512)S(1)} %get-tuple-element.11.items, s32[5]{0:T(128)S(1)} %get-tuple-element.12.counts, bf16[128,128,128]{2,1,0:T(8,128)(2,1)S(1)} %get-tuple-element.13.a, bf16[4,128,128]{2,1,0:T(8,128)(2,1)S(1)} %collective-permute-done.rest_0_, ...), custom_call_target="tpu_custom_call" | custom-call | flops 2147483648 | bytes 1048576 | tf_op jit(solution)/shard_map/coarse_chunk/pallas_call | solution.py:133
  21.8 3.4 %collective-permute-start.7 = (bf16[12,128,128]{2,1,0:T(8,128)(2,1)S(1)}, bf16[12,128,128]{2,1,0:T(8,128)(2,1)S(1)}, u32[]{:S(2)}, u32[]{:S(2)}) collective-permute-start(bf16[12,128,128]{2,1,0:T(8,128)(2,1)S(1)} %get-tuple-element.16.rest_6_), channel_id=1, source_target_pairs={{0,2},{3,1},{4,6},{7,5},{8,10},{11,9},{12,14},{15,13},{16,18},{19,... | collective-permute-start | bytes 1179656 | tf_op jit(solution)/shard_map/ppermute | solution.py:178
  25.2 1.8 %coarse_chunk.6.refs_2_ = bf16[12,128,128]{2,1,0:T(8,128)(2,1)S(1)} custom-call(s32[512]{0:T(512)S(1)} %get-tuple-element.11.items, s32[5]{0:T(128)S(1)} %get-tuple-element.12.counts, bf16[128,128,128]{2,1,0:T(8,128)(2,1)S(1)} %get-tuple-element.13.a, bf16[4,128,128]{2,1,0:T(8,128)(2,1)S(1)} %collective-permute-done.rest_0_, ...), custom_call_target="tpu_custom_call" | custom-call | flops 2147483648 | bytes 1048576 | tf_op jit(solution)/shard_map/coarse_chunk/pallas_call | solution.py:133
  27.1 0.1 collective-permute-start.8
  27.2 1.9 %collective-permute-done.5.refs_1_ = bf16[12,128,128]{2,1,0:T(8,128)(2,1)S(1)} collective-permute-done((bf16[12,128,128]{2,1,0:T(8,128)(2,1)S(1)}, bf16[12,128,128]{2,1,0:T(8,128)(2,1)S(1)}, u32[]{:S(2)}, u32[]{:S(2)}) %collective-permute-start.5) | collective-permute-done | bytes 393248 | tf_op jit(solution)/shard_map/ppermute | solution.py:178
  29.1 0.1 added.4.rest_6_
  29.1 1.3 %collective-permute-start.9 = (bf16[12,128,128]{2,1,0:T(8,128)(2,1)S(1)}, bf16[12,128,128]{2,1,0:T(8,128)(2,1)S(1)}, u32[]{:S(2)}, u32[]{:S(2)}) collective-permute-start(bf16[12,128,128]{2,1,0:T(8,128)(2,1)S(1)} %added.4.rest_6_), channel_id=1, source_target_pairs={{1,3},{2,0},{5,7},{6,4},{9,11},{10,8},{13,15},{14,12},{17,19},{18,... | collective-permute-start | bytes 1179656 | tf_op jit(solution)/shard_map/ppermute | solution.py:178
  30.4 1.5 %coarse_chunk.7.refs_0_ = f32[12,128,128]{2,1,0:T(8,128)S(1)} custom-call(s32[512]{0:T(512)S(1)} %get-tuple-element.11.items, s32[5]{0:T(128)S(1)} %get-tuple-element.12.counts, bf16[128,128,128]{2,1,0:T(8,128)(2,1)S(1)} %get-tuple-element.13.a, bf16[4,128,128]{2,1,0:T(8,128)(2,1)S(1)} %collective-permute-done.rest_0_, ...), custom_call_target="tpu_custom_call" | custom-call | flops 2147483648 | bytes 1048576 | tf_op jit(solution)/shard_map/coarse_chunk/pallas_call | solution.py:133
  32.0 0.0 collective-permute-done.6.refs_1_
  32.0 11.8 %collective-permute-done.8.refs_3_ = bf16[12,128,128]{2,1,0:T(8,128)(2,1)S(1)} collective-permute-done((bf16[12,128,128]{2,1,0:T(8,128)(2,1)S(1)}, bf16[12,128,128]{2,1,0:T(8,128)(2,1)S(1)}, u32[]{:S(2)}, u32[]{:S(2)}) %collective-permute-start.8) | collective-permute-done | bytes 393248 | tf_op jit(solution)/shard_map/ppermute | solution.py:178
  43.7 0.0 collective-permute-done.7.refs_2_
  43.7 0.2 added.6.refs_0_
  43.9 2.8 %collective-permute-done.9.refs_1_ = bf16[12,128,128]{2,1,0:T(8,128)(2,1)S(1)} collective-permute-done((bf16[12,128,128]{2,1,0:T(8,128)(2,1)S(1)}, bf16[12,128,128]{2,1,0:T(8,128)(2,1)S(1)}, u32[]{:S(2)}, u32[]{:S(2)}) %collective-permute-start.9) | collective-permute-done | bytes 393248 | tf_op jit(solution)/shard_map/ppermute | solution.py:178
  46.7 0.8 %added.7 = bf16[12,128,128]{2,1,0:T(8,128)(2,1)} custom-call(f32[12,128,128]{2,1,0:T(8,128)S(1)} %added.6.refs_0_, bf16[12,128,128]{2,1,0:T(8,128)(2,1)S(1)} %collective-permute-done.9.refs_1_), custom_call_target="tpu_custom_call" | custom-call | tf_op jit(solution)/shard_map/added/pallas_call | solution.py:158
  (1 shorter events, 0.0 us)
Async XLA Ops:
  0.0 11.2 %collective-permute-start.2 = (bf16[4,128,128]{2,1,0:T(8,128)(2,1)}, bf16[4,128,128]{2,1,0:T(8,128)(2,1)S(1)}, u32[]{:S(2)}, u32[]{:S(2)}) collective-permute-start(bf16[4,128,128]{2,1,0:T(8,128)(2,1)} %p.1), channel_id=1, source_target_pairs={{0,3},{1,2},{2,1},{3,0},{4,7},{5,6},{6,5},{7,4},{8,11},{9,10},{10,... | collective-permute-start | bytes 393224 | tf_op jit(solution)/shard_map/ppermute | solution.py:178
  5.0 7.6 %collective-permute-start.1 = (bf16[4,128,128]{2,1,0:T(8,128)(2,1)}, bf16[4,128,128]{2,1,0:T(8,128)(2,1)S(1)}, u32[]{:S(2)}, u32[]{:S(2)}) collective-permute-start(bf16[4,128,128]{2,1,0:T(8,128)(2,1)} %p.1), channel_id=1, source_target_pairs={{0,1},{1,0},{2,3},{3,2},{4,5},{5,4},{6,7},{7,6},{8,9},{9,8},{10,11... | collective-permute-start | bytes 393224 | tf_op jit(solution)/shard_map/ppermute | solution.py:178
  5.1 11.3 %collective-permute-start = (bf16[4,128,128]{2,1,0:T(8,128)(2,1)}, bf16[4,128,128]{2,1,0:T(8,128)(2,1)S(1)}, u32[]{:S(2)}, u32[]{:S(2)}) collective-permute-start(bf16[4,128,128]{2,1,0:T(8,128)(2,1)} %p.1), channel_id=1, source_target_pairs={{0,2},{1,3},{2,0},{3,1},{4,6},{5,7},{6,4},{7,5},{8,10},{9,11},{10,... | collective-permute-start | bytes 393224 | tf_op jit(solution)/shard_map/ppermute | solution.py:178
  5.6 10.7 %collective-permute-start.4 = (bf16[4,128,128]{2,1,0:T(8,128)(2,1)}, bf16[4,128,128]{2,1,0:T(8,128)(2,1)S(1)}, u32[]{:S(2)}, u32[]{:S(2)}) collective-permute-start(bf16[4,128,128]{2,1,0:T(8,128)(2,1)} %p.1), channel_id=1, source_target_pairs={{4,0},{8,4},{12,8},{16,12},{20,16},{24,20},{28,24},{0,28},{5,1},{9... | collective-permute-start | bytes 393224 | tf_op jit(solution)/shard_map/ppermute | solution.py:170
  6.9 9.4 %collective-permute-start.3 = (bf16[4,128,128]{2,1,0:T(8,128)(2,1)}, bf16[4,128,128]{2,1,0:T(8,128)(2,1)S(1)}, u32[]{:S(2)}, u32[]{:S(2)}) collective-permute-start(bf16[4,128,128]{2,1,0:T(8,128)(2,1)} %p.1), channel_id=1, source_target_pairs={{28,0},{0,4},{4,8},{8,12},{12,16},{16,20},{20,24},{24,28},{29,1},{... | collective-permute-start | bytes 393224 | tf_op jit(solution)/shard_map/ppermute | solution.py:170
  18.2 10.8 %collective-permute-start.5 = (bf16[12,128,128]{2,1,0:T(8,128)(2,1)S(1)}, bf16[12,128,128]{2,1,0:T(8,128)(2,1)S(1)}, u32[]{:S(2)}, u32[]{:S(2)}) collective-permute-start(bf16[12,128,128]{2,1,0:T(8,128)(2,1)S(1)} %coarse_chunk.4.rest_6_.refs_0_), channel_id=1, source_target_pairs={{0,1},{3,2},{4,5},{7,6},{8,9},{11,10},{12,13},{15,14},{16,17},{19,... | collective-permute-start | bytes 1179656 | tf_op jit(solution)/shard_map/ppermute | solution.py:178
  19.5 12.4 %collective-permute-start.6 = (bf16[12,128,128]{2,1,0:T(8,128)(2,1)S(1)}, bf16[12,128,128]{2,1,0:T(8,128)(2,1)S(1)}, u32[]{:S(2)}, u32[]{:S(2)}) collective-permute-start(bf16[12,128,128]{2,1,0:T(8,128)(2,1)S(1)} %added.5), channel_id=1, source_target_pairs={{1,2},{2,1},{5,6},{6,5},{9,10},{10,9},{13,14},{14,13},{17,18},{18,... | collective-permute-start | bytes 1179656 | tf_op jit(solution)/shard_map/ppermute | solution.py:178
  21.8 22.0 %collective-permute-start.7 = (bf16[12,128,128]{2,1,0:T(8,128)(2,1)S(1)}, bf16[12,128,128]{2,1,0:T(8,128)(2,1)S(1)}, u32[]{:S(2)}, u32[]{:S(2)}) collective-permute-start(bf16[12,128,128]{2,1,0:T(8,128)(2,1)S(1)} %get-tuple-element.16.rest_6_), channel_id=1, source_target_pairs={{0,2},{3,1},{4,6},{7,5},{8,10},{11,9},{12,14},{15,13},{16,18},{19,... | collective-permute-start | bytes 1179656 | tf_op jit(solution)/shard_map/ppermute | solution.py:178
  27.1 16.7 %collective-permute-start.8 = (bf16[12,128,128]{2,1,0:T(8,128)(2,1)S(1)}, bf16[12,128,128]{2,1,0:T(8,128)(2,1)S(1)}, u32[]{:S(2)}, u32[]{:S(2)}) collective-permute-start(bf16[12,128,128]{2,1,0:T(8,128)(2,1)S(1)} %coarse_chunk.6.refs_2_), channel_id=1, source_target_pairs={{0,1},{1,0},{2,3},{3,2},{4,5},{5,4},{6,7},{7,6},{8,9},{9,8},{10,11... | collective-permute-start | bytes 1179656 | tf_op jit(solution)/shard_map/ppermute | solution.py:178
  29.1 17.5 %collective-permute-start.9 = (bf16[12,128,128]{2,1,0:T(8,128)(2,1)S(1)}, bf16[12,128,128]{2,1,0:T(8,128)(2,1)S(1)}, u32[]{:S(2)}, u32[]{:S(2)}) collective-permute-start(bf16[12,128,128]{2,1,0:T(8,128)(2,1)S(1)} %added.4.rest_6_), channel_id=1, source_target_pairs={{1,3},{2,0},{5,7},{6,4},{9,11},{10,8},{13,15},{14,12},{17,19},{18,... | collective-permute-start | bytes 1179656 | tf_op jit(solution)/shard_map/ppermute | solution.py:178

commit v4 on v3

--- a/solution.py
+++ b/solution.py
@@ -61,8 +61,8 @@
     return pl.pallas_call(
         functools.partial(plan_kernel, held, n),
         out_shape=(
-            jax.ShapeDtypeStruct((n * a_row.shape[0],), jnp.int32),
-            jax.ShapeDtypeStruct((n + 1,), jnp.int32),
+            pltpu.SMEM((n * a_row.shape[0],), jnp.int32),
+            pltpu.SMEM((n + 1,), jnp.int32),
             pltpu.VMEM(a_tiles.shape, a_tiles.dtype),
             pltpu.VMEM(p_tiles.shape, p_tiles.dtype),
         ),
@@ -74,13 +74,13 @@
     )(me, a_row, a_col, a_count, a_tiles, p_tiles)
 
 
-def chunk_kernel(held, flip, n_block, n_out, items, counts, a, *rest):
-    blocks, outs, (right, left, accum) = rest[:n_block], rest[-3 - n_out : -3], rest[-3:]
-    slots, chunk = a.shape[0], outs[0].shape[0]
+def chunk_kernel(held, pick, n_block, parts, items, counts, a, *rest):
+    blocks, outs, (right, left, accum) = rest[:n_block], rest[-3 - len(parts) : -3], rest[-3:]
+    slots, chunk = a.shape[0], accum.shape[0] - 1
     me = counts[counts.shape[0] - 1]
-    d = 0 if flip is None else me ^ flip
+    d = 0 if pick is None else sum(jnp.where(me == i, x, 0) for i, x in enumerate(pick))
     base, count = d * slots, counts[d]
-    if flip is None:
+    if pick is None:
         rights, rows = blocks[:3], blocks[3]
         for i in range(left.shape[0]):
             left[i] = rows[i].T
@@ -99,7 +99,7 @@
         item = items[base + jnp.minimum(e, count - 1)]
         t, item = item & ((1 << bits(slots)) - 1), item >> bits(slots)
         col, row = item & ((1 << bits(3 * held)) - 1), item >> bits(3 * held)
-        if flip is None:
+        if pick is None:
             s = divide(row, held)[1] * (3 * held) + col
         else:
             row, s = divide(row, held)[0] ^ me, col
@@ -121,20 +121,20 @@
         steps = lax.div(jnp.maximum(count - done, 0) + unroll - smaller - 1, unroll)
         lax.fori_loop(0, steps, advance, 0)
         done = done + steps * unroll
-    for out in outs:
-        out[...] = accum[:chunk].astype(out.dtype)
-
-
-def coarse_chunk(flip, listed, blocks, dtypes, after=()):
+    for out, start in zip(outs, parts):
+        out[...] = accum[start : start + out.shape[0]].astype(out.dtype)
+
+
+def coarse_chunk(pick, listed, blocks, outs, after=()):
     items, counts, a = listed
     held, width = blocks[0].shape[0], a.shape[1]
-    chunk = 3 * held * (held if flip is None else 1)
-    n_left = blocks[-1].shape[0] if flip is None else 4
-    return pl.pallas_call(
-        functools.partial(chunk_kernel, held, flip, len(blocks), len(dtypes)),
-        out_shape=[jax.ShapeDtypeStruct((chunk, width, width), dtype) for dtype in dtypes],
+    chunk = 3 * held * (held if pick is None else 1)
+    n_left = blocks[-1].shape[0] if pick is None else 4
+    return pl.pallas_call(
+        functools.partial(chunk_kernel, held, pick, len(blocks), [start for start, _, _ in outs]),
+        out_shape=[jax.ShapeDtypeStruct((end - start, width, width), dtype) for start, end, dtype in outs],
         in_specs=[SMEM] * 2 + [VMEM] * (1 + len(blocks)) + [pl.BlockSpec(memory_space=pl.ANY)] * len(after),
-        out_specs=[VMEM] * len(dtypes),
+        out_specs=[VMEM] * len(outs),
         scratch_shapes=[
             pltpu.VMEM((3 * held, width, width), jnp.bfloat16),
             pltpu.VMEM((n_left, width, width), jnp.bfloat16),
@@ -144,6 +144,46 @@
         cost_estimate=pl.CostEstimate(flops=1 << 31, bytes_accessed=1 << 20, transcendentals=0),
         name="coarse_chunk",
     )(items, counts, a, *blocks, *after)
+
+
+def mix_kernel(counts, x, y, z, *rest):
+    out = rest[-1]
+    me = counts[counts.shape[0] - 1]
+    f32 = jnp.float32
+    total = y[...].astype(f32) + z[...].astype(f32)
+    out[...] = jnp.where((me == 0) | (me == 3), x[...].astype(f32), total).astype(out.dtype)
+
+
+def mixed(counts, x, y, z, after=()):
+    return pl.pallas_call(
+        mix_kernel,
+        out_shape=jax.ShapeDtypeStruct(x.shape, x.dtype),
+        in_specs=[SMEM] + [VMEM] * 3 + [pl.BlockSpec(memory_space=pl.ANY)] * len(after),
+        out_specs=VMEM,
+        compiler_params=pltpu.CompilerParams(vmem_limit_bytes=LIMIT),
+        name="mixed",
+    )(counts, x, y, z, *after)
+
+
+def finish_kernel(counts, most, far_a, far_b, near_a, near_b, out):
+    me = counts[counts.shape[0] - 1]
+    half = far_a.shape[0]
+    f32 = jnp.float32
+    end = (me == 0) | (me == 3)
+    for i, (far, near) in enumerate(((far_a, near_a), (far_b, near_b))):
+        part = slice(i * half, (i + 1) * half)
+        out[part] = (most[part] + jnp.where(end, far[...], near[...]).astype(f32)).astype(out.dtype)
+
+
+def finished(counts, most, *got):
+    return pl.pallas_call(
+        finish_kernel,
+        out_shape=jax.ShapeDtypeStruct(most.shape, got[0].dtype),
+        in_specs=[SMEM] + [VMEM] * 5,
+        out_specs=VMEM,
+        compiler_params=pltpu.CompilerParams(vmem_limit_bytes=LIMIT),
+        name="finished",
+    )(counts, most, *got)
 
 
 def add_kernel(n, *refs):
@@ -186,18 +226,26 @@
     listed, blocks = (items, counts, a), [part[name] for name in PARTS]
 
     bf16, f32 = jnp.bfloat16, jnp.float32
-    (first,) = coarse_chunk(3, listed, blocks, [bf16])
-    got1 = cross(first, [(0, 1), (3, 2)])
-    got3 = cross(added([first], bf16), [(1, 2), (2, 1)])
-    second, wide = coarse_chunk(2, listed, blocks, [bf16, f32], [first])
-    got5 = cross(second, [(0, 2), (3, 1)])
-    (third,) = coarse_chunk(1, listed, blocks, [bf16], [second])
-    got2 = cross(third, flips[1])
-    joined = added([wide, got1], bf16, [third])
-    got4 = cross(joined, [(1, 3), (2, 0)])
-    (last,) = coarse_chunk(0, listed, blocks, [f32], [joined])
-    most = added([last, got3, got5, got2], f32)
-    return added([most, got4], bf16)
+    chunk, half = 3 * held, 3 * held // 2
+    cut = [(0, half), (half, chunk)]
+    halves = [(*c, bf16) for c in cut] + [(*c, f32) for c in cut]
+    ends, middles, over = [(0, 1), (3, 2)], [(1, 2), (2, 1)], [(1, 3), (2, 0)]
+    *first, wide_a, wide_b = coarse_chunk((3, 3, 0, 0), listed, blocks, halves)
+    got1 = cross(first[0], ends)
+    *second, next_a, next_b = coarse_chunk((2, 2, 1, 1), listed, blocks, halves, first[:1])
+    got2 = cross(added(first[1:], bf16, second[:1]), ends)
+    sent3 = mixed(counts, second[0], wide_a, got1)
+    got3 = cross(sent3, ends + over)
+    sent4 = mixed(counts, second[1], wide_b, got2, [sent3])
+    got4 = cross(sent4, ends + over)
+    (third,) = coarse_chunk((1, 0, 3, 2), listed, blocks, [(0, chunk, bf16)], [sent4])
+    got5 = cross(third, flips[1])
+    sent6 = added([next_a, got3], bf16, [third])
+    got6 = cross(sent6, middles)
+    sent7 = added([next_b, got4], bf16, [sent6])
+    got7 = cross(sent7, middles)
+    (last,) = coarse_chunk((0, 1, 2, 3), listed, blocks, [(0, chunk, f32)], [sent7])
+    return finished(counts, added([last, got5], f32), got3, got4, got6, got7)
 
 
 def any_columns(a_tiles, a_row, a_col, a_count, p_tiles):
@@ -209,7 +257,7 @@
     me = jnp.zeros((1,), jnp.int32)
     items, counts, a, own = plan(held, 1, me, a_row, a_col, a_count, a_tiles, p_tiles)
     blocks = (rights[0], own, rights[2], row_side)
-    (sums,) = coarse_chunk(None, (items, counts, a), blocks, [jnp.bfloat16])
+    (sums,) = coarse_chunk(None, (items, counts, a), blocks, [(0, total, jnp.bfloat16)])
     parts = sums.reshape(n, total // n, *sums.shape[1:])
     parts = lax.all_to_all(parts, "col", 0, 0, tiled=True)
     return jnp.sum(parts.astype(jnp.float32), axis=0).astype(jnp.bfloat16)

time: 47.8 us -> 44.9 us (0.939)
  Pallas kernels: 11.4 us -> 8.69 us
  waiting for transfers between devices: 21.6 us -> 18.9 us
  starting transfers between devices: 13.7 us -> 16.1 us
    ppermute x8 -> x10, waiting for transfers between devices: 21.6 us -> 18.9 us  [line_of_four(): cross = lambda block, pairs: lax.ppermute(block, 'col', pairs)]
    ppermute x8 -> x10, starting transfers between devices: 12.4 us -> 14.7 us  [line_of_four(): cross = lambda block, pairs: lax.ppermute(block, 'col', pairs)]
    pallas_call x5 -> x8, Pallas kernels: 10.3 us -> 8.53 us  [the longest x4 4.59 us: coarse_chunk(): pl.pallas_call(functools.partial(chunk_kernel, held, pick, len(blocks), [...]
    pallas_call x4, Pallas kernels: 1.09 us -> 0.15 us  [added(): pl.pallas_call(functools.partial(add_kernel, len(xs)), out_shape=jax.Shap...]
  transfers between devices with their start and end apart: 10 -> 12, of which waited for: 5 -> 7; matrix products, arithmetic and copies ran while one was open for 0% -> 0% of each run, Pallas kernels for 18% -> 15%
where the time goes in v4:
time: 44.9 us; the launch traced here: 44.4 us
  waiting for transfers between devices  18.9 us (42%)
  starting transfers between devices  16.1 us (36%)
  Pallas kernels  8.69 us (19%)
  between operations  0.79 us (2%)
    ppermute x10, waiting for transfers between devices, line_of_four(): cross = lambda block, pairs: lax.ppermute(block, 'col', pairs)  18.9 us
    ppermute x10, starting transfers between devices, line_of_four(): cross = lambda block, pairs: lax.ppermute(block, 'col', pairs)  14.7 us
    pallas_call x4, Pallas kernels, coarse_chunk(): pl.pallas_call(functools.partial(chunk_kernel, held, pick, len(blocks), [...  4.59 us
    pallas_call x1, Pallas kernels, plan(): pl.pallas_call(functools.partial(plan_kernel, held, n), out_shape=(pltpu....  2.97 us
    ppermute x2, starting transfers between devices, shifted(): lax.ppermute(block, axis, [((i - distance) % n, i) for i in range(n)])  1.33 us
  transfers between devices with their start and end apart: 12, of which 7 were waited for; matrix products, arithmetic and copies ran while one was open for 0% of the time, Pallas kernels for 15%

profile of v4, /device:TPU:0, one launch (start us, length us, event | category | flops | bytes accessed | tf_op | source)
XLA Modules:
  0.0 44.4 jit_solution(13706581235940324935)
XLA Ops:
  0.0 5.0 %collective-permute-start.2 = (bf16[4,128,128]{2,1,0:T(8,128)(2,1)}, bf16[4,128,128]{2,1,0:T(8,128)(2,1)S(1)}, u32[]{:S(2)}, u32[]{:S(2)}) collective-permute-start(bf16[4,128,128]{2,1,0:T(8,128)(2,1)} %p.1), channel_id=1, source_target_pairs={{0,3},{1,2},{2,1},{3,0},{4,7},{5,6},{6,5},{7,4},{8,11},{9,10},{10,... | collective-permute-start | bytes 393224 | tf_op jit(solution)/shard_map/ppermute | solution.py:218
  5.0 0.0 collective-permute-start.1
  5.1 0.6 %collective-permute-start = (bf16[4,128,128]{2,1,0:T(8,128)(2,1)}, bf16[4,128,128]{2,1,0:T(8,128)(2,1)S(1)}, u32[]{:S(2)}, u32[]{:S(2)}) collective-permute-start(bf16[4,128,128]{2,1,0:T(8,128)(2,1)} %p.1), channel_id=1, source_target_pairs={{0,2},{1,3},{2,0},{3,1},{4,6},{5,7},{6,4},{7,5},{8,10},{9,11},{10,... | collective-permute-start | bytes 393224 | tf_op jit(solution)/shard_map/ppermute | solution.py:218
  5.6 1.3 %collective-permute-start.4 = (bf16[4,128,128]{2,1,0:T(8,128)(2,1)}, bf16[4,128,128]{2,1,0:T(8,128)(2,1)S(1)}, u32[]{:S(2)}, u32[]{:S(2)}) collective-permute-start(bf16[4,128,128]{2,1,0:T(8,128)(2,1)} %p.1), channel_id=1, source_target_pairs={{4,0},{8,4},{12,8},{16,12},{20,16},{24,20},{28,24},{0,28},{5,1},{9... | collective-permute-start | bytes 393224 | tf_op jit(solution)/shard_map/ppermute | solution.py:210
  6.9 0.0 collective-permute-start.3
  7.6 3.0 %plan.1 = (s32[512]{0:T(512)S(4)}, s32[5]{0:T(128)S(4)}, bf16[128,128,128]{2,1,0:T(8,128)(2,1)S(1)}, bf16[4,128,128]{2,1,0:T(8,128)(2,1)S(1)}) custom-call(s32[1]{0:T(128)} %bitcast.me, s32[128]{0:T(128)} %a_row.1, s32[128]{0:T(128)} %a_col.1, s32[1]{0:T(128)S(6)} %copy.6.a_count, bf16[128,128,128]{2,1,0:T(8,128)(2,1)} %a.1, bf16[4,128,128]{2,1,0:T(8,128)(2,1)} %p.1), custom_call_target="tpu_custom_call" | custom-call | tf_op jit(solution)/shard_map/plan/pallas_call | solution.py:61
  10.6 0.0 collective-permute-done.2.rest_2_
  10.6 2.1 %collective-permute-done.1.rest_1_ = bf16[4,128,128]{2,1,0:T(8,128)(2,1)S(1)} collective-permute-done((bf16[4,128,128]{2,1,0:T(8,128)(2,1)}, bf16[4,128,128]{2,1,0:T(8,128)(2,1)S(1)}, u32[]{:S(2)}, u32[]{:S(2)}) %collective-permute-start.1) | collective-permute-done | bytes 131104 | tf_op jit(solution)/shard_map/ppermute | solution.py:218
  12.7 3.7 %collective-permute-done.rest_0_ = bf16[4,128,128]{2,1,0:T(8,128)(2,1)S(1)} collective-permute-done((bf16[4,128,128]{2,1,0:T(8,128)(2,1)}, bf16[4,128,128]{2,1,0:T(8,128)(2,1)S(1)}, u32[]{:S(2)}, u32[]{:S(2)}) %collective-permute-start) | collective-permute-done | bytes 131104 | tf_op jit(solution)/shard_map/ppermute | solution.py:218
  16.3 0.0 collective-permute-done.4.rest_5_
  16.3 0.0 collective-permute-done.3.rest_3_
  16.3 1.0 %coarse_chunk.4 = (bf16[6,128,128]{2,1,0:T(8,128)(2,1)S(1)}, bf16[6,128,128]{2,1,0:T(8,128)(2,1)S(1)}, f32[6,128,128]{2,1,0:T(8,128)S(1)}, f32[6,128,128]{2,1,0:T(8,128)S(1)}) custom-call(s32[512]{0:T(512)S(4)} %get-tuple-element.18.items, s32[5]{0:T(128)S(4)} %get-tuple-element.17.counts, bf16[128,128,128]{2,1,0:T(8,128)(2,1)S(1)} %get-tuple-element.19.a, ...), custom_call_target="tpu_custom_call" | custom-call | flops 2147483648 | bytes 1048576 | tf_op jit(solution)/shard_map/coarse_chunk/pallas_call | solution.py:133
  17.3 1.3 %collective-permute-start.6 = (bf16[6,128,128]{2,1,0:T(8,128)(2,1)S(1)}, bf16[6,128,128]{2,1,0:T(8,128)(2,1)S(1)}, u32[]{:S(2)}, u32[]{:S(2)}) collective-permute-start(bf16[6,128,128]{2,1,0:T(8,128)(2,1)S(1)} %get-tuple-element.21.rest_6_), channel_id=1, source_target_pairs={{0,1},{3,2},{4,5},{7,6},{8,9},{11,10},{12,13},{15,14},{16,17},{19,... | collective-permute-start | bytes 589832 | tf_op jit(solution)/shard_map/ppermute | solution.py:218
  18.7 1.0 %coarse_chunk.5 = (bf16[6,128,128]{2,1,0:T(8,128)(2,1)S(1)}, bf16[6,128,128]{2,1,0:T(8,128)(2,1)S(1)}, f32[6,128,128]{2,1,0:T(8,128)S(1)}, f32[6,128,128]{2,1,0:T(8,128)S(1)}) custom-call(s32[512]{0:T(512)S(4)} %get-tuple-element.18.items, s32[5]{0:T(128)S(4)} %get-tuple-element.17.counts, bf16[128,128,128]{2,1,0:T(8,128)(2,1)S(1)} %get-tuple-element.19.a, ...), custom_call_target="tpu_custom_call" | custom-call | flops 2147483648 | bytes 1048576 | tf_op jit(solution)/shard_map/coarse_chunk/pallas_call | solution.py:133
  19.7 1.3 %collective-permute-start.5 = (bf16[6,128,128]{2,1,0:T(8,128)(2,1)S(1)}, bf16[6,128,128]{2,1,0:T(8,128)(2,1)S(1)}, u32[]{:S(2)}, u32[]{:S(2)}) collective-permute-start(bf16[6,128,128]{2,1,0:T(8,128)(2,1)S(1)} %added.4), channel_id=1, source_target_pairs={{0,1},{3,2},{4,5},{7,6},{8,9},{11,10},{12,13},{15,14},{16,17},{19,... | collective-permute-start | bytes 589832 | tf_op jit(solution)/shard_map/ppermute | solution.py:218
  21.0 3.0 %collective-permute-done.6.z = bf16[6,128,128]{2,1,0:T(8,128)(2,1)S(1)} collective-permute-done((bf16[6,128,128]{2,1,0:T(8,128)(2,1)S(1)}, bf16[6,128,128]{2,1,0:T(8,128)(2,1)S(1)}, u32[]{:S(2)}, u32[]{:S(2)}) %collective-permute-start.6) | collective-permute-done | bytes 196640 | tf_op jit(solution)/shard_map/ppermute | solution.py:218
  24.0 0.1 mixed.2.rest_0_
  24.1 2.5 %collective-permute-start.8 = (bf16[6,128,128]{2,1,0:T(8,128)(2,1)S(1)}, bf16[6,128,128]{2,1,0:T(8,128)(2,1)S(1)}, u32[]{:S(2)}, u32[]{:S(2)}) collective-permute-start(bf16[6,128,128]{2,1,0:T(8,128)(2,1)S(1)} %mixed.2.rest_0_), channel_id=1, source_target_pairs={{0,1},{3,2},{1,3},{2,0},{4,5},{7,6},{5,7},{6,4},{8,9},{11,10},{9,1... | collective-permute-start | bytes 589832 | tf_op jit(solution)/shard_map/ppermute | solution.py:218
  26.6 1.6 %collective-permute-done.5.z = bf16[6,128,128]{2,1,0:T(8,128)(2,1)S(1)} collective-permute-done((bf16[6,128,128]{2,1,0:T(8,128)(2,1)S(1)}, bf16[6,128,128]{2,1,0:T(8,128)(2,1)S(1)}, u32[]{:S(2)}, u32[]{:S(2)}) %collective-permute-start.5) | collective-permute-done | bytes 196640 | tf_op jit(solution)/shard_map/ppermute | solution.py:218
  28.2 0.1 mixed.3.rest_6_
  28.3 2.5 %collective-permute-start.7 = (bf16[6,128,128]{2,1,0:T(8,128)(2,1)S(1)}, bf16[6,128,128]{2,1,0:T(8,128)(2,1)S(1)}, u32[]{:S(2)}, u32[]{:S(2)}) collective-permute-start(bf16[6,128,128]{2,1,0:T(8,128)(2,1)S(1)} %mixed.3.rest_6_), channel_id=1, source_target_pairs={{0,1},{3,2},{1,3},{2,0},{4,5},{7,6},{5,7},{6,4},{8,9},{11,10},{9,1... | collective-permute-start | bytes 589832 | tf_op jit(solution)/shard_map/ppermute | solution.py:218
  30.8 1.3 %coarse_chunk.6.refs_2_ = bf16[12,128,128]{2,1,0:T(8,128)(2,1)S(1)} custom-call(s32[512]{0:T(512)S(4)} %get-tuple-element.18.items, s32[5]{0:T(128)S(4)} %get-tuple-element.17.counts, bf16[128,128,128]{2,1,0:T(8,128)(2,1)S(1)} %get-tuple-element.19.a, bf16[4,128,128]{2,1,0:T(8,128)(2,1)S(1)} %collective-permute-done.rest_0_, ...), custom_call_target="tpu_custom_call" | custom-call | flops 2147483648 | bytes 1048576 | tf_op jit(solution)/shard_map/coarse_chunk/pallas_call | solution.py:133
  32.1 0.1 collective-permute-start.9
  32.2 0.8 %collective-permute-done.8.refs_1_.far_a = bf16[6,128,128]{2,1,0:T(8,128)(2,1)S(1)} collective-permute-done((bf16[6,128,128]{2,1,0:T(8,128)(2,1)S(1)}, bf16[6,128,128]{2,1,0:T(8,128)(2,1)S(1)}, u32[]{:S(2)}, u32[]{:S(2)}) %collective-permute-start.8) | collective-permute-done | bytes 196640 | tf_op jit(solution)/shard_map/ppermute | solution.py:218
  33.1 0.7 %collective-permute-start.10 = (bf16[6,128,128]{2,1,0:T(8,128)(2,1)S(1)}, bf16[6,128,128]{2,1,0:T(8,128)(2,1)S(1)}, u32[]{:S(2)}, u32[]{:S(2)}) collective-permute-start(bf16[6,128,128]{2,1,0:T(8,128)(2,1)S(1)} %added.5.refs_2_), channel_id=1, source_target_pairs={{1,2},{2,1},{5,6},{6,5},{9,10},{10,9},{13,14},{14,13},{17,18},{18,... | collective-permute-start | bytes 589832 | tf_op jit(solution)/shard_map/ppermute | solution.py:218
  33.7 2.9 %collective-permute-done.7.refs_1_.far_b = bf16[6,128,128]{2,1,0:T(8,128)(2,1)S(1)} collective-permute-done((bf16[6,128,128]{2,1,0:T(8,128)(2,1)S(1)}, bf16[6,128,128]{2,1,0:T(8,128)(2,1)S(1)}, u32[]{:S(2)}, u32[]{:S(2)}) %collective-permute-start.7) | collective-permute-done | bytes 196640 | tf_op jit(solution)/shard_map/ppermute | solution.py:218
  36.7 0.7 %collective-permute-start.11 = (bf16[6,128,128]{2,1,0:T(8,128)(2,1)S(1)}, bf16[6,128,128]{2,1,0:T(8,128)(2,1)S(1)}, u32[]{:S(2)}, u32[]{:S(2)}) collective-permute-start(bf16[6,128,128]{2,1,0:T(8,128)(2,1)S(1)} %added.6.rest_6_), channel_id=1, source_target_pairs={{1,2},{2,1},{5,6},{6,5},{9,10},{10,9},{13,14},{14,13},{17,18},{18,... | collective-permute-start | bytes 589832 | tf_op jit(solution)/shard_map/ppermute | solution.py:218
  37.3 1.3 %coarse_chunk.7.refs_0_ = f32[12,128,128]{2,1,0:T(8,128)S(1)} custom-call(s32[512]{0:T(512)S(4)} %get-tuple-element.18.items, s32[5]{0:T(128)S(4)} %get-tuple-element.17.counts, bf16[128,128,128]{2,1,0:T(8,128)(2,1)S(1)} %get-tuple-element.19.a, bf16[4,128,128]{2,1,0:T(8,128)(2,1)S(1)} %collective-permute-done.rest_0_, ...), custom_call_target="tpu_custom_call" | custom-call | flops 2147483648 | bytes 1048576 | tf_op jit(solution)/shard_map/coarse_chunk/pallas_call | solution.py:133
  38.7 4.8 %collective-permute-done.9.refs_1_ = bf16[12,128,128]{2,1,0:T(8,128)(2,1)S(1)} collective-permute-done((bf16[12,128,128]{2,1,0:T(8,128)(2,1)S(1)}, bf16[12,128,128]{2,1,0:T(8,128)(2,1)S(1)}, u32[]{:S(2)}, u32[]{:S(2)}) %collective-permute-start.9) | collective-permute-done | bytes 393248 | tf_op jit(solution)/shard_map/ppermute | solution.py:218
  43.4 0.1 added.7.most
  43.5 0.0 collective-permute-done.11.near_b
  43.5 0.0 collective-permute-done.10.near_a
  43.5 0.9 %finished.1 = bf16[12,128,128]{2,1,0:T(8,128)(2,1)} custom-call(s32[5]{0:T(128)S(4)} %get-tuple-element.17.counts, f32[12,128,128]{2,1,0:T(8,128)S(1)} %added.7.most, bf16[6,128,128]{2,1,0:T(8,128)(2,1)S(1)} %collective-permute-done.8.refs_1_.far_a, bf16[6,128,128]{2,1,0:T(8,128)(2,1)S(1)} %collective-permute-done.7.refs_1_.far_b, ...), custom_call_target="tpu_custom_call" | custom-call | tf_op jit(solution)/shard_map/finished/pallas_call | solution.py:179
  (3 shorter events, 0.1 us)
Async XLA Ops:
  0.0 10.6 %collective-permute-start.2 = (bf16[4,128,128]{2,1,0:T(8,128)(2,1)}, bf16[4,128,128]{2,1,0:T(8,128)(2,1)S(1)}, u32[]{:S(2)}, u32[]{:S(2)}) collective-permute-start(bf16[4,128,128]{2,1,0:T(8,128)(2,1)} %p.1), channel_id=1, source_target_pairs={{0,3},{1,2},{2,1},{3,0},{4,7},{5,6},{6,5},{7,4},{8,11},{9,10},{10,... | collective-permute-start | bytes 393224 | tf_op jit(solution)/shard_map/ppermute | solution.py:218
  5.0 7.6 %collective-permute-start.1 = (bf16[4,128,128]{2,1,0:T(8,128)(2,1)}, bf16[4,128,128]{2,1,0:T(8,128)(2,1)S(1)}, u32[]{:S(2)}, u32[]{:S(2)}) collective-permute-start(bf16[4,128,128]{2,1,0:T(8,128)(2,1)} %p.1), channel_id=1, source_target_pairs={{0,1},{1,0},{2,3},{3,2},{4,5},{5,4},{6,7},{7,6},{8,9},{9,8},{10,11... | collective-permute-start | bytes 393224 | tf_op jit(solution)/shard_map/ppermute | solution.py:218
  5.1 11.3 %collective-permute-start = (bf16[4,128,128]{2,1,0:T(8,128)(2,1)}, bf16[4,128,128]{2,1,0:T(8,128)(2,1)S(1)}, u32[]{:S(2)}, u32[]{:S(2)}) collective-permute-start(bf16[4,128,128]{2,1,0:T(8,128)(2,1)} %p.1), channel_id=1, source_target_pairs={{0,2},{1,3},{2,0},{3,1},{4,6},{5,7},{6,4},{7,5},{8,10},{9,11},{10,... | collective-permute-start | bytes 393224 | tf_op jit(solution)/shard_map/ppermute | solution.py:218
  5.6 10.7 %collective-permute-start.4 = (bf16[4,128,128]{2,1,0:T(8,128)(2,1)}, bf16[4,128,128]{2,1,0:T(8,128)(2,1)S(1)}, u32[]{:S(2)}, u32[]{:S(2)}) collective-permute-start(bf16[4,128,128]{2,1,0:T(8,128)(2,1)} %p.1), channel_id=1, source_target_pairs={{4,0},{8,4},{12,8},{16,12},{20,16},{24,20},{28,24},{0,28},{5,1},{9... | collective-permute-start | bytes 393224 | tf_op jit(solution)/shard_map/ppermute | solution.py:210
  6.9 9.4 %collective-permute-start.3 = (bf16[4,128,128]{2,1,0:T(8,128)(2,1)}, bf16[4,128,128]{2,1,0:T(8,128)(2,1)S(1)}, u32[]{:S(2)}, u32[]{:S(2)}) collective-permute-start(bf16[4,128,128]{2,1,0:T(8,128)(2,1)} %p.1), channel_id=1, source_target_pairs={{28,0},{0,4},{4,8},{8,12},{12,16},{16,20},{20,24},{24,28},{29,1},{... | collective-permute-start | bytes 393224 | tf_op jit(solution)/shard_map/ppermute | solution.py:210
  17.3 6.7 %collective-permute-start.6 = (bf16[6,128,128]{2,1,0:T(8,128)(2,1)S(1)}, bf16[6,128,128]{2,1,0:T(8,128)(2,1)S(1)}, u32[]{:S(2)}, u32[]{:S(2)}) collective-permute-start(bf16[6,128,128]{2,1,0:T(8,128)(2,1)S(1)} %get-tuple-element.21.rest_6_), channel_id=1, source_target_pairs={{0,1},{3,2},{4,5},{7,6},{8,9},{11,10},{12,13},{15,14},{16,17},{19,... | collective-permute-start | bytes 589832 | tf_op jit(solution)/shard_map/ppermute | solution.py:218
  19.7 8.5 %collective-permute-start.5 = (bf16[6,128,128]{2,1,0:T(8,128)(2,1)S(1)}, bf16[6,128,128]{2,1,0:T(8,128)(2,1)S(1)}, u32[]{:S(2)}, u32[]{:S(2)}) collective-permute-start(bf16[6,128,128]{2,1,0:T(8,128)(2,1)S(1)} %added.4), channel_id=1, source_target_pairs={{0,1},{3,2},{4,5},{7,6},{8,9},{11,10},{12,13},{15,14},{16,17},{19,... | collective-permute-start | bytes 589832 | tf_op jit(solution)/shard_map/ppermute | solution.py:218
  24.1 9.0 %collective-permute-start.8 = (bf16[6,128,128]{2,1,0:T(8,128)(2,1)S(1)}, bf16[6,128,128]{2,1,0:T(8,128)(2,1)S(1)}, u32[]{:S(2)}, u32[]{:S(2)}) collective-permute-start(bf16[6,128,128]{2,1,0:T(8,128)(2,1)S(1)} %mixed.2.rest_0_), channel_id=1, source_target_pairs={{0,1},{3,2},{1,3},{2,0},{4,5},{7,6},{5,7},{6,4},{8,9},{11,10},{9,1... | collective-permute-start | bytes 589832 | tf_op jit(solution)/shard_map/ppermute | solution.py:218
  28.3 8.4 %collective-permute-start.7 = (bf16[6,128,128]{2,1,0:T(8,128)(2,1)S(1)}, bf16[6,128,128]{2,1,0:T(8,128)(2,1)S(1)}, u32[]{:S(2)}, u32[]{:S(2)}) collective-permute-start(bf16[6,128,128]{2,1,0:T(8,128)(2,1)S(1)} %mixed.3.rest_6_), channel_id=1, source_target_pairs={{0,1},{3,2},{1,3},{2,0},{4,5},{7,6},{5,7},{6,4},{8,9},{11,10},{9,1... | collective-permute-start | bytes 589832 | tf_op jit(solution)/shard_map/ppermute | solution.py:218
  32.1 11.3 %collective-permute-start.9 = (bf16[12,128,128]{2,1,0:T(8,128)(2,1)S(1)}, bf16[12,128,128]{2,1,0:T(8,128)(2,1)S(1)}, u32[]{:S(2)}, u32[]{:S(2)}) collective-permute-start(bf16[12,128,128]{2,1,0:T(8,128)(2,1)S(1)} %coarse_chunk.6.refs_2_), channel_id=1, source_target_pairs={{0,1},{1,0},{2,3},{3,2},{4,5},{5,4},{6,7},{7,6},{8,9},{9,8},{10,11... | collective-permute-start | bytes 1179656 | tf_op jit(solution)/shard_map/ppermute | solution.py:218
  33.1 10.5 %collective-permute-start.10 = (bf16[6,128,128]{2,1,0:T(8,128)(2,1)S(1)}, bf16[6,128,128]{2,1,0:T(8,128)(2,1)S(1)}, u32[]{:S(2)}, u32[]{:S(2)}) collective-permute-start(bf16[6,128,128]{2,1,0:T(8,128)(2,1)S(1)} %added.5.refs_2_), channel_id=1, source_target_pairs={{1,2},{2,1},{5,6},{6,5},{9,10},{10,9},{13,14},{14,13},{17,18},{18,... | collective-permute-start | bytes 589832 | tf_op jit(solution)/shard_map/ppermute | solution.py:218
  36.7 6.8 %collective-permute-start.11 = (bf16[6,128,128]{2,1,0:T(8,128)(2,1)S(1)}, bf16[6,128,128]{2,1,0:T(8,128)(2,1)S(1)}, u32[]{:S(2)}, u32[]{:S(2)}) collective-permute-start(bf16[6,128,128]{2,1,0:T(8,128)(2,1)S(1)} %added.6.rest_6_), channel_id=1, source_target_pairs={{1,2},{2,1},{5,6},{6,5},{9,10},{10,9},{13,14},{14,13},{17,18},{18,... | collective-permute-start | bytes 589832 | tf_op jit(solution)/shard_map/ppermute | solution.py:218

commit v5 on v4

--- a/solution.py
+++ b/solution.py
@@ -79,50 +79,53 @@
     slots, chunk = a.shape[0], accum.shape[0] - 1
     me = counts[counts.shape[0] - 1]
     d = 0 if pick is None else sum(jnp.where(me == i, x, 0) for i, x in enumerate(pick))
-    base, count = d * slots, counts[d]
-    if pick is None:
-        rights, rows = blocks[:3], blocks[3]
-        for i in range(left.shape[0]):
-            left[i] = rows[i].T
-    else:
-        part = dict(zip(PARTS, blocks))
-        rights = part["below"], part["own"], part["above"]
-        left[0] = part["own"][d].T
-        left[1] = part["once"][d].T
-        left[2] = part["twice"][d].T
-        left[3] = part["thrice"][d].T
-    for i, ref in enumerate(rights):
-        right[i * held : (i + 1) * held] = ref[...]
-    accum[...] = jnp.zeros_like(accum)
-
-    def unpack(e):
-        item = items[base + jnp.minimum(e, count - 1)]
-        t, item = item & ((1 << bits(slots)) - 1), item >> bits(slots)
-        col, row = item & ((1 << bits(3 * held)) - 1), item >> bits(3 * held)
+
+    @pl.when(d >= 0)
+    def _():
+        base, count = d * slots, counts[d]
         if pick is None:
-            s = divide(row, held)[1] * (3 * held) + col
+            rights, rows = blocks[:3], blocks[3]
+            for i in range(left.shape[0]):
+                left[i] = rows[i].T
         else:
-            row, s = divide(row, held)[0] ^ me, col
-        return t, col, row, jnp.where(e < count, s, chunk)
-
-    done = jnp.int32(0)
-    for unroll, smaller in zip(UNROLLS, (*UNROLLS[1:], 0)):
-
-        def advance(step, carry, done=done, unroll=unroll):
-            work = [unpack(done + step * unroll + u) for u in range(unroll)]
-            f32 = jnp.float32
-            images = [jnp.dot(a[t], right[col], preferred_element_type=f32) for t, col, _, _ in work]
-            images = [image.astype(jnp.bfloat16) for image in images]
-            terms = [jnp.dot(left[w[2]], x, preferred_element_type=f32) for w, x in zip(work, images)]
-            for w, term in zip(work, terms):
-                accum[w[3]] += term
-            return carry
-
-        steps = lax.div(jnp.maximum(count - done, 0) + unroll - smaller - 1, unroll)
-        lax.fori_loop(0, steps, advance, 0)
-        done = done + steps * unroll
-    for out, start in zip(outs, parts):
-        out[...] = accum[start : start + out.shape[0]].astype(out.dtype)
+            part = dict(zip(PARTS, blocks))
+            rights = part["below"], part["own"], part["above"]
+            left[0] = part["own"][d].T
+            left[1] = part["once"][d].T
+            left[2] = part["twice"][d].T
+            left[3] = part["thrice"][d].T
+        for i, ref in enumerate(rights):
+            right[i * held : (i + 1) * held] = ref[...]
+        accum[...] = jnp.zeros_like(accum)
+
+        def unpack(e):
+            item = items[base + jnp.minimum(e, count - 1)]
+            t, item = item & ((1 << bits(slots)) - 1), item >> bits(slots)
+            col, row = item & ((1 << bits(3 * held)) - 1), item >> bits(3 * held)
+            if pick is None:
+                s = divide(row, held)[1] * (3 * held) + col
+            else:
+                row, s = divide(row, held)[0] ^ me, col
+            return t, col, row, jnp.where(e < count, s, chunk)
+
+        done = jnp.int32(0)
+        for unroll, smaller in zip(UNROLLS, (*UNROLLS[1:], 0)):
+
+            def advance(step, carry, done=done, unroll=unroll):
+                work = [unpack(done + step * unroll + u) for u in range(unroll)]
+                f32 = jnp.float32
+                images = [jnp.dot(a[t], right[col], preferred_element_type=f32) for t, col, _, _ in work]
+                images = [image.astype(jnp.bfloat16) for image in images]
+                terms = [jnp.dot(left[w[2]], x, preferred_element_type=f32) for w, x in zip(work, images)]
+                for w, term in zip(work, terms):
+                    accum[w[3]] += term
+                return carry
+
+            steps = lax.div(jnp.maximum(count - done, 0) + unroll - smaller - 1, unroll)
+            lax.fori_loop(0, steps, advance, 0)
+            done = done + steps * unroll
+        for out, start in zip(outs, parts):
+            out[...] = accum[start : start + out.shape[0]].astype(out.dtype)
 
 
 def coarse_chunk(pick, listed, blocks, outs, after=()):
@@ -165,25 +168,41 @@
     )(counts, x, y, z, *after)
 
 
-def finish_kernel(counts, most, far_a, far_b, near_a, near_b, out):
+def most_kernel(counts, at_end, elsewhere, far, near, out):
     me = counts[counts.shape[0] - 1]
-    half = far_a.shape[0]
+    end = (me == 0) | (me == 3)
     f32 = jnp.float32
-    end = (me == 0) | (me == 3)
-    for i, (far, near) in enumerate(((far_a, near_a), (far_b, near_b))):
+    out[...] = jnp.where(end, at_end[...], elsewhere[...]) + jnp.where(end, far[...], near[...]).astype(f32)
+
+
+def finish_kernel(most_a, most_b, got, out):
+    half = most_a.shape[0]
+    for i, most in enumerate((most_a, most_b)):
         part = slice(i * half, (i + 1) * half)
-        out[part] = (most[part] + jnp.where(end, far[...], near[...]).astype(f32)).astype(out.dtype)
-
-
-def finished(counts, most, *got):
+        out[part] = (most[...] + got[part].astype(jnp.float32)).astype(out.dtype)
+
+
+def finished(counts, own, got, last):
+    params = pltpu.CompilerParams(vmem_limit_bytes=LIMIT)
+    most = [
+        pl.pallas_call(
+            most_kernel,
+            out_shape=jax.ShapeDtypeStruct(x.shape, x.dtype),
+            in_specs=[SMEM] + [VMEM] * 4,
+            out_specs=VMEM,
+            compiler_params=params,
+            name="most",
+        )(counts, x, y, far, near)
+        for x, y, far, near in zip(*own, *got)
+    ]
     return pl.pallas_call(
         finish_kernel,
-        out_shape=jax.ShapeDtypeStruct(most.shape, got[0].dtype),
-        in_specs=[SMEM] + [VMEM] * 5,
+        out_shape=jax.ShapeDtypeStruct(last.shape, last.dtype),
+        in_specs=[VMEM] * 3,
         out_specs=VMEM,
-        compiler_params=pltpu.CompilerParams(vmem_limit_bytes=LIMIT),
+        compiler_params=params,
         name="finished",
-    )(counts, most, *got)
+    )(*most, last)
 
 
 def add_kernel(n, *refs):
@@ -228,24 +247,26 @@
     bf16, f32 = jnp.bfloat16, jnp.float32
     chunk, half = 3 * held, 3 * held // 2
     cut = [(0, half), (half, chunk)]
-    halves = [(*c, bf16) for c in cut] + [(*c, f32) for c in cut]
+    narrow, full = [(*c, bf16) for c in cut], [(*c, f32) for c in cut]
     ends, middles, over = [(0, 1), (3, 2)], [(1, 2), (2, 1)], [(1, 3), (2, 0)]
-    *first, wide_a, wide_b = coarse_chunk((3, 3, 0, 0), listed, blocks, halves)
+    part = lambda pick, outs, after=(): coarse_chunk(pick, listed, blocks, outs, after)
+    first = part((3, -1, -1, 0), narrow)
     got1 = cross(first[0], ends)
-    *second, next_a, next_b = coarse_chunk((2, 2, 1, 1), listed, blocks, halves, first[:1])
+    *second, wide_a, wide_b = part((2, 3, 0, 1), narrow + full, first[:1])
     got2 = cross(added(first[1:], bf16, second[:1]), ends)
     sent3 = mixed(counts, second[0], wide_a, got1)
     got3 = cross(sent3, ends + over)
     sent4 = mixed(counts, second[1], wide_b, got2, [sent3])
     got4 = cross(sent4, ends + over)
-    (third,) = coarse_chunk((1, 0, 3, 2), listed, blocks, [(0, chunk, bf16)], [sent4])
+    (third,) = part((1, 0, 3, 2), [(0, chunk, bf16)], [sent4])
     got5 = cross(third, flips[1])
-    sent6 = added([next_a, got3], bf16, [third])
+    fourth = part((0, 2, 1, 3), full, [third])
+    sent6 = added([fourth[0], got3], bf16, [third])
     got6 = cross(sent6, middles)
-    sent7 = added([next_b, got4], bf16, [sent6])
+    sent7 = added([fourth[1], got4], bf16, [sent6])
     got7 = cross(sent7, middles)
-    (last,) = coarse_chunk((0, 1, 2, 3), listed, blocks, [(0, chunk, f32)], [sent7])
-    return finished(counts, added([last, got5], f32), got3, got4, got6, got7)
+    fifth = part((-1, 1, 2, -1), full, [sent7])
+    return finished(counts, [fourth, fifth], [(got3, got4), (got6, got7)], got5)
 
 
 def any_columns(a_tiles, a_row, a_col, a_count, p_tiles):

time: 44.9 us -> 45.2 us (level)
  the two profiles are of different devices: /device:TPU:0 before, /device:TPU:8 now
where the time goes in v5:
time: 45.2 us; the launch traced here: 44.6 us
  starting transfers between devices  19.7 us (44%)
  waiting for transfers between devices  17.5 us (39%)
  Pallas kernels  6.58 us (15%)
  between operations  0.78 us (2%)
    ppermute x10, starting transfers between devices, line_of_four(): cross = lambda block, pairs: lax.ppermute(block, 'col', pairs)  18.4 us
    ppermute x10, waiting for transfers between devices, line_of_four(): cross = lambda block, pairs: lax.ppermute(block, 'col', pairs)  17.5 us
    pallas_call x1, Pallas kernels, plan(): pl.pallas_call(functools.partial(plan_kernel, held, n), out_shape=(pltpu....  2.97 us
    pallas_call x5, Pallas kernels, coarse_chunk(): pl.pallas_call(functools.partial(chunk_kernel, held, pick, len(blocks), [...  2.45 us
    ppermute x2, starting transfers between devices, shifted(): lax.ppermute(block, axis, [((i - distance) % n, i) for i in range(n)])  1.33 us
  transfers between devices with their start and end apart: 12, of which 8 were waited for; matrix products, arithmetic and copies ran while one was open for 0% of the time, Pallas kernels for 13%

profile of v5, /device:TPU:8, one launch (start us, length us, event | category | flops | bytes accessed | tf_op | source)
XLA Modules:
  0.0 44.6 jit_solution(11218543410428370838)
XLA Ops:
  0.0 1.6 %collective-permute-start.2 = (bf16[4,128,128]{2,1,0:T(8,128)(2,1)}, bf16[4,128,128]{2,1,0:T(8,128)(2,1)S(1)}, u32[]{:S(2)}, u32[]{:S(2)}) collective-permute-start(bf16[4,128,128]{2,1,0:T(8,128)(2,1)} %p.1), channel_id=1, source_target_pairs={{0,3},{1,2},{2,1},{3,0},{4,7},{5,6},{6,5},{7,4},{8,11},{9,10},{10,... | collective-permute-start | bytes 393224 | tf_op jit(solution)/shard_map/ppermute | solution.py:237
  1.6 2.5 %collective-permute-start.1 = (bf16[4,128,128]{2,1,0:T(8,128)(2,1)}, bf16[4,128,128]{2,1,0:T(8,128)(2,1)S(1)}, u32[]{:S(2)}, u32[]{:S(2)}) collective-permute-start(bf16[4,128,128]{2,1,0:T(8,128)(2,1)} %p.1), channel_id=1, source_target_pairs={{0,1},{1,0},{2,3},{3,2},{4,5},{5,4},{6,7},{7,6},{8,9},{9,8},{10,11... | collective-permute-start | bytes 393224 | tf_op jit(solution)/shard_map/ppermute | solution.py:237
  4.1 0.0 collective-permute-start
  4.1 1.3 %collective-permute-start.4 = (bf16[4,128,128]{2,1,0:T(8,128)(2,1)}, bf16[4,128,128]{2,1,0:T(8,128)(2,1)S(1)}, u32[]{:S(2)}, u32[]{:S(2)}) collective-permute-start(bf16[4,128,128]{2,1,0:T(8,128)(2,1)} %p.1), channel_id=1, source_target_pairs={{4,0},{8,4},{12,8},{16,12},{20,16},{24,20},{28,24},{0,28},{5,1},{9... | collective-permute-start | bytes 393224 | tf_op jit(solution)/shard_map/ppermute | solution.py:229
  5.4 0.0 collective-permute-start.3
  6.0 3.0 %plan.1 = (s32[512]{0:T(512)S(4)}, s32[5]{0:T(128)S(4)}, bf16[128,128,128]{2,1,0:T(8,128)(2,1)S(1)}, bf16[4,128,128]{2,1,0:T(8,128)(2,1)S(1)}) custom-call(s32[1]{0:T(128)} %bitcast.me, s32[128]{0:T(128)} %a_row.1, s32[128]{0:T(128)} %a_col.1, s32[1]{0:T(128)S(6)} %copy.6.a_count, bf16[128,128,128]{2,1,0:T(8,128)(2,1)} %a.1, bf16[4,128,128]{2,1,0:T(8,128)(2,1)} %p.1), custom_call_target="tpu_custom_call" | custom-call | tf_op jit(solution)/shard_map/plan/pallas_call | solution.py:61
  9.0 1.0 %collective-permute-done.2.rest_2_ = bf16[4,128,128]{2,1,0:T(8,128)(2,1)S(1)} collective-permute-done((bf16[4,128,128]{2,1,0:T(8,128)(2,1)}, bf16[4,128,128]{2,1,0:T(8,128)(2,1)S(1)}, u32[]{:S(2)}, u32[]{:S(2)}) %collective-permute-start.2) | collective-permute-done | bytes 131104 | tf_op jit(solution)/shard_map/ppermute | solution.py:237
  10.1 1.4 %collective-permute-done.1.rest_1_ = bf16[4,128,128]{2,1,0:T(8,128)(2,1)S(1)} collective-permute-done((bf16[4,128,128]{2,1,0:T(8,128)(2,1)}, bf16[4,128,128]{2,1,0:T(8,128)(2,1)S(1)}, u32[]{:S(2)}, u32[]{:S(2)}) %collective-permute-start.1) | collective-permute-done | bytes 131104 | tf_op jit(solution)/shard_map/ppermute | solution.py:237
  11.4 1.6 %collective-permute-done.rest_0_ = bf16[4,128,128]{2,1,0:T(8,128)(2,1)S(1)} collective-permute-done((bf16[4,128,128]{2,1,0:T(8,128)(2,1)}, bf16[4,128,128]{2,1,0:T(8,128)(2,1)S(1)}, u32[]{:S(2)}, u32[]{:S(2)}) %collective-permute-start) | collective-permute-done | bytes 131104 | tf_op jit(solution)/shard_map/ppermute | solution.py:237
  13.1 0.0 collective-permute-done.4.rest_5_
  13.1 0.0 collective-permute-done.3.rest_3_
  13.1 1.3 %collective-permute-start.6 = (bf16[6,128,128]{2,1,0:T(8,128)(2,1)S(1)}, bf16[6,128,128]{2,1,0:T(8,128)(2,1)S(1)}, u32[]{:S(2)}, u32[]{:S(2)}) collective-permute-start(bf16[6,128,128]{2,1,0:T(8,128)(2,1)S(1)} %get-tuple-element.23.rest_6_), channel_id=1, source_target_pairs={{0,1},{3,2},{4,5},{7,6},{8,9},{11,10},{12,13},{15,14},{16,17},{19,... | collective-permute-start | bytes 589832 | tf_op jit(solution)/shard_map/ppermute | solution.py:237
  14.4 0.7 %coarse_chunk.6 = (bf16[6,128,128]{2,1,0:T(8,128)(2,1)S(1)}, bf16[6,128,128]{2,1,0:T(8,128)(2,1)S(1)}, f32[6,128,128]{2,1,0:T(8,128)S(1)}, f32[6,128,128]{2,1,0:T(8,128)S(1)}) custom-call(s32[512]{0:T(512)S(4)} %get-tuple-element.20.items, s32[5]{0:T(128)S(4)} %get-tuple-element.19.counts, bf16[128,128,128]{2,1,0:T(8,128)(2,1)S(1)} %get-tuple-element.21.a, ...), custom_call_target="tpu_custom_call" | custom-call | flops 2147483648 | bytes 1048576 | tf_op jit(solution)/shard_map/coarse_chunk/pallas_call | solution.py:136
  15.1 1.3 %collective-permute-start.5 = (bf16[6,128,128]{2,1,0:T(8,128)(2,1)S(1)}, bf16[6,128,128]{2,1,0:T(8,128)(2,1)S(1)}, u32[]{:S(2)}, u32[]{:S(2)}) collective-permute-start(bf16[6,128,128]{2,1,0:T(8,128)(2,1)S(1)} %added.3), channel_id=1, source_target_pairs={{0,1},{3,2},{4,5},{7,6},{8,9},{11,10},{12,13},{15,14},{16,17},{19,... | collective-permute-start | bytes 589832 | tf_op jit(solution)/shard_map/ppermute | solution.py:237
  16.4 7.0 %collective-permute-done.6.z = bf16[6,128,128]{2,1,0:T(8,128)(2,1)S(1)} collective-permute-done((bf16[6,128,128]{2,1,0:T(8,128)(2,1)S(1)}, bf16[6,128,128]{2,1,0:T(8,128)(2,1)S(1)}, u32[]{:S(2)}, u32[]{:S(2)}) %collective-permute-start.6) | collective-permute-done | bytes 196640 | tf_op jit(solution)/shard_map/ppermute | solution.py:237
  23.4 0.1 mixed.2.rest_0_
  23.4 1.1 %collective-permute-start.8 = (bf16[6,128,128]{2,1,0:T(8,128)(2,1)S(1)}, bf16[6,128,128]{2,1,0:T(8,128)(2,1)S(1)}, u32[]{:S(2)}, u32[]{:S(2)}) collective-permute-start(bf16[6,128,128]{2,1,0:T(8,128)(2,1)S(1)} %mixed.2.rest_0_), channel_id=1, source_target_pairs={{0,1},{3,2},{1,3},{2,0},{4,5},{7,6},{5,7},{6,4},{8,9},{11,10},{9,1... | collective-permute-start | bytes 589832 | tf_op jit(solution)/shard_map/ppermute | solution.py:237
  24.5 3.1 %collective-permute-done.5.z = bf16[6,128,128]{2,1,0:T(8,128)(2,1)S(1)} collective-permute-done((bf16[6,128,128]{2,1,0:T(8,128)(2,1)S(1)}, bf16[6,128,128]{2,1,0:T(8,128)(2,1)S(1)}, u32[]{:S(2)}, u32[]{:S(2)}) %collective-permute-start.5) | collective-permute-done | bytes 196640 | tf_op jit(solution)/shard_map/ppermute | solution.py:237
  27.6 0.1 mixed.3.rest_6_
  27.6 1.1 %collective-permute-start.7 = (bf16[6,128,128]{2,1,0:T(8,128)(2,1)S(1)}, bf16[6,128,128]{2,1,0:T(8,128)(2,1)S(1)}, u32[]{:S(2)}, u32[]{:S(2)}) collective-permute-start(bf16[6,128,128]{2,1,0:T(8,128)(2,1)S(1)} %mixed.3.rest_6_), channel_id=1, source_target_pairs={{0,1},{3,2},{1,3},{2,0},{4,5},{7,6},{5,7},{6,4},{8,9},{11,10},{9,1... | collective-permute-start | bytes 589832 | tf_op jit(solution)/shard_map/ppermute | solution.py:237
  28.7 0.6 %coarse_chunk.7.rest_6_.refs_2_ = bf16[12,128,128]{2,1,0:T(8,128)(2,1)S(1)} custom-call(s32[512]{0:T(512)S(4)} %get-tuple-element.20.items, s32[5]{0:T(128)S(4)} %get-tuple-element.19.counts, bf16[128,128,128]{2,1,0:T(8,128)(2,1)S(1)} %get-tuple-element.21.a, bf16[4,128,128]{2,1,0:T(8,128)(2,1)S(1)} %collective-permute-done.rest_0_, ...), custom_call_target="tpu_custom_call" | custom-call | flops 2147483648 | bytes 1048576 | tf_op jit(solution)/shard_map/coarse_chunk/pallas_call | solution.py:136
  29.3 1.8 %collective-permute-start.11 = (bf16[12,128,128]{2,1,0:T(8,128)(2,1)S(1)}, bf16[12,128,128]{2,1,0:T(8,128)(2,1)S(1)}, u32[]{:S(2)}, u32[]{:S(2)}) collective-permute-start(bf16[12,128,128]{2,1,0:T(8,128)(2,1)S(1)} %coarse_chunk.7.rest_6_.refs_2_), channel_id=1, source_target_pairs={{0,1},{1,0},{2,3},{3,2},{4,5},{5,4},{6,7},{7,6},{8,9},{9,8},{10,11... | collective-permute-start | bytes 1179656 | tf_op jit(solution)/shard_map/ppermute | solution.py:237
  31.1 0.6 %coarse_chunk.8 = (f32[6,128,128]{2,1,0:T(8,128)S(1)}, f32[6,128,128]{2,1,0:T(8,128)S(1)}) custom-call(s32[512]{0:T(512)S(4)} %get-tuple-element.20.items, s32[5]{0:T(128)S(4)} %get-tuple-element.19.counts, bf16[128,128,128]{2,1,0:T(8,128)(2,1)S(1)} %get-tuple-element.21.a, bf16[4,128,128]{2,1,0:T(8,128)(2,1)S(1)} %collective-permute-done.rest_0_, ...), custom_call_target="tpu_custom_call" | custom-call | flops 2147483648 | bytes 1048576 | tf_op jit(solution)/shard_map/coarse_chunk/pallas_call | solution.py:136
  31.6 0.1 collective-permute-done.8.refs_1_.far
  31.8 3.9 %collective-permute-start.9 = (bf16[6,128,128]{2,1,0:T(8,128)(2,1)S(1)}, bf16[6,128,128]{2,1,0:T(8,128)(2,1)S(1)}, u32[]{:S(2)}, u32[]{:S(2)}) collective-permute-start(bf16[6,128,128]{2,1,0:T(8,128)(2,1)S(1)} %added.4.refs_2_), channel_id=1, source_target_pairs={{1,2},{2,1},{5,6},{6,5},{9,10},{10,9},{13,14},{14,13},{17,18},{18,... | collective-permute-start | bytes 589832 | tf_op jit(solution)/shard_map/ppermute | solution.py:237
  35.8 0.2 collective-permute-done.7.refs_1_.far
  36.1 3.9 %collective-permute-start.10 = (bf16[6,128,128]{2,1,0:T(8,128)(2,1)S(1)}, bf16[6,128,128]{2,1,0:T(8,128)(2,1)S(1)}, u32[]{:S(2)}, u32[]{:S(2)}) collective-permute-start(bf16[6,128,128]{2,1,0:T(8,128)(2,1)S(1)} %added.5.rest_6_), channel_id=1, source_target_pairs={{1,2},{2,1},{5,6},{6,5},{9,10},{10,9},{13,14},{14,13},{17,18},{18,... | collective-permute-start | bytes 589832 | tf_op jit(solution)/shard_map/ppermute | solution.py:237
  40.0 0.6 %coarse_chunk.9 = (f32[6,128,128]{2,1,0:T(8,128)S(1)}, f32[6,128,128]{2,1,0:T(8,128)S(1)}) custom-call(s32[512]{0:T(512)S(4)} %get-tuple-element.20.items, s32[5]{0:T(128)S(4)} %get-tuple-element.19.counts, bf16[128,128,128]{2,1,0:T(8,128)(2,1)S(1)} %get-tuple-element.21.a, bf16[4,128,128]{2,1,0:T(8,128)(2,1)S(1)} %collective-permute-done.rest_0_, ...), custom_call_target="tpu_custom_call" | custom-call | flops 2147483648 | bytes 1048576 | tf_op jit(solution)/shard_map/coarse_chunk/pallas_call | solution.py:136
  40.6 3.0 %collective-permute-done.10.near = bf16[6,128,128]{2,1,0:T(8,128)(2,1)S(1)} collective-permute-done((bf16[6,128,128]{2,1,0:T(8,128)(2,1)S(1)}, bf16[6,128,128]{2,1,0:T(8,128)(2,1)S(1)}, u32[]{:S(2)}, u32[]{:S(2)}) %collective-permute-start.10) | collective-permute-done | bytes 196640 | tf_op jit(solution)/shard_map/ppermute | solution.py:237
  43.6 0.1 most.3.most_b
  43.7 0.0 collective-permute-done.9.near
  43.7 0.1 most.2.most_a
  43.8 0.0 collective-permute-done.11.got
  43.8 0.8 %finished.1 = bf16[12,128,128]{2,1,0:T(8,128)(2,1)} custom-call(f32[6,128,128]{2,1,0:T(8,128)S(1)} %most.2.most_a, f32[6,128,128]{2,1,0:T(8,128)S(1)} %most.3.most_b, bf16[12,128,128]{2,1,0:T(8,128)(2,1)S(1)} %collective-permute-done.11.got), custom_call_target="tpu_custom_call" | custom-call | tf_op jit(solution)/shard_map/finished/pallas_call | solution.py:198
  (4 shorter events, 0.1 us)
Async XLA Ops:
  0.0 10.1 %collective-permute-start.2 = (bf16[4,128,128]{2,1,0:T(8,128)(2,1)}, bf16[4,128,128]{2,1,0:T(8,128)(2,1)S(1)}, u32[]{:S(2)}, u32[]{:S(2)}) collective-permute-start(bf16[4,128,128]{2,1,0:T(8,128)(2,1)} %p.1), channel_id=1, source_target_pairs={{0,3},{1,2},{2,1},{3,0},{4,7},{5,6},{6,5},{7,4},{8,11},{9,10},{10,... | collective-permute-start | bytes 393224 | tf_op jit(solution)/shard_map/ppermute | solution.py:237
  1.6 9.9 %collective-permute-start.1 = (bf16[4,128,128]{2,1,0:T(8,128)(2,1)}, bf16[4,128,128]{2,1,0:T(8,128)(2,1)S(1)}, u32[]{:S(2)}, u32[]{:S(2)}) collective-permute-start(bf16[4,128,128]{2,1,0:T(8,128)(2,1)} %p.1), channel_id=1, source_target_pairs={{0,1},{1,0},{2,3},{3,2},{4,5},{5,4},{6,7},{7,6},{8,9},{9,8},{10,11... | collective-permute-start | bytes 393224 | tf_op jit(solution)/shard_map/ppermute | solution.py:237
  4.1 9.0 %collective-permute-start = (bf16[4,128,128]{2,1,0:T(8,128)(2,1)}, bf16[4,128,128]{2,1,0:T(8,128)(2,1)S(1)}, u32[]{:S(2)}, u32[]{:S(2)}) collective-permute-start(bf16[4,128,128]{2,1,0:T(8,128)(2,1)} %p.1), channel_id=1, source_target_pairs={{0,2},{1,3},{2,0},{3,1},{4,6},{5,7},{6,4},{7,5},{8,10},{9,11},{10,... | collective-permute-start | bytes 393224 | tf_op jit(solution)/shard_map/ppermute | solution.py:237
  4.1 9.0 %collective-permute-start.4 = (bf16[4,128,128]{2,1,0:T(8,128)(2,1)}, bf16[4,128,128]{2,1,0:T(8,128)(2,1)S(1)}, u32[]{:S(2)}, u32[]{:S(2)}) collective-permute-start(bf16[4,128,128]{2,1,0:T(8,128)(2,1)} %p.1), channel_id=1, source_target_pairs={{4,0},{8,4},{12,8},{16,12},{20,16},{24,20},{28,24},{0,28},{5,1},{9... | collective-permute-start | bytes 393224 | tf_op jit(solution)/shard_map/ppermute | solution.py:229
  5.4 7.7 %collective-permute-start.3 = (bf16[4,128,128]{2,1,0:T(8,128)(2,1)}, bf16[4,128,128]{2,1,0:T(8,128)(2,1)S(1)}, u32[]{:S(2)}, u32[]{:S(2)}) collective-permute-start(bf16[4,128,128]{2,1,0:T(8,128)(2,1)} %p.1), channel_id=1, source_target_pairs={{28,0},{0,4},{4,8},{8,12},{12,16},{16,20},{20,24},{24,28},{29,1},{... | collective-permute-start | bytes 393224 | tf_op jit(solution)/shard_map/ppermute | solution.py:229
  13.1 10.3 %collective-permute-start.6 = (bf16[6,128,128]{2,1,0:T(8,128)(2,1)S(1)}, bf16[6,128,128]{2,1,0:T(8,128)(2,1)S(1)}, u32[]{:S(2)}, u32[]{:S(2)}) collective-permute-start(bf16[6,128,128]{2,1,0:T(8,128)(2,1)S(1)} %get-tuple-element.23.rest_6_), channel_id=1, source_target_pairs={{0,1},{3,2},{4,5},{7,6},{8,9},{11,10},{12,13},{15,14},{16,17},{19,... | collective-permute-start | bytes 589832 | tf_op jit(solution)/shard_map/ppermute | solution.py:237
  15.1 12.5 %collective-permute-start.5 = (bf16[6,128,128]{2,1,0:T(8,128)(2,1)S(1)}, bf16[6,128,128]{2,1,0:T(8,128)(2,1)S(1)}, u32[]{:S(2)}, u32[]{:S(2)}) collective-permute-start(bf16[6,128,128]{2,1,0:T(8,128)(2,1)S(1)} %added.3), channel_id=1, source_target_pairs={{0,1},{3,2},{4,5},{7,6},{8,9},{11,10},{12,13},{15,14},{16,17},{19,... | collective-permute-start | bytes 589832 | tf_op jit(solution)/shard_map/ppermute | solution.py:237
  23.4 8.4 %collective-permute-start.8 = (bf16[6,128,128]{2,1,0:T(8,128)(2,1)S(1)}, bf16[6,128,128]{2,1,0:T(8,128)(2,1)S(1)}, u32[]{:S(2)}, u32[]{:S(2)}) collective-permute-start(bf16[6,128,128]{2,1,0:T(8,128)(2,1)S(1)} %mixed.2.rest_0_), channel_id=1, source_target_pairs={{0,1},{3,2},{1,3},{2,0},{4,5},{7,6},{5,7},{6,4},{8,9},{11,10},{9,1... | collective-permute-start | bytes 589832 | tf_op jit(solution)/shard_map/ppermute | solution.py:237
  27.6 8.4 %collective-permute-start.7 = (bf16[6,128,128]{2,1,0:T(8,128)(2,1)S(1)}, bf16[6,128,128]{2,1,0:T(8,128)(2,1)S(1)}, u32[]{:S(2)}, u32[]{:S(2)}) collective-permute-start(bf16[6,128,128]{2,1,0:T(8,128)(2,1)S(1)} %mixed.3.rest_6_), channel_id=1, source_target_pairs={{0,1},{3,2},{1,3},{2,0},{4,5},{7,6},{5,7},{6,4},{8,9},{11,10},{9,1... | collective-permute-start | bytes 589832 | tf_op jit(solution)/shard_map/ppermute | solution.py:237
  29.3 14.5 %collective-permute-start.11 = (bf16[12,128,128]{2,1,0:T(8,128)(2,1)S(1)}, bf16[12,128,128]{2,1,0:T(8,128)(2,1)S(1)}, u32[]{:S(2)}, u32[]{:S(2)}) collective-permute-start(bf16[12,128,128]{2,1,0:T(8,128)(2,1)S(1)} %coarse_chunk.7.rest_6_.refs_2_), channel_id=1, source_target_pairs={{0,1},{1,0},{2,3},{3,2},{4,5},{5,4},{6,7},{7,6},{8,9},{9,8},{10,11... | collective-permute-start | bytes 1179656 | tf_op jit(solution)/shard_map/ppermute | solution.py:237
  31.8 11.9 %collective-permute-start.9 = (bf16[6,128,128]{2,1,0:T(8,128)(2,1)S(1)}, bf16[6,128,128]{2,1,0:T(8,128)(2,1)S(1)}, u32[]{:S(2)}, u32[]{:S(2)}) collective-permute-start(bf16[6,128,128]{2,1,0:T(8,128)(2,1)S(1)} %added.4.refs_2_), channel_id=1, source_target_pairs={{1,2},{2,1},{5,6},{6,5},{9,10},{10,9},{13,14},{14,13},{17,18},{18,... | collective-permute-start | bytes 589832 | tf_op jit(solution)/shard_map/ppermute | solution.py:237
  36.1 7.6 %collective-permute-start.10 = (bf16[6,128,128]{2,1,0:T(8,128)(2,1)S(1)}, bf16[6,128,128]{2,1,0:T(8,128)(2,1)S(1)}, u32[]{:S(2)}, u32[]{:S(2)}) collective-permute-start(bf16[6,128,128]{2,1,0:T(8,128)(2,1)S(1)} %added.5.rest_6_), channel_id=1, source_target_pairs={{1,2},{2,1},{5,6},{6,5},{9,10},{10,9},{13,14},{14,13},{17,18},{18,... | collective-permute-start | bytes 589832 | tf_op jit(solution)/shard_map/ppermute | solution.py:237

commit v6 on v5

--- a/solution.py
+++ b/solution.py
@@ -8,7 +8,7 @@
 from jax.sharding import PartitionSpec as P
 
 UNROLLS = (32, 16, 8, 4)
-PARTS = ("twice", "once", "thrice", "below", "own", "above")
+PARTS = ("opposite", "across", "beside", "below", "own", "above")
 LIMIT = 12 * 1024 * 1024
 VMEM = pl.BlockSpec(memory_space=pltpu.VMEM)
 SMEM = pl.BlockSpec(memory_space=pltpu.SMEM)
@@ -91,9 +91,10 @@
             part = dict(zip(PARTS, blocks))
             rights = part["below"], part["own"], part["above"]
             left[0] = part["own"][d].T
-            left[1] = part["once"][d].T
-            left[2] = part["twice"][d].T
-            left[3] = part["thrice"][d].T
+            end = (me == 0) | (me == 3)
+            left[1] = jnp.where(end, part["beside"][d], part["across"][d]).T
+            left[2] = jnp.where(end, part["across"][d], part["beside"][d]).T
+            left[3] = part["opposite"][d].T
         for i, ref in enumerate(rights):
             right[i * held : (i + 1) * held] = ref[...]
         accum[...] = jnp.zeros_like(accum)
@@ -236,21 +237,26 @@
     a_tiles, a_row, a_col, p_tiles = stay(a_tiles), stay(a_row), stay(a_col), stay(p_tiles)
     cross = lambda block, pairs: lax.ppermute(block, "col", pairs)
     flips = [[(i, i ^ m) for i in range(4)] for m in range(4)]
-    once, twice, thrice = (cross(p_tiles, flips[m]) for m in (1, 2, 3))
+    across = cross(p_tiles, [(2, 0), (1, 3), (0, 1), (3, 2)])
+    beside = cross(p_tiles, [(1, 0), (2, 3), (0, 2), (3, 1)])
+    opposite = cross(p_tiles, [(0, 3), (3, 0)])
+    middle = cross(p_tiles, [(1, 2), (2, 1)])
     items, counts, a, own = plan(held, 4, me, a_row, a_col, a_count, a_tiles, p_tiles)
     below, above = shifted(p_tiles, "row", 1), shifted(p_tiles, "row", -1)
-    part = dict(once=once, twice=twice, thrice=thrice, below=below, above=above)
+    part = dict(across=across, beside=beside, opposite=opposite, middle=middle, below=below, above=above)
     part = {name: pltpu.with_memory_space_constraint(x, pltpu.VMEM) for name, x in part.items()}
     part["own"] = own
     listed, blocks = (items, counts, a), [part[name] for name in PARTS]
+    part["opposite"] = added([part["opposite"], part["middle"]], p_tiles.dtype)
+    later = [part[name] for name in PARTS]
 
     bf16, f32 = jnp.bfloat16, jnp.float32
     chunk, half = 3 * held, 3 * held // 2
     cut = [(0, half), (half, chunk)]
     narrow, full = [(*c, bf16) for c in cut], [(*c, f32) for c in cut]
     ends, middles, over = [(0, 1), (3, 2)], [(1, 2), (2, 1)], [(1, 3), (2, 0)]
-    part = lambda pick, outs, after=(): coarse_chunk(pick, listed, blocks, outs, after)
-    first = part((3, -1, -1, 0), narrow)
+    part = lambda pick, outs, after=(): coarse_chunk(pick, listed, later, outs, after)
+    (*first,) = coarse_chunk((3, -1, -1, 0), listed, blocks, narrow)
     got1 = cross(first[0], ends)
     *second, wide_a, wide_b = part((2, 3, 0, 1), narrow + full, first[:1])
     got2 = cross(added(first[1:], bf16, second[:1]), ends)

time: 45.2 us -> 44.2 us (0.978)
  the two profiles are of different devices: /device:TPU:8 before, /device:TPU:0 now
where the time goes in v6:
time: 44.2 us; the launch traced here: 43.8 us
  starting transfers between devices  20.4 us (46%)
  waiting for transfers between devices  13.5 us (31%)
  Pallas kernels  8.99 us (20%)
  between operations  0.88 us (2%)
    ppermute x11, starting transfers between devices, line_of_four(): cross = lambda block, pairs: lax.ppermute(block, 'col', pairs)  19.3 us
    ppermute x11, waiting for transfers between devices, line_of_four(): cross = lambda block, pairs: lax.ppermute(block, 'col', pairs)  11.9 us
    pallas_call x5, Pallas kernels, coarse_chunk(): pl.pallas_call(functools.partial(chunk_kernel, held, pick, len(blocks), [...  4.81 us
    pallas_call x1, Pallas kernels, plan(): pl.pallas_call(functools.partial(plan_kernel, held, n), out_shape=(pltpu....  2.97 us
    ppermute x2, waiting for transfers between devices, shifted(): lax.ppermute(block, axis, [((i - distance) % n, i) for i in range(n)])  1.6 us
    ppermute x2, starting transfers between devices, shifted(): lax.ppermute(block, axis, [((i - distance) % n, i) for i in range(n)])  1.1 us
  transfers between devices with their start and end apart: 13, of which 4 were waited for; matrix products, arithmetic and copies ran while one was open for 0% of the time, Pallas kernels for 19%

profile of v6, /device:TPU:0, one launch (start us, length us, event | category | flops | bytes accessed | tf_op | source)
XLA Modules:
  0.0 43.8 jit_solution(7072589866013501605)
XLA Ops:
  0.0 0.0 copy-start
  0.0 4.0 %collective-permute-start.3 = (bf16[4,128,128]{2,1,0:T(8,128)(2,1)}, bf16[4,128,128]{2,1,0:T(8,128)(2,1)S(1)}, u32[]{:S(2)}, u32[]{:S(2)}) collective-permute-start(bf16[4,128,128]{2,1,0:T(8,128)(2,1)} %p.1), channel_id=1, source_target_pairs={{1,0},{2,3},{0,2},{3,1},{5,4},{6,7},{4,6},{7,5},{9,8},{10,11},{8,1... | collective-permute-start | bytes 393224 | tf_op jit(solution)/shard_map/ppermute | solution.py:238
  4.0 0.0 collective-permute-start.2
  4.0 4.9 %collective-permute-start = (bf16[4,128,128]{2,1,0:T(8,128)(2,1)}, bf16[4,128,128]{2,1,0:T(8,128)(2,1)S(1)}, u32[]{:S(2)}, u32[]{:S(2)}) collective-permute-start(bf16[4,128,128]{2,1,0:T(8,128)(2,1)} %p.1), channel_id=1, source_target_pairs={{0,3},{3,0},{4,7},{7,4},{8,11},{11,8},{12,15},{15,12},{16,19},{19,... | collective-permute-start | bytes 393224 | tf_op jit(solution)/shard_map/ppermute | solution.py:238
  9.0 1.1 %collective-permute-start.5 = (bf16[4,128,128]{2,1,0:T(8,128)(2,1)}, bf16[4,128,128]{2,1,0:T(8,128)(2,1)S(1)}, u32[]{:S(2)}, u32[]{:S(2)}) collective-permute-start(bf16[4,128,128]{2,1,0:T(8,128)(2,1)} %p.1), channel_id=1, source_target_pairs={{4,0},{8,4},{12,8},{16,12},{20,16},{24,20},{28,24},{0,28},{5,1},{9... | collective-permute-start | bytes 393224 | tf_op jit(solution)/shard_map/ppermute | solution.py:230
  10.1 0.0 collective-permute-start.4
  10.7 3.0 %plan.1 = (s32[512]{0:T(512)S(4)}, s32[5]{0:T(128)S(4)}, bf16[128,128,128]{2,1,0:T(8,128)(2,1)S(1)}, bf16[4,128,128]{2,1,0:T(8,128)(2,1)S(1)}) custom-call(s32[1]{0:T(128)} %bitcast.me, s32[128]{0:T(128)} %a_row.1, s32[128]{0:T(128)} %a_col.1, s32[1]{0:T(128)S(6)} %copy.6.a_count, bf16[128,128,128]{2,1,0:T(8,128)(2,1)} %a.1, bf16[4,128,128]{2,1,0:T(8,128)(2,1)} %p.1), custom_call_target="tpu_custom_call" | custom-call | tf_op jit(solution)/shard_map/plan/pallas_call | solution.py:61
  13.7 0.0 collective-permute-done.3.rest_2_
  13.7 0.0 copy-done
  13.7 0.7 %collective-permute-start.1 = (bf16[4,128,128]{2,1,0:T(8,128)(2,1)S(1)}, bf16[4,128,128]{2,1,0:T(8,128)(2,1)S(1)}, u32[]{:S(2)}, u32[]{:S(2)}) collective-permute-start(bf16[4,128,128]{2,1,0:T(8,128)(2,1)S(1)} %copy-done), channel_id=1, source_target_pairs={{1,2},{2,1},{5,6},{6,5},{9,10},{10,9},{13,14},{14,13},{17,18},{18,... | collective-permute-start | bytes 393224 | tf_op jit(solution)/shard_map/ppermute | solution.py:238
  14.4 0.0 collective-permute-done.2.rest_1_
  14.4 0.0 collective-permute-done.refs_0_.rest_0_
  14.4 0.0 collective-permute-done.5.rest_5_
  14.4 1.6 %collective-permute-done.4.rest_3_ = bf16[4,128,128]{2,1,0:T(8,128)(2,1)S(1)} collective-permute-done((bf16[4,128,128]{2,1,0:T(8,128)(2,1)}, bf16[4,128,128]{2,1,0:T(8,128)(2,1)S(1)}, u32[]{:S(2)}, u32[]{:S(2)}) %collective-permute-start.4) | collective-permute-done | bytes 131104 | tf_op jit(solution)/shard_map/ppermute | solution.py:230
  16.0 0.9 %coarse_chunk.5 = (bf16[6,128,128]{2,1,0:T(8,128)(2,1)S(1)}, bf16[6,128,128]{2,1,0:T(8,128)(2,1)S(1)}) custom-call(s32[512]{0:T(512)S(4)} %get-tuple-element.20.items, s32[5]{0:T(128)S(4)} %get-tuple-element.19.counts, bf16[128,128,128]{2,1,0:T(8,128)(2,1)S(1)} %get-tuple-element.21.a, bf16[4,128,128]{2,1,0:T(8,128)(2,1)S(1)} %collective-permute-done.refs_0_.rest_0_, ...), custom_call_target="tpu_custom_call" | custom-call | flops 2147483648 | bytes 1048576 | tf_op jit(solution)/shard_map/coarse_chunk/pallas_call | solution.py:137
  17.0 1.3 %collective-permute-start.7 = (bf16[6,128,128]{2,1,0:T(8,128)(2,1)S(1)}, bf16[6,128,128]{2,1,0:T(8,128)(2,1)S(1)}, u32[]{:S(2)}, u32[]{:S(2)}) collective-permute-start(bf16[6,128,128]{2,1,0:T(8,128)(2,1)S(1)} %get-tuple-element.23.rest_6_), channel_id=1, source_target_pairs={{0,1},{3,2},{4,5},{7,6},{8,9},{11,10},{12,13},{15,14},{16,17},{19,... | collective-permute-start | bytes 589832 | tf_op jit(solution)/shard_map/ppermute | solution.py:238
  18.3 0.0 collective-permute-done.1.refs_1_
  18.3 1.3 %coarse_chunk.6 = (bf16[6,128,128]{2,1,0:T(8,128)(2,1)S(1)}, bf16[6,128,128]{2,1,0:T(8,128)(2,1)S(1)}, f32[6,128,128]{2,1,0:T(8,128)S(1)}, f32[6,128,128]{2,1,0:T(8,128)S(1)}) custom-call(s32[512]{0:T(512)S(4)} %get-tuple-element.20.items, s32[5]{0:T(128)S(4)} %get-tuple-element.19.counts, bf16[128,128,128]{2,1,0:T(8,128)(2,1)S(1)} %get-tuple-element.21.a, ...), custom_call_target="tpu_custom_call" | custom-call | flops 2147483648 | bytes 1048576 | tf_op jit(solution)/shard_map/coarse_chunk/pallas_call | solution.py:137
  19.7 2.3 %collective-permute-start.6 = (bf16[6,128,128]{2,1,0:T(8,128)(2,1)S(1)}, bf16[6,128,128]{2,1,0:T(8,128)(2,1)S(1)}, u32[]{:S(2)}, u32[]{:S(2)}) collective-permute-start(bf16[6,128,128]{2,1,0:T(8,128)(2,1)S(1)} %added.5), channel_id=1, source_target_pairs={{0,1},{3,2},{4,5},{7,6},{8,9},{11,10},{12,13},{15,14},{16,17},{19,... | collective-permute-start | bytes 589832 | tf_op jit(solution)/shard_map/ppermute | solution.py:238
  22.0 0.0 collective-permute-done.7.z
  22.0 0.1 mixed.2.rest_0_
  22.1 2.2 %collective-permute-start.9 = (bf16[6,128,128]{2,1,0:T(8,128)(2,1)S(1)}, bf16[6,128,128]{2,1,0:T(8,128)(2,1)S(1)}, u32[]{:S(2)}, u32[]{:S(2)}) collective-permute-start(bf16[6,128,128]{2,1,0:T(8,128)(2,1)S(1)} %mixed.2.rest_0_), channel_id=1, source_target_pairs={{0,1},{3,2},{1,3},{2,0},{4,5},{7,6},{5,7},{6,4},{8,9},{11,10},{9,1... | collective-permute-start | bytes 589832 | tf_op jit(solution)/shard_map/ppermute | solution.py:238
  24.2 3.0 %collective-permute-done.6.z = bf16[6,128,128]{2,1,0:T(8,128)(2,1)S(1)} collective-permute-done((bf16[6,128,128]{2,1,0:T(8,128)(2,1)S(1)}, bf16[6,128,128]{2,1,0:T(8,128)(2,1)S(1)}, u32[]{:S(2)}, u32[]{:S(2)}) %collective-permute-start.6) | collective-permute-done | bytes 196640 | tf_op jit(solution)/shard_map/ppermute | solution.py:238
  27.3 0.1 mixed.3.rest_6_
  27.3 2.5 %collective-permute-start.8 = (bf16[6,128,128]{2,1,0:T(8,128)(2,1)S(1)}, bf16[6,128,128]{2,1,0:T(8,128)(2,1)S(1)}, u32[]{:S(2)}, u32[]{:S(2)}) collective-permute-start(bf16[6,128,128]{2,1,0:T(8,128)(2,1)S(1)} %mixed.3.rest_6_), channel_id=1, source_target_pairs={{0,1},{3,2},{1,3},{2,0},{4,5},{7,6},{5,7},{6,4},{8,9},{11,10},{9,1... | collective-permute-start | bytes 589832 | tf_op jit(solution)/shard_map/ppermute | solution.py:238
  29.9 1.3 %coarse_chunk.7.rest_6_.refs_2_ = bf16[12,128,128]{2,1,0:T(8,128)(2,1)S(1)} custom-call(s32[512]{0:T(512)S(4)} %get-tuple-element.20.items, s32[5]{0:T(128)S(4)} %get-tuple-element.19.counts, bf16[128,128,128]{2,1,0:T(8,128)(2,1)S(1)} %get-tuple-element.21.a, bf16[4,128,128]{2,1,0:T(8,128)(2,1)S(1)} %added.4.rest_0_, ...), custom_call_target="tpu_custom_call" | custom-call | flops 2147483648 | bytes 1048576 | tf_op jit(solution)/shard_map/coarse_chunk/pallas_call | solution.py:137
  31.1 0.1 collective-permute-start.12
  31.2 1.3 %coarse_chunk.8 = (f32[6,128,128]{2,1,0:T(8,128)S(1)}, f32[6,128,128]{2,1,0:T(8,128)S(1)}) custom-call(s32[512]{0:T(512)S(4)} %get-tuple-element.20.items, s32[5]{0:T(128)S(4)} %get-tuple-element.19.counts, bf16[128,128,128]{2,1,0:T(8,128)(2,1)S(1)} %get-tuple-element.21.a, bf16[4,128,128]{2,1,0:T(8,128)(2,1)S(1)} %added.4.rest_0_, ...), custom_call_target="tpu_custom_call" | custom-call | flops 2147483648 | bytes 1048576 | tf_op jit(solution)/shard_map/coarse_chunk/pallas_call | solution.py:137
  32.5 0.0 collective-permute-done.9.refs_1_.far
  32.5 0.7 %collective-permute-start.10 = (bf16[6,128,128]{2,1,0:T(8,128)(2,1)S(1)}, bf16[6,128,128]{2,1,0:T(8,128)(2,1)S(1)}, u32[]{:S(2)}, u32[]{:S(2)}) collective-permute-start(bf16[6,128,128]{2,1,0:T(8,128)(2,1)S(1)} %added.6.refs_2_), channel_id=1, source_target_pairs={{1,2},{2,1},{5,6},{6,5},{9,10},{10,9},{13,14},{14,13},{17,18},{18,... | collective-permute-start | bytes 589832 | tf_op jit(solution)/shard_map/ppermute | solution.py:238
  33.2 2.5 %collective-permute-done.8.refs_1_.far = bf16[6,128,128]{2,1,0:T(8,128)(2,1)S(1)} collective-permute-done((bf16[6,128,128]{2,1,0:T(8,128)(2,1)S(1)}, bf16[6,128,128]{2,1,0:T(8,128)(2,1)S(1)}, u32[]{:S(2)}, u32[]{:S(2)}) %collective-permute-start.8) | collective-permute-done | bytes 196640 | tf_op jit(solution)/shard_map/ppermute | solution.py:238
  35.7 0.7 %collective-permute-start.11 = (bf16[6,128,128]{2,1,0:T(8,128)(2,1)S(1)}, bf16[6,128,128]{2,1,0:T(8,128)(2,1)S(1)}, u32[]{:S(2)}, u32[]{:S(2)}) collective-permute-start(bf16[6,128,128]{2,1,0:T(8,128)(2,1)S(1)} %added.7.rest_6_), channel_id=1, source_target_pairs={{1,2},{2,1},{5,6},{6,5},{9,10},{10,9},{13,14},{14,13},{17,18},{18,... | collective-permute-start | bytes 589832 | tf_op jit(solution)/shard_map/ppermute | solution.py:238
  36.4 0.0 collective-permute-done.11.near
  36.4 0.1 most.3.most_b
  36.5 0.0 collective-permute-done.10.near
  36.5 0.1 most.2.most_a
  36.6 6.3 %collective-permute-done.12.got = bf16[12,128,128]{2,1,0:T(8,128)(2,1)S(1)} collective-permute-done((bf16[12,128,128]{2,1,0:T(8,128)(2,1)S(1)}, bf16[12,128,128]{2,1,0:T(8,128)(2,1)S(1)}, u32[]{:S(2)}, u32[]{:S(2)}) %collective-permute-start.12) | collective-permute-done | bytes 393248 | tf_op jit(solution)/shard_map/ppermute | solution.py:238
  42.9 0.8 %finished.1 = bf16[12,128,128]{2,1,0:T(8,128)(2,1)} custom-call(f32[6,128,128]{2,1,0:T(8,128)S(1)} %most.2.most_a, f32[6,128,128]{2,1,0:T(8,128)S(1)} %most.3.most_b, bf16[12,128,128]{2,1,0:T(8,128)(2,1)S(1)} %collective-permute-done.12.got), custom_call_target="tpu_custom_call" | custom-call | tf_op jit(solution)/shard_map/finished/pallas_call | solution.py:199
  (5 shorter events, 0.1 us)
Async XLA Ops:
  0.0 13.7 %copy-start = (bf16[4,128,128]{2,1,0:T(8,128)(2,1)S(1)}, bf16[4,128,128]{2,1,0:T(8,128)(2,1)}, u32[]{:S(2)}) copy-start(bf16[4,128,128]{2,1,0:T(8,128)(2,1)} %p.1) | copy-start | bytes 393220
  0.0 13.7 %collective-permute-start.3 = (bf16[4,128,128]{2,1,0:T(8,128)(2,1)}, bf16[4,128,128]{2,1,0:T(8,128)(2,1)S(1)}, u32[]{:S(2)}, u32[]{:S(2)}) collective-permute-start(bf16[4,128,128]{2,1,0:T(8,128)(2,1)} %p.1), channel_id=1, source_target_pairs={{1,0},{2,3},{0,2},{3,1},{5,4},{6,7},{4,6},{7,5},{9,8},{10,11},{8,1... | collective-permute-start | bytes 393224 | tf_op jit(solution)/shard_map/ppermute | solution.py:238
  4.0 10.4 %collective-permute-start.2 = (bf16[4,128,128]{2,1,0:T(8,128)(2,1)}, bf16[4,128,128]{2,1,0:T(8,128)(2,1)S(1)}, u32[]{:S(2)}, u32[]{:S(2)}) collective-permute-start(bf16[4,128,128]{2,1,0:T(8,128)(2,1)} %p.1), channel_id=1, source_target_pairs={{2,0},{1,3},{0,1},{3,2},{6,4},{5,7},{4,5},{7,6},{10,8},{9,11},{8,9... | collective-permute-start | bytes 393224 | tf_op jit(solution)/shard_map/ppermute | solution.py:238
  4.0 10.4 %collective-permute-start = (bf16[4,128,128]{2,1,0:T(8,128)(2,1)}, bf16[4,128,128]{2,1,0:T(8,128)(2,1)S(1)}, u32[]{:S(2)}, u32[]{:S(2)}) collective-permute-start(bf16[4,128,128]{2,1,0:T(8,128)(2,1)} %p.1), channel_id=1, source_target_pairs={{0,3},{3,0},{4,7},{7,4},{8,11},{11,8},{12,15},{15,12},{16,19},{19,... | collective-permute-start | bytes 393224 | tf_op jit(solution)/shard_map/ppermute | solution.py:238
  9.0 5.5 %collective-permute-start.5 = (bf16[4,128,128]{2,1,0:T(8,128)(2,1)}, bf16[4,128,128]{2,1,0:T(8,128)(2,1)S(1)}, u32[]{:S(2)}, u32[]{:S(2)}) collective-permute-start(bf16[4,128,128]{2,1,0:T(8,128)(2,1)} %p.1), channel_id=1, source_target_pairs={{4,0},{8,4},{12,8},{16,12},{20,16},{24,20},{28,24},{0,28},{5,1},{9... | collective-permute-start | bytes 393224 | tf_op jit(solution)/shard_map/ppermute | solution.py:230
  10.1 6.0 %collective-permute-start.4 = (bf16[4,128,128]{2,1,0:T(8,128)(2,1)}, bf16[4,128,128]{2,1,0:T(8,128)(2,1)S(1)}, u32[]{:S(2)}, u32[]{:S(2)}) collective-permute-start(bf16[4,128,128]{2,1,0:T(8,128)(2,1)} %p.1), channel_id=1, source_target_pairs={{28,0},{0,4},{4,8},{8,12},{12,16},{16,20},{20,24},{24,28},{29,1},{... | collective-permute-start | bytes 393224 | tf_op jit(solution)/shard_map/ppermute | solution.py:230
  13.7 4.6 %collective-permute-start.1 = (bf16[4,128,128]{2,1,0:T(8,128)(2,1)S(1)}, bf16[4,128,128]{2,1,0:T(8,128)(2,1)S(1)}, u32[]{:S(2)}, u32[]{:S(2)}) collective-permute-start(bf16[4,128,128]{2,1,0:T(8,128)(2,1)S(1)} %copy-done), channel_id=1, source_target_pairs={{1,2},{2,1},{5,6},{6,5},{9,10},{10,9},{13,14},{14,13},{17,18},{18,... | collective-permute-start | bytes 393224 | tf_op jit(solution)/shard_map/ppermute | solution.py:238
  17.0 5.0 %collective-permute-start.7 = (bf16[6,128,128]{2,1,0:T(8,128)(2,1)S(1)}, bf16[6,128,128]{2,1,0:T(8,128)(2,1)S(1)}, u32[]{:S(2)}, u32[]{:S(2)}) collective-permute-start(bf16[6,128,128]{2,1,0:T(8,128)(2,1)S(1)} %get-tuple-element.23.rest_6_), channel_id=1, source_target_pairs={{0,1},{3,2},{4,5},{7,6},{8,9},{11,10},{12,13},{15,14},{16,17},{19,... | collective-permute-start | bytes 589832 | tf_op jit(solution)/shard_map/ppermute | solution.py:238
  19.7 7.6 %collective-permute-start.6 = (bf16[6,128,128]{2,1,0:T(8,128)(2,1)S(1)}, bf16[6,128,128]{2,1,0:T(8,128)(2,1)S(1)}, u32[]{:S(2)}, u32[]{:S(2)}) collective-permute-start(bf16[6,128,128]{2,1,0:T(8,128)(2,1)S(1)} %added.5), channel_id=1, source_target_pairs={{0,1},{3,2},{4,5},{7,6},{8,9},{11,10},{12,13},{15,14},{16,17},{19,... | collective-permute-start | bytes 589832 | tf_op jit(solution)/shard_map/ppermute | solution.py:238
  22.1 10.4 %collective-permute-start.9 = (bf16[6,128,128]{2,1,0:T(8,128)(2,1)S(1)}, bf16[6,128,128]{2,1,0:T(8,128)(2,1)S(1)}, u32[]{:S(2)}, u32[]{:S(2)}) collective-permute-start(bf16[6,128,128]{2,1,0:T(8,128)(2,1)S(1)} %mixed.2.rest_0_), channel_id=1, source_target_pairs={{0,1},{3,2},{1,3},{2,0},{4,5},{7,6},{5,7},{6,4},{8,9},{11,10},{9,1... | collective-permute-start | bytes 589832 | tf_op jit(solution)/shard_map/ppermute | solution.py:238
  27.3 8.4 %collective-permute-start.8 = (bf16[6,128,128]{2,1,0:T(8,128)(2,1)S(1)}, bf16[6,128,128]{2,1,0:T(8,128)(2,1)S(1)}, u32[]{:S(2)}, u32[]{:S(2)}) collective-permute-start(bf16[6,128,128]{2,1,0:T(8,128)(2,1)S(1)} %mixed.3.rest_6_), channel_id=1, source_target_pairs={{0,1},{3,2},{1,3},{2,0},{4,5},{7,6},{5,7},{6,4},{8,9},{11,10},{9,1... | collective-permute-start | bytes 589832 | tf_op jit(solution)/shard_map/ppermute | solution.py:238
  31.1 11.8 %collective-permute-start.12 = (bf16[12,128,128]{2,1,0:T(8,128)(2,1)S(1)}, bf16[12,128,128]{2,1,0:T(8,128)(2,1)S(1)}, u32[]{:S(2)}, u32[]{:S(2)}) collective-permute-start(bf16[12,128,128]{2,1,0:T(8,128)(2,1)S(1)} %coarse_chunk.7.rest_6_.refs_2_), channel_id=1, source_target_pairs={{0,1},{1,0},{2,3},{3,2},{4,5},{5,4},{6,7},{7,6},{8,9},{9,8},{10,11... | collective-permute-start | bytes 1179656 | tf_op jit(solution)/shard_map/ppermute | solution.py:238
  32.5 4.0 %collective-permute-start.10 = (bf16[6,128,128]{2,1,0:T(8,128)(2,1)S(1)}, bf16[6,128,128]{2,1,0:T(8,128)(2,1)S(1)}, u32[]{:S(2)}, u32[]{:S(2)}) collective-permute-start(bf16[6,128,128]{2,1,0:T(8,128)(2,1)S(1)} %added.6.refs_2_), channel_id=1, source_target_pairs={{1,2},{2,1},{5,6},{6,5},{9,10},{10,9},{13,14},{14,13},{17,18},{18,... | collective-permute-start | bytes 589832 | tf_op jit(solution)/shard_map/ppermute | solution.py:238
  35.7 0.7 %collective-permute-start.11 = (bf16[6,128,128]{2,1,0:T(8,128)(2,1)S(1)}, bf16[6,128,128]{2,1,0:T(8,128)(2,1)S(1)}, u32[]{:S(2)}, u32[]{:S(2)}) collective-permute-start(bf16[6,128,128]{2,1,0:T(8,128)(2,1)S(1)} %added.7.rest_6_), channel_id=1, source_target_pairs={{1,2},{2,1},{5,6},{6,5},{9,10},{10,9},{13,14},{14,13},{17,18},{18,... | collective-permute-start | bytes 589832 | tf_op jit(solution)/shard_map/ppermute | solution.py:238

commit v7 on v6

--- a/solution.py
+++ b/solution.py
@@ -176,11 +176,18 @@
     out[...] = jnp.where(end, at_end[...], elsewhere[...]) + jnp.where(end, far[...], near[...]).astype(f32)
 
 
-def finish_kernel(most_a, most_b, got, out):
-    half = most_a.shape[0]
-    for i, most in enumerate((most_a, most_b)):
-        part = slice(i * half, (i + 1) * half)
-        out[part] = (most[...] + got[part].astype(jnp.float32)).astype(out.dtype)
+def finish_kernel(most_a, most_b, got, out, total, sems):
+    half, parts = most_a.shape[0], sems.shape[0]
+    size = 2 * half // parts
+    copies = []
+    for i in range(parts):
+        most, start = (most_a, i * size) if i * size < half else (most_b, i * size - half)
+        part = slice(i * size, (i + 1) * size)
+        total[part] = (most[start : start + size] + got[part].astype(jnp.float32)).astype(out.dtype)
+        copies.append(pltpu.make_async_copy(total.at[part], out.at[part], sems.at[i]))
+        copies[-1].start()
+    for copy in copies:
+        copy.wait()
 
 
 def finished(counts, own, got, last):
@@ -200,7 +207,8 @@
         finish_kernel,
         out_shape=jax.ShapeDtypeStruct(last.shape, last.dtype),
         in_specs=[VMEM] * 3,
-        out_specs=VMEM,
+        out_specs=HBM,
+        scratch_shapes=[pltpu.VMEM(last.shape, last.dtype), pltpu.SemaphoreType.DMA((4,))],
         compiler_params=params,
         name="finished",
     )(*most, last)

time: 44.2 us -> 44.6 us (level)
  the two profiles are of different devices: /device:TPU:0 before, /device:TPU:16 now
where the time goes in v7:
time: 44.6 us; the launch traced here: 44.4 us
  waiting for transfers between devices  17.5 us (39%)
  starting transfers between devices  17.3 us (39%)
  Pallas kernels  8.73 us (20%)
  between operations  0.87 us (2%)
    ppermute x11, waiting for transfers between devices, line_of_four(): cross = lambda block, pairs: lax.ppermute(block, 'col', pairs)  17.5 us
    ppermute x11, starting transfers between devices, line_of_four(): cross = lambda block, pairs: lax.ppermute(block, 'col', pairs)  15.9 us
    pallas_call x5, Pallas kernels, coarse_chunk(): pl.pallas_call(functools.partial(chunk_kernel, held, pick, len(blocks), [...  4.57 us
    pallas_call x1, Pallas kernels, plan(): pl.pallas_call(functools.partial(plan_kernel, held, n), out_shape=(pltpu....  2.97 us
    ppermute x2, starting transfers between devices, shifted(): lax.ppermute(block, axis, [((i - distance) % n, i) for i in range(n)])  1.38 us
  transfers between devices with their start and end apart: 13, of which 5 were waited for; matrix products, arithmetic and copies ran while one was open for 0% of the time, Pallas kernels for 18%

profile of v7, /device:TPU:16, one launch (start us, length us, event | category | flops | bytes accessed | tf_op | source)
XLA Modules:
  0.0 44.4 jit_solution(12926439069766247957)
XLA Ops:
  0.0 0.0 copy-start
  0.0 1.6 %collective-permute-start.3 = (bf16[4,128,128]{2,1,0:T(8,128)(2,1)}, bf16[4,128,128]{2,1,0:T(8,128)(2,1)S(1)}, u32[]{:S(2)}, u32[]{:S(2)}) collective-permute-start(bf16[4,128,128]{2,1,0:T(8,128)(2,1)} %p.1), channel_id=1, source_target_pairs={{1,0},{2,3},{0,2},{3,1},{5,4},{6,7},{4,6},{7,5},{9,8},{10,11},{8,1... | collective-permute-start | bytes 393224 | tf_op jit(solution)/shard_map/ppermute | solution.py:246
  1.6 1.3 %collective-permute-start.2 = (bf16[4,128,128]{2,1,0:T(8,128)(2,1)}, bf16[4,128,128]{2,1,0:T(8,128)(2,1)S(1)}, u32[]{:S(2)}, u32[]{:S(2)}) collective-permute-start(bf16[4,128,128]{2,1,0:T(8,128)(2,1)} %p.1), channel_id=1, source_target_pairs={{2,0},{1,3},{0,1},{3,2},{6,4},{5,7},{4,5},{7,6},{10,8},{9,11},{8,9... | collective-permute-start | bytes 393224 | tf_op jit(solution)/shard_map/ppermute | solution.py:246
  2.9 0.7 %collective-permute-start = (bf16[4,128,128]{2,1,0:T(8,128)(2,1)}, bf16[4,128,128]{2,1,0:T(8,128)(2,1)S(1)}, u32[]{:S(2)}, u32[]{:S(2)}) collective-permute-start(bf16[4,128,128]{2,1,0:T(8,128)(2,1)} %p.1), channel_id=1, source_target_pairs={{0,3},{3,0},{4,7},{7,4},{8,11},{11,8},{12,15},{15,12},{16,19},{19,... | collective-permute-start | bytes 393224 | tf_op jit(solution)/shard_map/ppermute | solution.py:246
  3.6 1.4 %collective-permute-start.5 = (bf16[4,128,128]{2,1,0:T(8,128)(2,1)}, bf16[4,128,128]{2,1,0:T(8,128)(2,1)S(1)}, u32[]{:S(2)}, u32[]{:S(2)}) collective-permute-start(bf16[4,128,128]{2,1,0:T(8,128)(2,1)} %p.1), channel_id=1, source_target_pairs={{4,0},{8,4},{12,8},{16,12},{20,16},{24,20},{28,24},{0,28},{5,1},{9... | collective-permute-start | bytes 393224 | tf_op jit(solution)/shard_map/ppermute | solution.py:238
  5.0 0.0 collective-permute-start.4
  5.6 3.0 %plan.1 = (s32[512]{0:T(512)S(4)}, s32[5]{0:T(128)S(4)}, bf16[128,128,128]{2,1,0:T(8,128)(2,1)S(1)}, bf16[4,128,128]{2,1,0:T(8,128)(2,1)S(1)}) custom-call(s32[1]{0:T(128)} %bitcast.me, s32[128]{0:T(128)} %a_row.1, s32[128]{0:T(128)} %a_col.1, s32[1]{0:T(128)S(6)} %copy.6.a_count, bf16[128,128,128]{2,1,0:T(8,128)(2,1)} %a.1, bf16[4,128,128]{2,1,0:T(8,128)(2,1)} %p.1), custom_call_target="tpu_custom_call" | custom-call | tf_op jit(solution)/shard_map/plan/pallas_call | solution.py:61
  8.6 0.0 collective-permute-done.3.rest_2_
  8.6 0.0 copy-done
  8.6 2.4 %collective-permute-start.1 = (bf16[4,128,128]{2,1,0:T(8,128)(2,1)S(1)}, bf16[4,128,128]{2,1,0:T(8,128)(2,1)S(1)}, u32[]{:S(2)}, u32[]{:S(2)}) collective-permute-start(bf16[4,128,128]{2,1,0:T(8,128)(2,1)S(1)} %copy-done), channel_id=1, source_target_pairs={{1,2},{2,1},{5,6},{6,5},{9,10},{10,9},{13,14},{14,13},{17,18},{18,... | collective-permute-start | bytes 393224 | tf_op jit(solution)/shard_map/ppermute | solution.py:246
  11.0 0.0 collective-permute-done.2.rest_1_
  11.0 0.0 collective-permute-done.refs_0_.rest_0_
  11.0 0.0 collective-permute-done.5.rest_5_
  11.0 0.0 collective-permute-done.4.rest_3_
  11.1 1.3 %collective-permute-start.7 = (bf16[6,128,128]{2,1,0:T(8,128)(2,1)S(1)}, bf16[6,128,128]{2,1,0:T(8,128)(2,1)S(1)}, u32[]{:S(2)}, u32[]{:S(2)}) collective-permute-start(bf16[6,128,128]{2,1,0:T(8,128)(2,1)S(1)} %get-tuple-element.23.rest_6_), channel_id=1, source_target_pairs={{0,1},{3,2},{4,5},{7,6},{8,9},{11,10},{12,13},{15,14},{16,17},{19,... | collective-permute-start | bytes 589832 | tf_op jit(solution)/shard_map/ppermute | solution.py:246
  12.4 3.9 %collective-permute-done.1.refs_1_ = bf16[4,128,128]{2,1,0:T(8,128)(2,1)S(1)} collective-permute-done((bf16[4,128,128]{2,1,0:T(8,128)(2,1)S(1)}, bf16[4,128,128]{2,1,0:T(8,128)(2,1)S(1)}, u32[]{:S(2)}, u32[]{:S(2)}) %collective-permute-start.1) | collective-permute-done | bytes 131104 | tf_op jit(solution)/shard_map/ppermute | solution.py:246
  16.3 1.0 %coarse_chunk.6 = (bf16[6,128,128]{2,1,0:T(8,128)(2,1)S(1)}, bf16[6,128,128]{2,1,0:T(8,128)(2,1)S(1)}, f32[6,128,128]{2,1,0:T(8,128)S(1)}, f32[6,128,128]{2,1,0:T(8,128)S(1)}) custom-call(s32[512]{0:T(512)S(4)} %get-tuple-element.20.items, s32[5]{0:T(128)S(4)} %get-tuple-element.19.counts, bf16[128,128,128]{2,1,0:T(8,128)(2,1)S(1)} %get-tuple-element.21.a, ...), custom_call_target="tpu_custom_call" | custom-call | flops 2147483648 | bytes 1048576 | tf_op jit(solution)/shard_map/coarse_chunk/pallas_call | solution.py:137
  17.3 1.3 %collective-permute-start.6 = (bf16[6,128,128]{2,1,0:T(8,128)(2,1)S(1)}, bf16[6,128,128]{2,1,0:T(8,128)(2,1)S(1)}, u32[]{:S(2)}, u32[]{:S(2)}) collective-permute-start(bf16[6,128,128]{2,1,0:T(8,128)(2,1)S(1)} %added.5), channel_id=1, source_target_pairs={{0,1},{3,2},{4,5},{7,6},{8,9},{11,10},{12,13},{15,14},{16,17},{19,... | collective-permute-start | bytes 589832 | tf_op jit(solution)/shard_map/ppermute | solution.py:246
  18.6 1.2 %collective-permute-done.7.z = bf16[6,128,128]{2,1,0:T(8,128)(2,1)S(1)} collective-permute-done((bf16[6,128,128]{2,1,0:T(8,128)(2,1)S(1)}, bf16[6,128,128]{2,1,0:T(8,128)(2,1)S(1)}, u32[]{:S(2)}, u32[]{:S(2)}) %collective-permute-start.7) | collective-permute-done | bytes 196640 | tf_op jit(solution)/shard_map/ppermute | solution.py:246
  19.8 0.1 mixed.2.rest_0_
  19.9 1.1 %collective-permute-start.9 = (bf16[6,128,128]{2,1,0:T(8,128)(2,1)S(1)}, bf16[6,128,128]{2,1,0:T(8,128)(2,1)S(1)}, u32[]{:S(2)}, u32[]{:S(2)}) collective-permute-start(bf16[6,128,128]{2,1,0:T(8,128)(2,1)S(1)} %mixed.2.rest_0_), channel_id=1, source_target_pairs={{0,1},{3,2},{1,3},{2,0},{4,5},{7,6},{5,7},{6,4},{8,9},{11,10},{9,1... | collective-permute-start | bytes 589832 | tf_op jit(solution)/shard_map/ppermute | solution.py:246
  21.0 6.1 %collective-permute-done.6.z = bf16[6,128,128]{2,1,0:T(8,128)(2,1)S(1)} collective-permute-done((bf16[6,128,128]{2,1,0:T(8,128)(2,1)S(1)}, bf16[6,128,128]{2,1,0:T(8,128)(2,1)S(1)}, u32[]{:S(2)}, u32[]{:S(2)}) %collective-permute-start.6) | collective-permute-done | bytes 196640 | tf_op jit(solution)/shard_map/ppermute | solution.py:246
  27.0 0.1 mixed.3.rest_6_
  27.1 0.1 collective-permute-start.8
  27.2 1.3 %coarse_chunk.7.rest_6_.refs_2_ = bf16[12,128,128]{2,1,0:T(8,128)(2,1)S(1)} custom-call(s32[512]{0:T(512)S(4)} %get-tuple-element.20.items, s32[5]{0:T(128)S(4)} %get-tuple-element.19.counts, bf16[128,128,128]{2,1,0:T(8,128)(2,1)S(1)} %get-tuple-element.21.a, bf16[4,128,128]{2,1,0:T(8,128)(2,1)S(1)} %added.4.rest_0_, ...), custom_call_target="tpu_custom_call" | custom-call | flops 2147483648 | bytes 1048576 | tf_op jit(solution)/shard_map/coarse_chunk/pallas_call | solution.py:137
  28.5 2.1 %collective-permute-start.12 = (bf16[12,128,128]{2,1,0:T(8,128)(2,1)S(1)}, bf16[12,128,128]{2,1,0:T(8,128)(2,1)S(1)}, u32[]{:S(2)}, u32[]{:S(2)}) collective-permute-start(bf16[12,128,128]{2,1,0:T(8,128)(2,1)S(1)} %coarse_chunk.7.rest_6_.refs_2_), channel_id=1, source_target_pairs={{0,1},{1,0},{2,3},{3,2},{4,5},{5,4},{6,7},{7,6},{8,9},{9,8},{10,11... | collective-permute-start | bytes 1179656 | tf_op jit(solution)/shard_map/ppermute | solution.py:246
  30.5 1.3 %coarse_chunk.8 = (f32[6,128,128]{2,1,0:T(8,128)S(1)}, f32[6,128,128]{2,1,0:T(8,128)S(1)}) custom-call(s32[512]{0:T(512)S(4)} %get-tuple-element.20.items, s32[5]{0:T(128)S(4)} %get-tuple-element.19.counts, bf16[128,128,128]{2,1,0:T(8,128)(2,1)S(1)} %get-tuple-element.21.a, bf16[4,128,128]{2,1,0:T(8,128)(2,1)S(1)} %added.4.rest_0_, ...), custom_call_target="tpu_custom_call" | custom-call | flops 2147483648 | bytes 1048576 | tf_op jit(solution)/shard_map/coarse_chunk/pallas_call | solution.py:137
  31.8 0.0 collective-permute-done.9.refs_1_.far
  31.9 1.9 %collective-permute-start.10 = (bf16[6,128,128]{2,1,0:T(8,128)(2,1)S(1)}, bf16[6,128,128]{2,1,0:T(8,128)(2,1)S(1)}, u32[]{:S(2)}, u32[]{:S(2)}) collective-permute-start(bf16[6,128,128]{2,1,0:T(8,128)(2,1)S(1)} %added.6.refs_2_), channel_id=1, source_target_pairs={{1,2},{2,1},{5,6},{6,5},{9,10},{10,9},{13,14},{14,13},{17,18},{18,... | collective-permute-start | bytes 589832 | tf_op jit(solution)/shard_map/ppermute | solution.py:246
  33.8 1.6 %collective-permute-done.8.refs_1_.far = bf16[6,128,128]{2,1,0:T(8,128)(2,1)S(1)} collective-permute-done((bf16[6,128,128]{2,1,0:T(8,128)(2,1)S(1)}, bf16[6,128,128]{2,1,0:T(8,128)(2,1)S(1)}, u32[]{:S(2)}, u32[]{:S(2)}) %collective-permute-start.8) | collective-permute-done | bytes 196640 | tf_op jit(solution)/shard_map/ppermute | solution.py:246
  35.5 2.3 %collective-permute-start.11 = (bf16[6,128,128]{2,1,0:T(8,128)(2,1)S(1)}, bf16[6,128,128]{2,1,0:T(8,128)(2,1)S(1)}, u32[]{:S(2)}, u32[]{:S(2)}) collective-permute-start(bf16[6,128,128]{2,1,0:T(8,128)(2,1)S(1)} %added.7.rest_6_), channel_id=1, source_target_pairs={{1,2},{2,1},{5,6},{6,5},{9,10},{10,9},{13,14},{14,13},{17,18},{18,... | collective-permute-start | bytes 589832 | tf_op jit(solution)/shard_map/ppermute | solution.py:246
  37.8 1.0 %coarse_chunk.9 = (f32[6,128,128]{2,1,0:T(8,128)S(1)}, f32[6,128,128]{2,1,0:T(8,128)S(1)}) custom-call(s32[512]{0:T(512)S(4)} %get-tuple-element.20.items, s32[5]{0:T(128)S(4)} %get-tuple-element.19.counts, bf16[128,128,128]{2,1,0:T(8,128)(2,1)S(1)} %get-tuple-element.21.a, bf16[4,128,128]{2,1,0:T(8,128)(2,1)S(1)} %added.4.rest_0_, ...), custom_call_target="tpu_custom_call" | custom-call | flops 2147483648 | bytes 1048576 | tf_op jit(solution)/shard_map/coarse_chunk/pallas_call | solution.py:137
  38.8 4.7 %collective-permute-done.11.near = bf16[6,128,128]{2,1,0:T(8,128)(2,1)S(1)} collective-permute-done((bf16[6,128,128]{2,1,0:T(8,128)(2,1)S(1)}, bf16[6,128,128]{2,1,0:T(8,128)(2,1)S(1)}, u32[]{:S(2)}, u32[]{:S(2)}) %collective-permute-start.11) | collective-permute-done | bytes 196640 | tf_op jit(solution)/shard_map/ppermute | solution.py:246
  43.5 0.1 most.3.most_b
  43.5 0.0 collective-permute-done.10.near
  43.5 0.1 most.2.most_a
  43.6 0.0 collective-permute-done.12.got
  43.6 0.8 %finished.1 = bf16[12,128,128]{2,1,0:T(8,128)(2,1)} custom-call(f32[6,128,128]{2,1,0:T(8,128)S(1)} %most.2.most_a, f32[6,128,128]{2,1,0:T(8,128)S(1)} %most.3.most_b, bf16[12,128,128]{2,1,0:T(8,128)(2,1)S(1)} %collective-permute-done.12.got), custom_call_target="tpu_custom_call" | custom-call | tf_op jit(solution)/shard_map/finished/pallas_call | solution.py:206
  (5 shorter events, 0.1 us)
Async XLA Ops:
  0.0 8.6 %copy-start = (bf16[4,128,128]{2,1,0:T(8,128)(2,1)S(1)}, bf16[4,128,128]{2,1,0:T(8,128)(2,1)}, u32[]{:S(2)}) copy-start(bf16[4,128,128]{2,1,0:T(8,128)(2,1)} %p.1) | copy-start | bytes 393220
  0.0 8.6 %collective-permute-start.3 = (bf16[4,128,128]{2,1,0:T(8,128)(2,1)}, bf16[4,128,128]{2,1,0:T(8,128)(2,1)S(1)}, u32[]{:S(2)}, u32[]{:S(2)}) collective-permute-start(bf16[4,128,128]{2,1,0:T(8,128)(2,1)} %p.1), channel_id=1, source_target_pairs={{1,0},{2,3},{0,2},{3,1},{5,4},{6,7},{4,6},{7,5},{9,8},{10,11},{8,1... | collective-permute-start | bytes 393224 | tf_op jit(solution)/shard_map/ppermute | solution.py:246
  1.6 9.4 %collective-permute-start.2 = (bf16[4,128,128]{2,1,0:T(8,128)(2,1)}, bf16[4,128,128]{2,1,0:T(8,128)(2,1)S(1)}, u32[]{:S(2)}, u32[]{:S(2)}) collective-permute-start(bf16[4,128,128]{2,1,0:T(8,128)(2,1)} %p.1), channel_id=1, source_target_pairs={{2,0},{1,3},{0,1},{3,2},{6,4},{5,7},{4,5},{7,6},{10,8},{9,11},{8,9... | collective-permute-start | bytes 393224 | tf_op jit(solution)/shard_map/ppermute | solution.py:246
  2.9 8.1 %collective-permute-start = (bf16[4,128,128]{2,1,0:T(8,128)(2,1)}, bf16[4,128,128]{2,1,0:T(8,128)(2,1)S(1)}, u32[]{:S(2)}, u32[]{:S(2)}) collective-permute-start(bf16[4,128,128]{2,1,0:T(8,128)(2,1)} %p.1), channel_id=1, source_target_pairs={{0,3},{3,0},{4,7},{7,4},{8,11},{11,8},{12,15},{15,12},{16,19},{19,... | collective-permute-start | bytes 393224 | tf_op jit(solution)/shard_map/ppermute | solution.py:246
  3.6 7.4 %collective-permute-start.5 = (bf16[4,128,128]{2,1,0:T(8,128)(2,1)}, bf16[4,128,128]{2,1,0:T(8,128)(2,1)S(1)}, u32[]{:S(2)}, u32[]{:S(2)}) collective-permute-start(bf16[4,128,128]{2,1,0:T(8,128)(2,1)} %p.1), channel_id=1, source_target_pairs={{4,0},{8,4},{12,8},{16,12},{20,16},{24,20},{28,24},{0,28},{5,1},{9... | collective-permute-start | bytes 393224 | tf_op jit(solution)/shard_map/ppermute | solution.py:238
  5.0 6.0 %collective-permute-start.4 = (bf16[4,128,128]{2,1,0:T(8,128)(2,1)}, bf16[4,128,128]{2,1,0:T(8,128)(2,1)S(1)}, u32[]{:S(2)}, u32[]{:S(2)}) collective-permute-start(bf16[4,128,128]{2,1,0:T(8,128)(2,1)} %p.1), channel_id=1, source_target_pairs={{28,0},{0,4},{4,8},{8,12},{12,16},{16,20},{20,24},{24,28},{29,1},{... | collective-permute-start | bytes 393224 | tf_op jit(solution)/shard_map/ppermute | solution.py:238
  8.6 7.6 %collective-permute-start.1 = (bf16[4,128,128]{2,1,0:T(8,128)(2,1)S(1)}, bf16[4,128,128]{2,1,0:T(8,128)(2,1)S(1)}, u32[]{:S(2)}, u32[]{:S(2)}) collective-permute-start(bf16[4,128,128]{2,1,0:T(8,128)(2,1)S(1)} %copy-done), channel_id=1, source_target_pairs={{1,2},{2,1},{5,6},{6,5},{9,10},{10,9},{13,14},{14,13},{17,18},{18,... | collective-permute-start | bytes 393224 | tf_op jit(solution)/shard_map/ppermute | solution.py:246
  11.1 8.8 %collective-permute-start.7 = (bf16[6,128,128]{2,1,0:T(8,128)(2,1)S(1)}, bf16[6,128,128]{2,1,0:T(8,128)(2,1)S(1)}, u32[]{:S(2)}, u32[]{:S(2)}) collective-permute-start(bf16[6,128,128]{2,1,0:T(8,128)(2,1)S(1)} %get-tuple-element.23.rest_6_), channel_id=1, source_target_pairs={{0,1},{3,2},{4,5},{7,6},{8,9},{11,10},{12,13},{15,14},{16,17},{19,... | collective-permute-start | bytes 589832 | tf_op jit(solution)/shard_map/ppermute | solution.py:246
  17.3 9.7 %collective-permute-start.6 = (bf16[6,128,128]{2,1,0:T(8,128)(2,1)S(1)}, bf16[6,128,128]{2,1,0:T(8,128)(2,1)S(1)}, u32[]{:S(2)}, u32[]{:S(2)}) collective-permute-start(bf16[6,128,128]{2,1,0:T(8,128)(2,1)S(1)} %added.5), channel_id=1, source_target_pairs={{0,1},{3,2},{4,5},{7,6},{8,9},{11,10},{12,13},{15,14},{16,17},{19,... | collective-permute-start | bytes 589832 | tf_op jit(solution)/shard_map/ppermute | solution.py:246
  19.9 12.0 %collective-permute-start.9 = (bf16[6,128,128]{2,1,0:T(8,128)(2,1)S(1)}, bf16[6,128,128]{2,1,0:T(8,128)(2,1)S(1)}, u32[]{:S(2)}, u32[]{:S(2)}) collective-permute-start(bf16[6,128,128]{2,1,0:T(8,128)(2,1)S(1)} %mixed.2.rest_0_), channel_id=1, source_target_pairs={{0,1},{3,2},{1,3},{2,0},{4,5},{7,6},{5,7},{6,4},{8,9},{11,10},{9,1... | collective-permute-start | bytes 589832 | tf_op jit(solution)/shard_map/ppermute | solution.py:246
  27.1 8.4 %collective-permute-start.8 = (bf16[6,128,128]{2,1,0:T(8,128)(2,1)S(1)}, bf16[6,128,128]{2,1,0:T(8,128)(2,1)S(1)}, u32[]{:S(2)}, u32[]{:S(2)}) collective-permute-start(bf16[6,128,128]{2,1,0:T(8,128)(2,1)S(1)} %mixed.3.rest_6_), channel_id=1, source_target_pairs={{0,1},{3,2},{1,3},{2,0},{4,5},{7,6},{5,7},{6,4},{8,9},{11,10},{9,1... | collective-permute-start | bytes 589832 | tf_op jit(solution)/shard_map/ppermute | solution.py:246
  28.5 15.2 %collective-permute-start.12 = (bf16[12,128,128]{2,1,0:T(8,128)(2,1)S(1)}, bf16[12,128,128]{2,1,0:T(8,128)(2,1)S(1)}, u32[]{:S(2)}, u32[]{:S(2)}) collective-permute-start(bf16[12,128,128]{2,1,0:T(8,128)(2,1)S(1)} %coarse_chunk.7.rest_6_.refs_2_), channel_id=1, source_target_pairs={{0,1},{1,0},{2,3},{3,2},{4,5},{5,4},{6,7},{7,6},{8,9},{9,8},{10,11... | collective-permute-start | bytes 1179656 | tf_op jit(solution)/shard_map/ppermute | solution.py:246
  31.9 11.6 %collective-permute-start.10 = (bf16[6,128,128]{2,1,0:T(8,128)(2,1)S(1)}, bf16[6,128,128]{2,1,0:T(8,128)(2,1)S(1)}, u32[]{:S(2)}, u32[]{:S(2)}) collective-permute-start(bf16[6,128,128]{2,1,0:T(8,128)(2,1)S(1)} %added.6.refs_2_), channel_id=1, source_target_pairs={{1,2},{2,1},{5,6},{6,5},{9,10},{10,9},{13,14},{14,13},{17,18},{18,... | collective-permute-start | bytes 589832 | tf_op jit(solution)/shard_map/ppermute | solution.py:246
  35.5 7.9 %collective-permute-start.11 = (bf16[6,128,128]{2,1,0:T(8,128)(2,1)S(1)}, bf16[6,128,128]{2,1,0:T(8,128)(2,1)S(1)}, u32[]{:S(2)}, u32[]{:S(2)}) collective-permute-start(bf16[6,128,128]{2,1,0:T(8,128)(2,1)S(1)} %added.7.rest_6_), channel_id=1, source_target_pairs={{1,2},{2,1},{5,6},{6,5},{9,10},{10,9},{13,14},{14,13},{17,18},{18,... | collective-permute-start | bytes 589832 | tf_op jit(solution)/shard_map/ppermute | solution.py:246

commit v8 on v7

--- a/solution.py
+++ b/solution.py
@@ -7,7 +7,7 @@
 from jax.experimental.pallas import tpu as pltpu
 from jax.sharding import PartitionSpec as P
 
-UNROLLS = (32, 16, 8, 4)
+UNROLLS = (32, 8)
 PARTS = ("opposite", "across", "beside", "below", "own", "above")
 LIMIT = 12 * 1024 * 1024
 VMEM = pl.BlockSpec(memory_space=pltpu.VMEM)

time: 44.6 us -> 44.2 us (level)
  the two profiles are of different devices: /device:TPU:16 before, /device:TPU:0 now
where the time goes in v8:
time: 44.2 us; the launch traced here: 43.7 us
  starting transfers between devices  21.3 us (48%)
  waiting for transfers between devices  13 us (29%)
  Pallas kernels  8.62 us (20%)
  between operations  0.87 us (2%)
    ppermute x11, starting transfers between devices, line_of_four(): cross = lambda block, pairs: lax.ppermute(block, 'col', pairs)  20.2 us
    ppermute x11, waiting for transfers between devices, line_of_four(): cross = lambda block, pairs: lax.ppermute(block, 'col', pairs)  11.4 us
    pallas_call x5, Pallas kernels, coarse_chunk(): pl.pallas_call(functools.partial(chunk_kernel, held, pick, len(blocks), [...  4.46 us
    pallas_call x1, Pallas kernels, plan(): pl.pallas_call(functools.partial(plan_kernel, held, n), out_shape=(pltpu....  2.97 us
    ppermute x2, waiting for transfers between devices, shifted(): lax.ppermute(block, axis, [((i - distance) % n, i) for i in range(n)])  1.6 us
    ppermute x2, starting transfers between devices, shifted(): lax.ppermute(block, axis, [((i - distance) % n, i) for i in range(n)])  1.1 us
  transfers between devices with their start and end apart: 13, of which 4 were waited for; matrix products, arithmetic and copies ran while one was open for 0% of the time, Pallas kernels for 18%

profile of v8, /device:TPU:0, one launch (start us, length us, event | category | flops | bytes accessed | tf_op | source)
XLA Modules:
  0.0 43.7 jit_solution(16496460272729502840)
XLA Ops:
  0.0 0.0 copy-start
  0.0 4.0 %collective-permute-start.3 = (bf16[4,128,128]{2,1,0:T(8,128)(2,1)}, bf16[4,128,128]{2,1,0:T(8,128)(2,1)S(1)}, u32[]{:S(2)}, u32[]{:S(2)}) collective-permute-start(bf16[4,128,128]{2,1,0:T(8,128)(2,1)} %p.1), channel_id=1, source_target_pairs={{1,0},{2,3},{0,2},{3,1},{5,4},{6,7},{4,6},{7,5},{9,8},{10,11},{8,1... | collective-permute-start | bytes 393224 | tf_op jit(solution)/shard_map/ppermute | solution.py:246
  4.0 0.0 collective-permute-start.2
  4.0 4.9 %collective-permute-start = (bf16[4,128,128]{2,1,0:T(8,128)(2,1)}, bf16[4,128,128]{2,1,0:T(8,128)(2,1)S(1)}, u32[]{:S(2)}, u32[]{:S(2)}) collective-permute-start(bf16[4,128,128]{2,1,0:T(8,128)(2,1)} %p.1), channel_id=1, source_target_pairs={{0,3},{3,0},{4,7},{7,4},{8,11},{11,8},{12,15},{15,12},{16,19},{19,... | collective-permute-start | bytes 393224 | tf_op jit(solution)/shard_map/ppermute | solution.py:246
  9.0 1.1 %collective-permute-start.5 = (bf16[4,128,128]{2,1,0:T(8,128)(2,1)}, bf16[4,128,128]{2,1,0:T(8,128)(2,1)S(1)}, u32[]{:S(2)}, u32[]{:S(2)}) collective-permute-start(bf16[4,128,128]{2,1,0:T(8,128)(2,1)} %p.1), channel_id=1, source_target_pairs={{4,0},{8,4},{12,8},{16,12},{20,16},{24,20},{28,24},{0,28},{5,1},{9... | collective-permute-start | bytes 393224 | tf_op jit(solution)/shard_map/ppermute | solution.py:238
  10.1 0.0 collective-permute-start.4
  10.7 3.0 %plan.1 = (s32[512]{0:T(512)S(4)}, s32[5]{0:T(128)S(4)}, bf16[128,128,128]{2,1,0:T(8,128)(2,1)S(1)}, bf16[4,128,128]{2,1,0:T(8,128)(2,1)S(1)}) custom-call(s32[1]{0:T(128)} %bitcast.me, s32[128]{0:T(128)} %a_row.1, s32[128]{0:T(128)} %a_col.1, s32[1]{0:T(128)S(6)} %copy.6.a_count, bf16[128,128,128]{2,1,0:T(8,128)(2,1)} %a.1, bf16[4,128,128]{2,1,0:T(8,128)(2,1)} %p.1), custom_call_target="tpu_custom_call" | custom-call | tf_op jit(solution)/shard_map/plan/pallas_call | solution.py:61
  13.7 0.0 collective-permute-done.3.rest_2_
  13.7 0.0 copy-done
  13.7 0.7 %collective-permute-start.1 = (bf16[4,128,128]{2,1,0:T(8,128)(2,1)S(1)}, bf16[4,128,128]{2,1,0:T(8,128)(2,1)S(1)}, u32[]{:S(2)}, u32[]{:S(2)}) collective-permute-start(bf16[4,128,128]{2,1,0:T(8,128)(2,1)S(1)} %copy-done), channel_id=1, source_target_pairs={{1,2},{2,1},{5,6},{6,5},{9,10},{10,9},{13,14},{14,13},{17,18},{18,... | collective-permute-start | bytes 393224 | tf_op jit(solution)/shard_map/ppermute | solution.py:246
  14.4 0.0 collective-permute-done.2.rest_1_
  14.4 0.0 collective-permute-done.refs_0_.rest_0_
  14.4 0.0 collective-permute-done.5.rest_5_
  14.4 1.6 %collective-permute-done.4.rest_3_ = bf16[4,128,128]{2,1,0:T(8,128)(2,1)S(1)} collective-permute-done((bf16[4,128,128]{2,1,0:T(8,128)(2,1)}, bf16[4,128,128]{2,1,0:T(8,128)(2,1)S(1)}, u32[]{:S(2)}, u32[]{:S(2)}) %collective-permute-start.4) | collective-permute-done | bytes 131104 | tf_op jit(solution)/shard_map/ppermute | solution.py:238
  16.0 1.3 %coarse_chunk.5 = (bf16[6,128,128]{2,1,0:T(8,128)(2,1)S(1)}, bf16[6,128,128]{2,1,0:T(8,128)(2,1)S(1)}) custom-call(s32[512]{0:T(512)S(4)} %get-tuple-element.20.items, s32[5]{0:T(128)S(4)} %get-tuple-element.19.counts, bf16[128,128,128]{2,1,0:T(8,128)(2,1)S(1)} %get-tuple-element.21.a, bf16[4,128,128]{2,1,0:T(8,128)(2,1)S(1)} %collective-permute-done.refs_0_.rest_0_, ...), custom_call_target="tpu_custom_call" | custom-call | flops 2147483648 | bytes 1048576 | tf_op jit(solution)/shard_map/coarse_chunk/pallas_call | solution.py:137
  17.3 1.3 %collective-permute-start.7 = (bf16[6,128,128]{2,1,0:T(8,128)(2,1)S(1)}, bf16[6,128,128]{2,1,0:T(8,128)(2,1)S(1)}, u32[]{:S(2)}, u32[]{:S(2)}) collective-permute-start(bf16[6,128,128]{2,1,0:T(8,128)(2,1)S(1)} %get-tuple-element.23.rest_6_), channel_id=1, source_target_pairs={{0,1},{3,2},{4,5},{7,6},{8,9},{11,10},{12,13},{15,14},{16,17},{19,... | collective-permute-start | bytes 589832 | tf_op jit(solution)/shard_map/ppermute | solution.py:246
  18.6 0.0 collective-permute-done.1.refs_1_
  18.7 1.0 %coarse_chunk.6 = (bf16[6,128,128]{2,1,0:T(8,128)(2,1)S(1)}, bf16[6,128,128]{2,1,0:T(8,128)(2,1)S(1)}, f32[6,128,128]{2,1,0:T(8,128)S(1)}, f32[6,128,128]{2,1,0:T(8,128)S(1)}) custom-call(s32[512]{0:T(512)S(4)} %get-tuple-element.20.items, s32[5]{0:T(128)S(4)} %get-tuple-element.19.counts, bf16[128,128,128]{2,1,0:T(8,128)(2,1)S(1)} %get-tuple-element.21.a, ...), custom_call_target="tpu_custom_call" | custom-call | flops 2147483648 | bytes 1048576 | tf_op jit(solution)/shard_map/coarse_chunk/pallas_call | solution.py:137
  19.7 2.2 %collective-permute-start.6 = (bf16[6,128,128]{2,1,0:T(8,128)(2,1)S(1)}, bf16[6,128,128]{2,1,0:T(8,128)(2,1)S(1)}, u32[]{:S(2)}, u32[]{:S(2)}) collective-permute-start(bf16[6,128,128]{2,1,0:T(8,128)(2,1)S(1)} %added.5), channel_id=1, source_target_pairs={{0,1},{3,2},{4,5},{7,6},{8,9},{11,10},{12,13},{15,14},{16,17},{19,... | collective-permute-start | bytes 589832 | tf_op jit(solution)/shard_map/ppermute | solution.py:246
  21.9 0.0 collective-permute-done.7.z
  21.9 0.1 mixed.2.rest_0_
  22.0 2.5 %collective-permute-start.9 = (bf16[6,128,128]{2,1,0:T(8,128)(2,1)S(1)}, bf16[6,128,128]{2,1,0:T(8,128)(2,1)S(1)}, u32[]{:S(2)}, u32[]{:S(2)}) collective-permute-start(bf16[6,128,128]{2,1,0:T(8,128)(2,1)S(1)} %mixed.2.rest_0_), channel_id=1, source_target_pairs={{0,1},{3,2},{1,3},{2,0},{4,5},{7,6},{5,7},{6,4},{8,9},{11,10},{9,1... | collective-permute-start | bytes 589832 | tf_op jit(solution)/shard_map/ppermute | solution.py:246
  24.5 2.7 %collective-permute-done.6.z = bf16[6,128,128]{2,1,0:T(8,128)(2,1)S(1)} collective-permute-done((bf16[6,128,128]{2,1,0:T(8,128)(2,1)S(1)}, bf16[6,128,128]{2,1,0:T(8,128)(2,1)S(1)}, u32[]{:S(2)}, u32[]{:S(2)}) %collective-permute-start.6) | collective-permute-done | bytes 196640 | tf_op jit(solution)/shard_map/ppermute | solution.py:246
  27.2 0.1 mixed.3.rest_6_
  27.2 2.5 %collective-permute-start.8 = (bf16[6,128,128]{2,1,0:T(8,128)(2,1)S(1)}, bf16[6,128,128]{2,1,0:T(8,128)(2,1)S(1)}, u32[]{:S(2)}, u32[]{:S(2)}) collective-permute-start(bf16[6,128,128]{2,1,0:T(8,128)(2,1)S(1)} %mixed.3.rest_6_), channel_id=1, source_target_pairs={{0,1},{3,2},{1,3},{2,0},{4,5},{7,6},{5,7},{6,4},{8,9},{11,10},{9,1... | collective-permute-start | bytes 589832 | tf_op jit(solution)/shard_map/ppermute | solution.py:246
  29.8 1.3 %coarse_chunk.7.rest_6_.refs_2_ = bf16[12,128,128]{2,1,0:T(8,128)(2,1)S(1)} custom-call(s32[512]{0:T(512)S(4)} %get-tuple-element.20.items, s32[5]{0:T(128)S(4)} %get-tuple-element.19.counts, bf16[128,128,128]{2,1,0:T(8,128)(2,1)S(1)} %get-tuple-element.21.a, bf16[4,128,128]{2,1,0:T(8,128)(2,1)S(1)} %added.4.rest_0_, ...), custom_call_target="tpu_custom_call" | custom-call | flops 2147483648 | bytes 1048576 | tf_op jit(solution)/shard_map/coarse_chunk/pallas_call | solution.py:137
  31.1 0.6 %collective-permute-start.12 = (bf16[12,128,128]{2,1,0:T(8,128)(2,1)S(1)}, bf16[12,128,128]{2,1,0:T(8,128)(2,1)S(1)}, u32[]{:S(2)}, u32[]{:S(2)}) collective-permute-start(bf16[12,128,128]{2,1,0:T(8,128)(2,1)S(1)} %coarse_chunk.7.rest_6_.refs_2_), channel_id=1, source_target_pairs={{0,1},{1,0},{2,3},{3,2},{4,5},{5,4},{6,7},{7,6},{8,9},{9,8},{10,11... | collective-permute-start | bytes 1179656 | tf_op jit(solution)/shard_map/ppermute | solution.py:246
  31.7 0.9 %coarse_chunk.8 = (f32[6,128,128]{2,1,0:T(8,128)S(1)}, f32[6,128,128]{2,1,0:T(8,128)S(1)}) custom-call(s32[512]{0:T(512)S(4)} %get-tuple-element.20.items, s32[5]{0:T(128)S(4)} %get-tuple-element.19.counts, bf16[128,128,128]{2,1,0:T(8,128)(2,1)S(1)} %get-tuple-element.21.a, bf16[4,128,128]{2,1,0:T(8,128)(2,1)S(1)} %added.4.rest_0_, ...), custom_call_target="tpu_custom_call" | custom-call | flops 2147483648 | bytes 1048576 | tf_op jit(solution)/shard_map/coarse_chunk/pallas_call | solution.py:137
  32.6 0.0 collective-permute-done.9.refs_1_.far
  32.7 0.7 %collective-permute-start.10 = (bf16[6,128,128]{2,1,0:T(8,128)(2,1)S(1)}, bf16[6,128,128]{2,1,0:T(8,128)(2,1)S(1)}, u32[]{:S(2)}, u32[]{:S(2)}) collective-permute-start(bf16[6,128,128]{2,1,0:T(8,128)(2,1)S(1)} %added.6.refs_2_), channel_id=1, source_target_pairs={{1,2},{2,1},{5,6},{6,5},{9,10},{10,9},{13,14},{14,13},{17,18},{18,... | collective-permute-start | bytes 589832 | tf_op jit(solution)/shard_map/ppermute | solution.py:246
  33.3 2.2 %collective-permute-done.8.refs_1_.far = bf16[6,128,128]{2,1,0:T(8,128)(2,1)S(1)} collective-permute-done((bf16[6,128,128]{2,1,0:T(8,128)(2,1)S(1)}, bf16[6,128,128]{2,1,0:T(8,128)(2,1)S(1)}, u32[]{:S(2)}, u32[]{:S(2)}) %collective-permute-start.8) | collective-permute-done | bytes 196640 | tf_op jit(solution)/shard_map/ppermute | solution.py:246
  35.6 0.7 %collective-permute-start.11 = (bf16[6,128,128]{2,1,0:T(8,128)(2,1)S(1)}, bf16[6,128,128]{2,1,0:T(8,128)(2,1)S(1)}, u32[]{:S(2)}, u32[]{:S(2)}) collective-permute-start(bf16[6,128,128]{2,1,0:T(8,128)(2,1)S(1)} %added.7.rest_6_), channel_id=1, source_target_pairs={{1,2},{2,1},{5,6},{6,5},{9,10},{10,9},{13,14},{14,13},{17,18},{18,... | collective-permute-start | bytes 589832 | tf_op jit(solution)/shard_map/ppermute | solution.py:246
  36.3 0.0 collective-permute-done.11.near
  36.3 0.1 most.3.most_b
  36.4 0.0 collective-permute-done.10.near
  36.4 0.1 most.2.most_a
  36.5 6.4 %collective-permute-done.12.got = bf16[12,128,128]{2,1,0:T(8,128)(2,1)S(1)} collective-permute-done((bf16[12,128,128]{2,1,0:T(8,128)(2,1)S(1)}, bf16[12,128,128]{2,1,0:T(8,128)(2,1)S(1)}, u32[]{:S(2)}, u32[]{:S(2)}) %collective-permute-start.12) | collective-permute-done | bytes 393248 | tf_op jit(solution)/shard_map/ppermute | solution.py:246
  42.9 0.8 %finished.1 = bf16[12,128,128]{2,1,0:T(8,128)(2,1)} custom-call(f32[6,128,128]{2,1,0:T(8,128)S(1)} %most.2.most_a, f32[6,128,128]{2,1,0:T(8,128)S(1)} %most.3.most_b, bf16[12,128,128]{2,1,0:T(8,128)(2,1)S(1)} %collective-permute-done.12.got), custom_call_target="tpu_custom_call" | custom-call | tf_op jit(solution)/shard_map/finished/pallas_call | solution.py:206
  (5 shorter events, 0.1 us)
Async XLA Ops:
  0.0 13.7 %copy-start = (bf16[4,128,128]{2,1,0:T(8,128)(2,1)S(1)}, bf16[4,128,128]{2,1,0:T(8,128)(2,1)}, u32[]{:S(2)}) copy-start(bf16[4,128,128]{2,1,0:T(8,128)(2,1)} %p.1) | copy-start | bytes 393220
  0.0 13.7 %collective-permute-start.3 = (bf16[4,128,128]{2,1,0:T(8,128)(2,1)}, bf16[4,128,128]{2,1,0:T(8,128)(2,1)S(1)}, u32[]{:S(2)}, u32[]{:S(2)}) collective-permute-start(bf16[4,128,128]{2,1,0:T(8,128)(2,1)} %p.1), channel_id=1, source_target_pairs={{1,0},{2,3},{0,2},{3,1},{5,4},{6,7},{4,6},{7,5},{9,8},{10,11},{8,1... | collective-permute-start | bytes 393224 | tf_op jit(solution)/shard_map/ppermute | solution.py:246
  4.0 10.4 %collective-permute-start.2 = (bf16[4,128,128]{2,1,0:T(8,128)(2,1)}, bf16[4,128,128]{2,1,0:T(8,128)(2,1)S(1)}, u32[]{:S(2)}, u32[]{:S(2)}) collective-permute-start(bf16[4,128,128]{2,1,0:T(8,128)(2,1)} %p.1), channel_id=1, source_target_pairs={{2,0},{1,3},{0,1},{3,2},{6,4},{5,7},{4,5},{7,6},{10,8},{9,11},{8,9... | collective-permute-start | bytes 393224 | tf_op jit(solution)/shard_map/ppermute | solution.py:246
  4.0 10.4 %collective-permute-start = (bf16[4,128,128]{2,1,0:T(8,128)(2,1)}, bf16[4,128,128]{2,1,0:T(8,128)(2,1)S(1)}, u32[]{:S(2)}, u32[]{:S(2)}) collective-permute-start(bf16[4,128,128]{2,1,0:T(8,128)(2,1)} %p.1), channel_id=1, source_target_pairs={{0,3},{3,0},{4,7},{7,4},{8,11},{11,8},{12,15},{15,12},{16,19},{19,... | collective-permute-start | bytes 393224 | tf_op jit(solution)/shard_map/ppermute | solution.py:246
  9.0 5.5 %collective-permute-start.5 = (bf16[4,128,128]{2,1,0:T(8,128)(2,1)}, bf16[4,128,128]{2,1,0:T(8,128)(2,1)S(1)}, u32[]{:S(2)}, u32[]{:S(2)}) collective-permute-start(bf16[4,128,128]{2,1,0:T(8,128)(2,1)} %p.1), channel_id=1, source_target_pairs={{4,0},{8,4},{12,8},{16,12},{20,16},{24,20},{28,24},{0,28},{5,1},{9... | collective-permute-start | bytes 393224 | tf_op jit(solution)/shard_map/ppermute | solution.py:238
  10.1 6.0 %collective-permute-start.4 = (bf16[4,128,128]{2,1,0:T(8,128)(2,1)}, bf16[4,128,128]{2,1,0:T(8,128)(2,1)S(1)}, u32[]{:S(2)}, u32[]{:S(2)}) collective-permute-start(bf16[4,128,128]{2,1,0:T(8,128)(2,1)} %p.1), channel_id=1, source_target_pairs={{28,0},{0,4},{4,8},{8,12},{12,16},{16,20},{20,24},{24,28},{29,1},{... | collective-permute-start | bytes 393224 | tf_op jit(solution)/shard_map/ppermute | solution.py:238
  13.7 4.9 %collective-permute-start.1 = (bf16[4,128,128]{2,1,0:T(8,128)(2,1)S(1)}, bf16[4,128,128]{2,1,0:T(8,128)(2,1)S(1)}, u32[]{:S(2)}, u32[]{:S(2)}) collective-permute-start(bf16[4,128,128]{2,1,0:T(8,128)(2,1)S(1)} %copy-done), channel_id=1, source_target_pairs={{1,2},{2,1},{5,6},{6,5},{9,10},{10,9},{13,14},{14,13},{17,18},{18,... | collective-permute-start | bytes 393224 | tf_op jit(solution)/shard_map/ppermute | solution.py:246
  17.3 4.5 %collective-permute-start.7 = (bf16[6,128,128]{2,1,0:T(8,128)(2,1)S(1)}, bf16[6,128,128]{2,1,0:T(8,128)(2,1)S(1)}, u32[]{:S(2)}, u32[]{:S(2)}) collective-permute-start(bf16[6,128,128]{2,1,0:T(8,128)(2,1)S(1)} %get-tuple-element.23.rest_6_), channel_id=1, source_target_pairs={{0,1},{3,2},{4,5},{7,6},{8,9},{11,10},{12,13},{15,14},{16,17},{19,... | collective-permute-start | bytes 589832 | tf_op jit(solution)/shard_map/ppermute | solution.py:246
  19.7 7.5 %collective-permute-start.6 = (bf16[6,128,128]{2,1,0:T(8,128)(2,1)S(1)}, bf16[6,128,128]{2,1,0:T(8,128)(2,1)S(1)}, u32[]{:S(2)}, u32[]{:S(2)}) collective-permute-start(bf16[6,128,128]{2,1,0:T(8,128)(2,1)S(1)} %added.5), channel_id=1, source_target_pairs={{0,1},{3,2},{4,5},{7,6},{8,9},{11,10},{12,13},{15,14},{16,17},{19,... | collective-permute-start | bytes 589832 | tf_op jit(solution)/shard_map/ppermute | solution.py:246
  22.0 10.6 %collective-permute-start.9 = (bf16[6,128,128]{2,1,0:T(8,128)(2,1)S(1)}, bf16[6,128,128]{2,1,0:T(8,128)(2,1)S(1)}, u32[]{:S(2)}, u32[]{:S(2)}) collective-permute-start(bf16[6,128,128]{2,1,0:T(8,128)(2,1)S(1)} %mixed.2.rest_0_), channel_id=1, source_target_pairs={{0,1},{3,2},{1,3},{2,0},{4,5},{7,6},{5,7},{6,4},{8,9},{11,10},{9,1... | collective-permute-start | bytes 589832 | tf_op jit(solution)/shard_map/ppermute | solution.py:246
  27.2 8.4 %collective-permute-start.8 = (bf16[6,128,128]{2,1,0:T(8,128)(2,1)S(1)}, bf16[6,128,128]{2,1,0:T(8,128)(2,1)S(1)}, u32[]{:S(2)}, u32[]{:S(2)}) collective-permute-start(bf16[6,128,128]{2,1,0:T(8,128)(2,1)S(1)} %mixed.3.rest_6_), channel_id=1, source_target_pairs={{0,1},{3,2},{1,3},{2,0},{4,5},{7,6},{5,7},{6,4},{8,9},{11,10},{9,1... | collective-permute-start | bytes 589832 | tf_op jit(solution)/shard_map/ppermute | solution.py:246
  31.1 11.9 %collective-permute-start.12 = (bf16[12,128,128]{2,1,0:T(8,128)(2,1)S(1)}, bf16[12,128,128]{2,1,0:T(8,128)(2,1)S(1)}, u32[]{:S(2)}, u32[]{:S(2)}) collective-permute-start(bf16[12,128,128]{2,1,0:T(8,128)(2,1)S(1)} %coarse_chunk.7.rest_6_.refs_2_), channel_id=1, source_target_pairs={{0,1},{1,0},{2,3},{3,2},{4,5},{5,4},{6,7},{7,6},{8,9},{9,8},{10,11... | collective-permute-start | bytes 1179656 | tf_op jit(solution)/shard_map/ppermute | solution.py:246
  32.7 3.8 %collective-permute-start.10 = (bf16[6,128,128]{2,1,0:T(8,128)(2,1)S(1)}, bf16[6,128,128]{2,1,0:T(8,128)(2,1)S(1)}, u32[]{:S(2)}, u32[]{:S(2)}) collective-permute-start(bf16[6,128,128]{2,1,0:T(8,128)(2,1)S(1)} %added.6.refs_2_), channel_id=1, source_target_pairs={{1,2},{2,1},{5,6},{6,5},{9,10},{10,9},{13,14},{14,13},{17,18},{18,... | collective-permute-start | bytes 589832 | tf_op jit(solution)/shard_map/ppermute | solution.py:246
  35.6 0.7 %collective-permute-start.11 = (bf16[6,128,128]{2,1,0:T(8,128)(2,1)S(1)}, bf16[6,128,128]{2,1,0:T(8,128)(2,1)S(1)}, u32[]{:S(2)}, u32[]{:S(2)}) collective-permute-start(bf16[6,128,128]{2,1,0:T(8,128)(2,1)S(1)} %added.7.rest_6_), channel_id=1, source_target_pairs={{1,2},{2,1},{5,6},{6,5},{9,10},{10,9},{13,14},{14,13},{17,18},{18,... | collective-permute-start | bytes 589832 | tf_op jit(solution)/shard_map/ppermute | solution.py:246
